TPU v7x, 512 devices: a whole 4x4x16 slice. The times are simulated.
512 devices in a mesh: fsdp: 64 (over x_hi, z, core), seq: 8 (over x_lo, y).
Axes of the slice: x: 4 (x_hi: 2, x_lo: 2; x = x_hi * 2 + x_lo), y: 4, z: 16, core: 2. Of those that a mesh axis runs over, the one named last changes fastest.
Arguments:
- attended: bfloat16 [64, 2, 1024, 1536], P('fsdp', None, 'seq'), may hold values from -6 to 6
- residual: bfloat16 [64, 2, 1024, 3072], P('fsdp', None, 'seq'), may hold values from -6 to 6
- targets: bfloat16 [64, 2, 1024, 64], P('fsdp', None, 'seq'), may hold values from -6 to 6
- repaint_mask: int32 [64, 1024], P('fsdp', 'seq'), may hold values from 0 to 1, as said below
- timesteps: int32 [64], P('fsdp'), may hold values from 0 to 999
- modulation: float32 [64, 3, 3072], P('fsdp'), may hold values from -4 to 4
- output_weight: bfloat16 [1536, 3072], P('fsdp'), may hold values from -0.15625 to 0.15625
- adapter_down: bfloat16 [1536, 128], P('fsdp'), may hold values from -0.15625 to 0.15625
- adapter_up: bfloat16 [3072, 128], P('fsdp'), may hold values from -0.15625 to 0.15625
- latent_weight: bfloat16 [3072, 64], P('fsdp'), may hold values from -0.109375 to 0.109375
Outputs:
- pair_loss: float32 [64], P('fsdp')
- grad_down: float32 [1536, 128], P('fsdp')
- up_gradient: float32 [3072, 128], P('fsdp')
Inputs may be any that keep to these rules, and one draw needn't show every extreme that they name: `repaint_mask`: 1 marks an image token to be repainted; a pair's winner and loser share the mask.
All inputs are finite; a program needn't handle non-finite values.
Results may differ from a plain program's by a relative error of at most 0.0065.
Values may be sent and summed in bfloat16 or wider, within the bound.
No kernel may reach another device: no remote copies, remote signals or barrier semaphores. Data moves between devices by JAX's collectives and lax.ppermute only.
A program may use at most 64 MiB of HBM per device.

v0:
```python
import jax
import jax.numpy as jnp
from jax import lax
from jax.sharding import PartitionSpec as P

NORM_EPS = 1e-06
DPO_BETA = 10.0
ADAPTER_SCALE = 1.0


def layer_norm(hidden):
    centred = hidden - jnp.mean(hidden, axis=-1, keepdims=True)
    inverse = lax.rsqrt(jnp.mean(centred * centred, axis=-1, keepdims=True) + NORM_EPS)
    return (centred * inverse, inverse)


def head_out(stream, update, gate_term, scale_term, shift_term, latent_weight):
    hidden = stream.astype(jnp.float32) + gate_term * update
    normed, inverse = layer_norm(hidden)
    modulated = (normed * (1.0 + scale_term) + shift_term).astype(jnp.bfloat16)
    flat_rows = modulated.reshape(-1, modulated.shape[-1])
    predicted = jnp.dot(flat_rows, latent_weight, preferred_element_type=jnp.float32)
    return (predicted.reshape(modulated.shape[:-1] + (latent_weight.shape[1],)), normed, inverse)


def head_back(grad_pred, normed, inverse, gate_term, scale_term, latent_weight):
    flat_grad = grad_pred.reshape(-1, grad_pred.shape[-1])
    grad_mod = lax.dot_general(
        flat_grad, latent_weight, (((1,), (1,)), ((), ())), preferred_element_type=jnp.float32
    )
    grad_norm = grad_mod.reshape(normed.shape) * (1.0 + scale_term)
    centred = grad_norm - jnp.mean(grad_norm, axis=-1, keepdims=True)
    grad_hidden = inverse * (
        centred - normed * jnp.mean(grad_norm * normed, axis=-1, keepdims=True)
    )
    return (gate_term * grad_hidden).astype(jnp.bfloat16)


def local(
    attended,
    residual,
    targets,
    repaint_mask,
    timesteps,
    modulation,
    output_weight,
    adapter_down,
    adapter_up,
    latent_weight,
):
    pair_count, kind_count, token_count, head_width = attended.shape
    model_width = residual.shape[-1]
    channels = targets.shape[-1]
    row_count = pair_count * kind_count * token_count
    flat_in = attended.reshape(row_count, head_width)
    down_all, up_gathered, final_all = (
        lax.all_gather(adapter_down, "fsdp", axis=0, tiled=True),
        lax.all_gather(adapter_up, "fsdp", axis=0, tiled=True),
        lax.all_gather(latent_weight, "fsdp", axis=0, tiled=True),
    )
    frozen_output = jnp.dot(
        flat_in,
        lax.all_gather(output_weight, "fsdp", axis=0, tiled=True),
        preferred_element_type=jnp.float32,
    )
    frozen_output = frozen_output.reshape(pair_count, kind_count, token_count, model_width)
    down_projected = jnp.dot(flat_in, down_all, preferred_element_type=jnp.float32).astype(
        jnp.bfloat16
    )
    adapter_term = lax.dot_general(
        down_projected, up_gathered, (((1,), (1,)), ((), ())), preferred_element_type=jnp.float32
    )
    policy_model = frozen_output + ADAPTER_SCALE * adapter_term.reshape(frozen_output.shape)
    shift_term = modulation[:, None, None, 0, :]
    scale_term = modulation[:, None, None, 1, :]
    gate_term = modulation[:, None, None, 2, :]
    pred_pol, normed, inverse = head_out(
        residual, policy_model, gate_term, scale_term, shift_term, final_all
    )
    pred_ref, unused_normed, unused_inverse = head_out(
        residual, frozen_output, gate_term, scale_term, shift_term, final_all
    )
    mask_rows = repaint_mask.astype(jnp.float32)[:, None, :, None]
    target_rows = targets.astype(jnp.float32)
    miss_pol = pred_pol - target_rows
    miss_ref = pred_ref - target_rows
    normaliser = float(token_count * lax.axis_size("seq") * channels)
    local_errors = (
        jnp.concatenate(
            [
                jnp.sum(mask_rows * miss_pol * miss_pol, axis=(2, 3)),
                jnp.sum(mask_rows * miss_ref * miss_ref, axis=(2, 3)),
            ],
            axis=1,
        )
        / normaliser
    )
    summed = lax.psum(local_errors, "seq")
    delta = summed[:, 0] - summed[:, 2] - (summed[:, 1] - summed[:, 3])
    weight_t = 2.0 - timesteps.astype(jnp.float32) / 1000.0
    logits = -DPO_BETA * weight_t * delta
    pair_loss = jax.nn.softplus(-logits)
    slope = jax.nn.sigmoid(-logits) * DPO_BETA * weight_t / normaliser
    signs = jnp.array([1.0, -1.0], jnp.float32)
    weighting = slope[:, None] * signs[None, :]
    grad_pred = (weighting[:, :, None, None] * 2.0 * mask_rows * miss_pol).astype(jnp.bfloat16)
    gradient_delta = head_back(
        grad_pred, normed, inverse, gate_term, scale_term, final_all
    ).reshape(row_count, model_width)
    up_gradient = ADAPTER_SCALE * lax.dot_general(
        gradient_delta, down_projected, (((0,), (0,)), ((), ())), preferred_element_type=jnp.float32
    )
    gradient_lowrank = (
        ADAPTER_SCALE * jnp.dot(gradient_delta, up_gathered, preferred_element_type=jnp.float32)
    ).astype(jnp.bfloat16)
    grad_down = lax.dot_general(
        flat_in, gradient_lowrank, (((0,), (0,)), ((), ())), preferred_element_type=jnp.float32
    )
    shard_down, shard_up = (
        lax.psum_scatter(grad_down, "fsdp", scatter_dimension=0, tiled=True),
        lax.psum_scatter(up_gradient, "fsdp", scatter_dimension=0, tiled=True),
    )
    shard_down, shard_up = lax.psum((shard_down, shard_up), "seq")
    return (pair_loss, shard_down, shard_up)


def solution(mesh):
    in_specs = (
        P("fsdp", None, "seq", None),
        P("fsdp", None, "seq", None),
        P("fsdp", None, "seq", None),
        P("fsdp", "seq"),
        P("fsdp"),
        P("fsdp", None, None),
        P("fsdp", None),
        P("fsdp", None),
        P("fsdp", None),
        P("fsdp", None),
    )
    out_specs = (P("fsdp"), P("fsdp", None), P("fsdp", None))
    return jax.shard_map(local, mesh=mesh, in_specs=in_specs, out_specs=out_specs, check_vma=False)
```

profile of v0, /device:TPU:4, one launch (start us, length us, event | category | flops | bytes accessed | tf_op | source)
XLA Modules:
  0.0 1042.9 jit_solution(1494011767243555528)
XLA Ops:
  7.2 0.7 all-gather.2.cloned.1.call-update
  8.6 82.1 %all_gather.13 = bf16[1536,128]{1,0:T(8,128)(2,1)S(1)} all-gather(bf16[24,128]{1,0:T(8,128)(2,1)} %param.18), channel_id=1, replica_groups=mesh['fsdp'=64,'seq'=8] {'fsdp'}, dimensions={0}, use_global_device_ids=true | all-gather | bytes 399360 | tf_op jit(solution)/shard_map/all_gather | solution.py:57
  90.7 75.0 %all_gather.15 = bf16[3072,64]{1,0:T(8,128)(2,1)S(1)} all-gather(bf16[48,64]{1,0:T(8,128)(2,1)} %param.20), channel_id=1, replica_groups=mesh['fsdp'=64,'seq'=8] {'fsdp'}, dimensions={0}, use_global_device_ids=true | all-gather | bytes 399360 | tf_op jit(solution)/shard_map/all_gather | solution.py:59
  166.8 75.4 %all_gather.14 = bf16[3072,128]{1,0:T(8,128)(2,1)S(1)} all-gather(bf16[48,128]{1,0:T(8,128)(2,1)} %param.19), channel_id=1, replica_groups=mesh['fsdp'=64,'seq'=8] {'fsdp'}, dimensions={0}, use_global_device_ids=true | all-gather | bytes 798720 | tf_op jit(solution)/shard_map/all_gather | solution.py:58
  242.1 2.2 fusion.41
  244.4 5.3 fusion.40
  250.2 2.5 copy-done.4
  252.7 3.2 convert_add_fusion.1
  255.9 2.1 reduce_sum.72
  258.0 2.5 multiply_reduce_fusion.1
  260.8 0.9 fusion.35
  261.8 2.6 fusion.30
  264.5 20.4 %psum.21 = f32[1,4]{1,0:T(1,128)S(1)} all-reduce(f32[1,4]{1,0:T(1,128)S(1)} %maximum_multiply_fusion), channel_id=1, replica_groups=mesh['fsdp'=64,'seq'=8] {'seq'}, use_global_device_ids=true, to_apply=%region_6.0 | all-reduce | flops 4 | bytes 32 | tf_op jit(solution)/shard_map/psum | solution.py:98
  288.2 4.4 fusion
  292.6 2.1 reduce_sum.78
  294.7 4.0 fusion.3
  298.8 1.7 convolution_bitcast_fusion
  300.6 1.8 fusion.42
  302.4 1.3 dynamic-slice
  304.4 484.5 %all-reduce.4.cloned.1.call-done = f32[1536,128]{0,1:T(8,128)} async-done(((f32[1536,128]{0,1:T(8,128)}), f32[1536,128]{0,1:T(8,128)}) %all-reduce.4.cloned.1.call-update) | async-done | bytes 786448
  788.9 1.0 constant_dynamic-slice_fusion
  789.9 208.8 %reduce-scatter.3.cloned.1.call-done = f32[48,128]{1,0:T(8,128)} async-done(((f32[3072,128]{1,0:T(8,128)}), f32[48,128]{1,0:T(8,128)}) %reduce-scatter.3.cloned.1.call-update) | async-done | bytes 24592 | tf_op jit(solution)/shard_map/reduce_scatter | solution.py:121
  998.7 35.8 %all-reduce.1 = (f32[24,128]{0,1:T(8,128)S(1)}, f32[48,128]{1,0:T(8,128)}) all-reduce(f32[24,128]{0,1:T(8,128)S(1)} %constant_dynamic-slice_fusion, f32[48,128]{1,0:T(8,128)} %reduce-scatter.3.cloned.1.call-done), channel_id=1, replica_groups=mesh['fsdp'=64,'seq'=8] {'seq'}, use_global_device_ids=true, to_apply=%region_10.11 | all-reduce | flops 9216 | bytes 73728 | tf_op jit(solution)/shard_map/psum | solution.py:123
  1034.6 0.7 copy.15
  (36 shorter events, 2.8 us)
Async XLA Ops:
  7.2 159.2 %copy-start = (bf16[1,2,128,1536]{3,2,1,0:T(8,128)(2,1)S(1)}, bf16[1,2,128,1536]{3,2,1,0:T(8,128)(2,1)}, u32[]{:S(2)}) copy-start(bf16[1,2,128,1536]{3,2,1,0:T(8,128)(2,1)} %param.11) | copy-start | bytes 2359300
  7.2 237.2 %all-gather.2.cloned.1.call-start = ((), (), s32[]{:S(2)}) async-start(), calls=%async_computation.1 | async-start | bytes 9584640 | tf_op jit(solution)/shard_map/all_gather | solution.py:63
  7.9 781.0 %all-reduce.4.cloned.1.call-start = ((), (), s32[]{:S(2)}) async-start(), calls=%async_computation.3 | async-start | bytes 1572864
  165.7 78.6 %copy-start.6 = (f32[1,3,3072]{2,0,1:T(1,128)S(1)}, f32[1,3,3072]{2,0,1:T(1,128)}, u32[]{:S(2)}) copy-start(f32[1,3,3072]{2,0,1:T(1,128)} %param.16) | copy-start | bytes 110596
  244.4 5.3 copy-start.5
  249.7 6.2 copy-start.2
  249.7 3.0 copy-start.4
  255.9 4.7 copy-start.7
  258.0 2.8 copy-start.1
  258.0 3.8 copy-start.3
  261.8 26.3 %copy-start.8 = (f32[2]{0:T(128)S(1)}, f32[2]{0:T(128)}, u32[]{:S(2)}) copy-start(f32[2]{0:T(128)} %constant.38.clone) | copy-start | bytes 28
  300.5 698.2 %reduce-scatter.3.cloned.1.call-start = ((), (), s32[]{:S(2)}) async-start(), calls=%async_computation.2 | async-start | bytes 1597440 | tf_op jit(solution)/shard_map/reduce_scatter | solution.py:121
Sparse Core Ops, SparseCore 0:
  11.3 171.5 all-gather.1
  300.6 488.2 all-reduce.3
  794.3 204.4 reduce-scatter.2
where the time goes:
time: 1040 us
  waiting for transfers between devices  694 us (67%)
  blocking collectives  289 us (28%)
  matrix products  19.3 us (2%)
  between operations  19 us (2%)
  other arithmetic  15.3 us (1%)
    unnamed x4, waiting for transfers between devices  485 us
    reduce_scatter x1, waiting for transfers between devices, local(): lax.psum_scatter(up_gradient, 'fsdp', scatter_dimension=0, tiled=True)  209 us
    all_gather x1, blocking collectives, local(): lax.all_gather(adapter_down, 'fsdp', axis=0, tiled=True)  82.1 us
    all_gather x1, blocking collectives, local(): lax.all_gather(adapter_up, 'fsdp', axis=0, tiled=True)  75.4 us
    all_gather x1, blocking collectives, local(): lax.all_gather(latent_weight, 'fsdp', axis=0, tiled=True)  75 us
    psum x1, blocking collectives, local(): shard_down, shard_up = lax.psum((shard_down, shard_up), 'seq')  35.8 us
  transfers between devices with their start and end apart: 3, of which 2 were waited for; matrix products, arithmetic and copies ran while one was open for 1% of the time, Pallas kernels for 0%

commit v1 on v0

v1 whole, which is shorter than its diff:
```python
import jax
import jax.numpy as jnp
from jax import lax
from jax.sharding import Mesh
from jax.sharding import PartitionSpec as P

NORM_EPS = 1e-06
DPO_BETA = 10.0
ADAPTER_SCALE = 1.0
FINE = ("xh", "z", "c", "xl", "y")
OWNERS = ("xh", "z", "c")
TOKENS = ("xl", "y")
LANES = 128


def layer_norm(hidden):
    centred = hidden - jnp.mean(hidden, axis=-1, keepdims=True)
    inverse = lax.rsqrt(jnp.mean(centred * centred, axis=-1, keepdims=True) + NORM_EPS)
    return (centred * inverse, inverse)


def head_out(stream, update, gate_term, scale_term, shift_term, latent_weight):
    hidden = stream.astype(jnp.float32) + gate_term * update
    normed, inverse = layer_norm(hidden)
    modulated = (normed * (1.0 + scale_term) + shift_term).astype(jnp.bfloat16)
    predicted = jnp.dot(modulated, latent_weight, preferred_element_type=jnp.float32)
    return (predicted, normed, inverse)


def head_back(grad_pred, normed, inverse, gate_term, scale_term, latent_weight):
    grad_mod = lax.dot_general(
        grad_pred, latent_weight, (((1,), (1,)), ((), ())), preferred_element_type=jnp.float32
    )
    grad_norm = grad_mod * (1.0 + scale_term)
    centred = grad_norm - jnp.mean(grad_norm, axis=-1, keepdims=True)
    grad_hidden = inverse * (
        centred - normed * jnp.mean(grad_norm * normed, axis=-1, keepdims=True)
    )
    return (gate_term * grad_hidden).astype(jnp.bfloat16)


def spread(value, axes, size):
    return lax.all_to_all(jnp.broadcast_to(value[None], (size,) + value.shape), axes, 0, 0)


def by_core(core, here, there):
    first = jnp.where(core == 0, here, there)
    second = jnp.where(core == 0, there, here)
    return first, second


def local(
    attended,
    residual,
    targets,
    repaint_mask,
    timesteps,
    modulation,
    output_weight,
    adapter_down,
    adapter_up,
    latent_weight,
):
    _, kinds, tokens, head_width = attended.shape
    width = residual.shape[-1]
    channels = targets.shape[-1]
    rank = adapter_down.shape[1]
    rows = kinds * tokens
    own = output_weight.shape[0]
    half = width // 2
    xs, zs = lax.axis_size("xh"), lax.axis_size("z")
    seqs = lax.axis_size("xl") * lax.axis_size("y")
    core = lax.axis_index("c")
    swap = [(0, 1), (1, 0)]

    packed = jnp.stack(
        [
            jnp.concatenate([output_weight[:, :half], adapter_down, adapter_up[:own]], axis=1),
            jnp.concatenate(
                [output_weight[:, half:], adapter_up[own:], latent_weight[:own], latent_weight[own:]],
                axis=1,
            ),
        ]
    )
    packed = jnp.broadcast_to(packed[None], (xs,) + packed.shape).reshape(
        (xs * 2,) + packed.shape[1:]
    )
    packed = lax.all_to_all(packed, ("xh", "c"), 0, 0)
    here = lax.all_gather(packed, "z", axis=0)
    here = here.reshape(head_width, -1)
    there = lax.ppermute(here, "c", swap)

    flat_in = attended.reshape(rows, head_width)
    flat_in = (
        flat_in.reshape(rows, xs, zs, -1).transpose(0, 2, 1, 3).reshape(rows, head_width)
    )
    stream = residual.reshape(rows, width)
    stream = jnp.where(core == 0, stream, jnp.roll(stream, half, axis=1))
    terms = modulation[0]
    terms = jnp.where(core == 0, terms, jnp.roll(terms, half, axis=1))
    shift_term, scale_term, gate_term = terms[0:1], terms[1:2], terms[2:3]

    out_here = jnp.dot(flat_in, here, preferred_element_type=jnp.float32)
    out_there = jnp.dot(flat_in, there, preferred_element_type=jnp.float32)
    frozen_output = jnp.concatenate([out_here[:, :half], out_there[:, :half]], axis=1)
    down_projected = jnp.where(
        core == 0, out_here[:, half : half + rank], out_there[:, half : half + rank]
    ).astype(jnp.bfloat16)

    small0, small1 = by_core(core, here[:, half:], there[:, half:])
    up_parts = jnp.stack([small0[:, rank:], small1[:, :rank]], axis=1)
    last_parts = small1[:, rank:].reshape(head_width, 2, channels)

    def features(parts):
        parts = parts.reshape(zs, xs, 2, own, 2, -1).transpose(1, 0, 2, 4, 3, 5)
        parts = parts.reshape(xs, half, -1)
        parts = jnp.where(core == 0, parts, parts[::-1])
        return parts.reshape(width, -1)

    up_all = features(up_parts)
    final_all = features(last_parts)

    adapter_term = lax.dot_general(
        down_projected, up_all, (((1,), (1,)), ((), ())), preferred_element_type=jnp.float32
    )
    policy_model = frozen_output + ADAPTER_SCALE * adapter_term
    pred_pol, normed, inverse = head_out(
        stream, policy_model, gate_term, scale_term, shift_term, final_all
    )
    pred_ref, _, _ = head_out(stream, frozen_output, gate_term, scale_term, shift_term, final_all)
    mask_rows = jnp.broadcast_to(
        repaint_mask.astype(jnp.float32)[0, None, :, None], (kinds, tokens, 1)
    ).reshape(rows, 1)
    target_rows = targets.reshape(rows, channels).astype(jnp.float32)
    miss_pol = pred_pol - target_rows
    miss_ref = pred_ref - target_rows
    normaliser = float(tokens * seqs * channels)

    def by_kind(value):
        return jnp.sum(value.reshape(kinds, -1), axis=1)

    errors = jnp.concatenate(
        [by_kind(mask_rows * miss_pol * miss_pol), by_kind(mask_rows * miss_ref * miss_ref)]
    )
    errors = jnp.pad((errors / normaliser)[None, :], ((0, 7), (0, LANES - 2 * kinds)))
    summed = jnp.sum(spread(errors, TOKENS, seqs)[:, 0], axis=0)
    delta = summed[0] - summed[2] - (summed[1] - summed[3])
    weight_t = 2.0 - timesteps.astype(jnp.float32) / 1000.0
    logits = -DPO_BETA * weight_t * delta
    pair_loss = jax.nn.softplus(-logits)
    slope = jax.nn.sigmoid(-logits) * DPO_BETA * weight_t / normaliser
    signs = jnp.repeat(jnp.array([1.0, -1.0], jnp.float32), tokens)[:, None]
    grad_pred = (slope * signs * 2.0 * mask_rows * miss_pol).astype(jnp.bfloat16)
    gradient_delta = head_back(grad_pred, normed, inverse, gate_term, scale_term, final_all)
    up_gradient = ADAPTER_SCALE * lax.dot_general(
        gradient_delta, down_projected, (((0,), (0,)), ((), ())), preferred_element_type=jnp.float32
    )
    gradient_lowrank = (
        ADAPTER_SCALE * jnp.dot(gradient_delta, up_all, preferred_element_type=jnp.float32)
    ).astype(jnp.bfloat16)
    grad_down = lax.dot_general(
        flat_in, gradient_lowrank, (((0,), (0,)), ((), ())), preferred_element_type=jnp.float32
    )

    up_gradient = up_gradient.astype(jnp.bfloat16).reshape(xs, zs, 2, 2 * own, rank)
    up_gradient = jnp.where(core == 0, up_gradient, up_gradient[::-1])
    grad_down = grad_down.astype(jnp.bfloat16).reshape(zs, xs, 2, own, rank).transpose(1, 0, 2, 3, 4)
    grads = jnp.concatenate([grad_down, up_gradient], axis=3)
    grads = grads.reshape(xs * zs, 2, 3 * own, rank)
    mine, other = by_core(core, grads[:, 0], grads[:, 1])
    mine = mine.astype(jnp.float32) + lax.ppermute(other, "c", swap).astype(jnp.float32)
    piece = 3 * own // seqs
    mine = mine.astype(jnp.bfloat16).reshape(xs * zs, seqs, piece, rank).transpose(1, 0, 2, 3)
    mine = lax.all_to_all(mine, TOKENS, 0, 0)
    mine = jnp.sum(mine.astype(jnp.float32), axis=0).astype(jnp.bfloat16)
    mine = lax.all_to_all(mine, ("xh", "z"), 0, 0)
    mine = jnp.sum(mine.astype(jnp.float32), axis=0)
    mine = spread(mine, TOKENS, seqs).reshape(3 * own, rank)
    return (pair_loss, mine[:own], mine[own:])


def solution(mesh):
    seqs = mesh.shape["seq"]
    fsdp = mesh.shape["fsdp"]
    fine = Mesh(mesh.devices.reshape(2, fsdp // 4, 2, 2, seqs // 2), FINE)
    in_specs = (
        P(OWNERS, None, TOKENS, None),
        P(OWNERS, None, TOKENS, None),
        P(OWNERS, None, TOKENS, None),
        P(OWNERS, TOKENS),
        P(OWNERS),
        P(OWNERS, None, None),
        P(OWNERS, None),
        P(OWNERS, None),
        P(OWNERS, None),
        P(OWNERS, None),
    )
    out_specs = (P(OWNERS), P(OWNERS, None), P(OWNERS, None))
    return jax.shard_map(local, mesh=fine, in_specs=in_specs, out_specs=out_specs, check_vma=False)
```

time: 1040 us -> 226 us (0.22)
  the two profiles are of different devices: /device:TPU:4 before, /device:TPU:2 now
where the time goes in v1:
time: 226 us
  waiting for transfers between devices  98.1 us (43%)
  blocking collectives  51.8 us (23%)
  between operations  19.2 us (8%)
  matrix products  17.7 us (8%)
  starting transfers between devices  14.7 us (7%)
  local copies, waits for them, and re-layouts  13.3 us (6%)
  other arithmetic  10.8 us (5%)
    all_gather x1, waiting for transfers between devices, local(): here = lax.all_gather(packed, 'z', axis=0)  85.6 us
    all_to_all x1, blocking collectives, local(): mine = lax.all_to_all(mine, ('xh', 'z'), 0, 0)  26.1 us
    all_to_all x1, blocking collectives, local(): mine = lax.all_to_all(mine, TOKENS, 0, 0)  13.9 us
    all_to_all x1, blocking collectives, local(): packed = lax.all_to_all(packed, ('xh', 'c'), 0, 0)  11.9 us
    all_to_all x2, starting transfers between devices, spread(): lax.all_to_all(jnp.broadcast_to(value[None], (size,) + value.shape), axes...  10.8 us
    all_to_all x2, waiting for transfers between devices, spread(): lax.all_to_all(jnp.broadcast_to(value[None], (size,) + value.shape), axes...  9.07 us
  transfers between devices with their start and end apart: 5, of which 5 were waited for; matrix products, arithmetic and copies ran while one was open for 3% of the time, Pallas kernels for 0%

profile of v1, /device:TPU:2, one launch (start us, length us, event | category | flops | bytes accessed | tf_op | source)
XLA Modules:
  0.0 225.6 jit_solution(7027059049320119897)
XLA Ops:
  7.2 1.0 fusion.17
  10.5 11.9 %all_to_all.25 = bf16[4,24,1792]{2,1,0:T(8,128)(2,1)} all-to-all(bf16[4,24,1792]{2,1,0:T(8,128)(2,1)S(1)} %bitcast.114), channel_id=1, replica_groups=mesh['xh'=2,'z'=16,'c'=2,'xl'=2,'y'=4] {'xh','c'}, dimensions={0} | all-to-all | bytes 688128 | tf_op jit(solution)/shard_map/all_to_all | solution.py:88
  22.4 85.6 %all-gather.3.cloned.1.call-done = bf16[64,24,1792]{2,1,0:T(8,128)(2,1)} async-done(((bf16[4,24,1792]{2,1,0:T(8,128)(2,1)}), bf16[64,24,1792]{2,1,0:T(8,128)(2,1)}) %all-gather.3.cloned.1.call-update) | async-done | bytes 5505040 | tf_op jit(solution)/shard_map/all_gather | solution.py:89
  108.0 1.9 collective-permute-start
  113.4 4.2 %convolution_bitcast_fusion.1 = f32[256,1792]{1,0:T(8,128)S(1)} fusion(bf16[1536,1792]{1,0:T(8,128)(2,1)} %bitcast.126, bf16[256,1536]{0,1:T(8,128)(2,1)S(1)} %bitcast.102), kind=kOutput, calls=%fused_computation.15 | convolution fusion | flops 1409286144 | bytes 8126464 | tf_op jit(solution)/shard_map/dot_general | solution.py:103
  117.8 1.4 collective-permute-done
  119.3 4.2 %convolution_bitcast_fusion = f32[256,1792]{1,0:T(8,128)S(1)} fusion(bf16[1536,1792]{1,0:T(8,128)(2,1)} %collective-permute-done, bf16[256,1536]{0,1:T(8,128)(2,1)S(1)} %bitcast.103), kind=kOutput, calls=%fused_computation.14 | convolution fusion | flops 1409286144 | bytes 8126464 | tf_op jit(solution)/shard_map/dot_general | solution.py:104
  123.7 2.1 fusion.14
  127.2 1.0 fusion.22
  129.3 1.3 reshape_reshape.7
  130.6 1.3 copy.63
  132.1 1.9 fusion.9
  134.7 1.0 fusion.12
  138.4 5.7 %all-to-all-start.1 = ((f32[8,8,128]{2,1,0:T(8,128)}), f32[8,8,128]{2,1,0:T(8,128)S(1)}, u32[]{:S(2)}, u32[]{:S(2)}) async-start(f32[8,8,128]{2,1,0:T(8,128)} %broadcast_in_dim.18), calls=%async_computation.1 | async-start | bytes 65536 | tf_op jit(solution)/shard_map/all_to_all | solution.py:43
  144.8 4.2 %all-to-all-done.1 = f32[8,8,128]{2,1,0:T(8,128)S(1)} async-done(((f32[8,8,128]{2,1,0:T(8,128)}), f32[8,8,128]{2,1,0:T(8,128)S(1)}, u32[]{:S(2)}, u32[]{:S(2)}) %all-to-all-start.1) | async-done | bytes 32800 | tf_op jit(solution)/shard_map/all_to_all | solution.py:43
  152.3 2.2 fusion.11
  154.6 2.4 %multiply_convert_fusion = bf16[256,3072]{1,0:T(8,128)(2,1)} fusion(f32[256,3072]{1,0:T(8,128)S(1)} %get-tuple-element.33, f32[256,3072]{1,0:T(8,128)S(1)} %get-tuple-element.30, f32[256]{0:T(256)S(1)} %broadcast_multiply_fusion.1, f32[256]{0:T(256)S(1)} %broadcast_multiply_fusion.2, f32[256]{0:T(256)S(1)} %copy-done.24, f32[256]{0:T(256)S(1)} %broadcast_multiply_fusion.3, ...), kind=kLoop, calls=%fused_computation.7 | loop fusion | flops 6291456 | bytes 7880704 | tf_op jit(solution)/shard_map/convert_element_type | solution.py:39
  157.0 2.9 %fusion.3 = bf16[1536,128]{0,1:T(8,128)(2,1)S(1)} fusion(bf16[256,1536]{0,1:T(8,128)(2,1)} %bitcast.104, bf16[256,3072]{1,0:T(8,128)(2,1)} %multiply_convert_fusion, bf16[3072,128]{1,0:T(8,128)(2,1)} %bitcast.98), kind=kOutput, calls=%fused_computation.17 | convolution fusion | flops 302219264 | bytes 3538944 | tf_op jit(solution)/shard_map/dot_general | solution.py:161
  161.4 1.9 collective-permute-start.1
  163.4 2.0 collective-permute-done.1
  165.6 13.9 %all_to_all.26 = bf16[8,32,9,128]{3,1,2,0:T(8,128)(2,1)S(1)} all-to-all(bf16[8,32,9,128]{3,1,2,0:T(8,128)(2,1)S(1)} %bitcast.110), channel_id=1, replica_groups=mesh['xh'=2,'z'=16,'c'=2,'xl'=2,'y'=4] {'xl','y'}, dimensions={0} | all-to-all | bytes 1179648 | tf_op jit(solution)/shard_map/all_to_all | solution.py:174
  179.6 26.1 %all_to_all.27 = bf16[32,9,128]{2,1,0:T(8,128)(2,1)S(1)} all-to-all(bf16[32,9,128]{2,1,0:T(8,128)(2,1)S(1)} %copy.69), channel_id=1, replica_groups=mesh['xh'=2,'z'=16,'c'=2,'xl'=2,'y'=4] {'xh','z'}, dimensions={0} | all-to-all | bytes 147456 | tf_op jit(solution)/shard_map/all_to_all | solution.py:176
  206.4 5.1 %all-to-all-start.4 = ((f32[8,9,128]{2,1,0:T(8,128)}), f32[8,9,128]{2,1,0:T(8,128)S(1)}, u32[]{:S(2)}, u32[]{:S(2)}) async-start(f32[8,9,128]{2,1,0:T(8,128)} %broadcast_in_dim.20), calls=%async_computation.4 | async-start | bytes 131072 | tf_op jit(solution)/shard_map/all_to_all | solution.py:43
  211.5 4.9 %all-to-all-done.4 = f32[8,9,128]{2,1,0:T(8,128)S(1)} async-done(((f32[8,9,128]{2,1,0:T(8,128)}), f32[8,9,128]{2,1,0:T(8,128)S(1)}, u32[]{:S(2)}, u32[]{:S(2)}) %all-to-all-start.4) | async-done | bytes 36896 | tf_op jit(solution)/shard_map/all_to_all | solution.py:43
  (121 shorter events, 16.4 us)
Async XLA Ops:
  7.2 102.8 %copy-start.15 = (bf16[1,2,128,1536]{3,2,1,0:T(8,128)(2,1)S(1)}, bf16[1,2,128,1536]{3,2,1,0:T(8,128)(2,1)}, u32[]{:S(2)}) copy-start(bf16[1,2,128,1536]{3,2,1,0:T(8,128)(2,1)} %param.11) | copy-start | bytes 2359300
  7.2 100.8 %all-gather.3.cloned.1.call-start = ((), (), s32[]{:S(2)}) async-start(), calls=%async_computation.5 | async-start | bytes 5849088 | tf_op jit(solution)/shard_map/all_gather | solution.py:89
  10.4 100.7 %copy-start.21 = (f32[1,3,3072]{2,0,1:T(1,128)S(1)}, f32[1,3,3072]{2,0,1:T(1,128)}, u32[]{:S(2)}) copy-start(f32[1,3,3072]{2,0,1:T(1,128)} %param.16) | copy-start | bytes 110596
  10.5 100.7 %copy-start.23 = (bf16[1,2,128,64]{2,3,1,0:T(8,128)(2,1)S(1)}, bf16[1,2,128,64]{2,3,1,0:T(8,128)(2,1)}, u32[]{:S(2)}) copy-start(bf16[1,2,128,64]{2,3,1,0:T(8,128)(2,1)} %param.13) | copy-start | bytes 98308
  10.5 101.4 %copy-start.28 = (s32[1,128]{1,0:T(1,128)S(1)}, s32[1,128]{1,0:T(1,128)}, u32[]{:S(2)}) copy-start(s32[1,128]{1,0:T(1,128)} %param.14) | copy-start | bytes 1540
  10.5 102.0 %copy-start.1 = (bf16[1,2,128,3072]{3,2,1,0:T(8,128)(2,1)S(1)}, bf16[1,2,128,3072]{3,2,1,0:T(8,128)(2,1)}, u32[]{:S(2)}) copy-start(bf16[1,2,128,3072]{3,2,1,0:T(8,128)(2,1)} %param.12) | copy-start | bytes 4718596
  108.0 11.3 %collective-permute-start = (bf16[1536,1792]{1,0:T(8,128)(2,1)}, bf16[1536,1792]{1,0:T(8,128)(2,1)}, u32[]{:S(2)}, u32[]{:S(2)}) collective-permute-start(bf16[1536,1792]{1,0:T(8,128)(2,1)} %bitcast.125), channel_id=1, source_target_pairs={{0,8},{8,0},{1,9},{9,1},{2,10},{10,2},{3,11},{11,3},{4,12},{12,4},... | collective-permute-start | bytes 16515080 | tf_op jit(solution)/shard_map/ppermute | solution.py:91
  111.1 8.1 %copy-start.14 = (bf16[256,16,2,48]{0,3,2,1:T(8,128)(2,1)}, bf16[256,16,2,48]{0,3,2,1:T(8,128)(2,1)S(1)}, u32[]{:S(2)}) copy-start(bf16[256,16,2,48]{0,3,2,1:T(8,128)(2,1)S(1)} %copy.61) | copy-start | bytes 2359300
  112.6 13.6 %copy-start.10 = (bf16[256,1536]{1,0:T(8,128)(2,1)}, bf16[256,1536]{1,0:T(8,128)(2,1)S(1)}, u32[]{:S(2)}) copy-start(bf16[256,1536]{1,0:T(8,128)(2,1)S(1)} %get-tuple-element.10) | copy-start | bytes 2359300
  112.7 13.6 %copy-start.12 = (bf16[256,1536]{1,0:T(8,128)(2,1)}, bf16[256,1536]{1,0:T(8,128)(2,1)S(1)}, u32[]{:S(2)}) copy-start(bf16[256,1536]{1,0:T(8,128)(2,1)S(1)} %get-tuple-element.11) | copy-start | bytes 2359300
  113.4 12.9 %copy-start.19 = (f32[1,3072]{1,0:T(1,128)}, f32[1,3072]{1,0:T(1,128)S(1)}, u32[]{:S(2)}) copy-start(f32[1,3072]{1,0:T(1,128)S(1)} %get-tuple-element.18) | copy-start | bytes 36868
  117.8 8.5 %copy-start.4 = (f32[256,1536]{1,0:T(8,128)}, f32[256,1536]{1,0:T(8,128)S(1)}, u32[]{:S(2)}) copy-start(f32[256,1536]{1,0:T(8,128)S(1)} %slice.133) | copy-start | bytes 4718596
  123.5 2.8 %copy-start.16 = (bf16[256,128]{1,0:T(8,128)(2,1)}, bf16[256,128]{1,0:T(8,128)(2,1)S(1)}, u32[]{:S(2)}) copy-start(bf16[256,128]{1,0:T(8,128)(2,1)S(1)} %fusion.7) | copy-start | bytes 196612
  130.5 3.6 %copy-start.13 = (bf16[256,1536]{1,0:T(8,128)(2,1)S(1)}, bf16[256,1536]{1,0:T(8,128)(2,1)}, u32[]{:S(2)}) copy-start(bf16[256,1536]{1,0:T(8,128)(2,1)} %copy-done.12) | copy-start | bytes 2359300
  131.9 2.8 %copy-start.11 = (bf16[256,1536]{1,0:T(8,128)(2,1)S(1)}, bf16[256,1536]{1,0:T(8,128)(2,1)}, u32[]{:S(2)}) copy-start(bf16[256,1536]{1,0:T(8,128)(2,1)} %copy-done.10) | copy-start | bytes 2359300
  131.9 2.8 %copy-start.20 = (f32[1,3072]{1,0:T(1,128)S(1)}, f32[1,3072]{1,0:T(1,128)}, u32[]{:S(2)}) copy-start(f32[1,3072]{1,0:T(1,128)} %copy-done.19) | copy-start | bytes 36868
  132.1 4.8 %copy-start.8 = (bf16[2,1536,64]{2,1,0:T(8,128)(2,1)}, bf16[2,1536,64]{2,1,0:T(8,128)(2,1)S(1)}, u32[]{:S(2)}) copy-start(bf16[2,1536,64]{2,1,0:T(8,128)(2,1)S(1)} %reverse_select_fusion.1) | copy-start | bytes 1179652
  136.2 16.1 %copy-start.29 = (f32[2]{0:T(128)S(1)}, f32[2]{0:T(128)}, u32[]{:S(2)}) copy-start(f32[2]{0:T(128)} %constant.49.clone) | copy-start | bytes 28
  136.2 16.1 %copy-start.27 = (f32[128]{0:T(128)S(1)}, f32[128]{0:T(128)}, u32[]{:S(2)}) copy-start(f32[128]{0:T(128)} %copy-done.26) | copy-start | bytes 1540
  138.4 10.6 %all-to-all-start.1 = ((f32[8,8,128]{2,1,0:T(8,128)}), f32[8,8,128]{2,1,0:T(8,128)S(1)}, u32[]{:S(2)}, u32[]{:S(2)}) async-start(f32[8,8,128]{2,1,0:T(8,128)} %broadcast_in_dim.18), calls=%async_computation.1 | async-start | bytes 65536 | tf_op jit(solution)/shard_map/all_to_all | solution.py:43
  157.0 2.9 %copy-start = (bf16[256,3072]{1,0:T(8,128)(2,1)S(1)}, bf16[256,3072]{1,0:T(8,128)(2,1)}, u32[]{:S(2)}) copy-start(bf16[256,3072]{1,0:T(8,128)(2,1)} %multiply_convert_fusion) | copy-start | bytes 4718596
  157.0 2.9 %copy-start.17 = (bf16[256,128]{1,0:T(8,128)(2,1)S(1)}, bf16[256,128]{1,0:T(8,128)(2,1)}, u32[]{:S(2)}) copy-start(bf16[256,128]{1,0:T(8,128)(2,1)} %copy-done.16) | copy-start | bytes 196612
  161.4 3.9 %collective-permute-start.1 = (bf16[32,72,128]{2,0,1:T(8,128)(2,1)S(1)}, bf16[32,72,128]{2,0,1:T(8,128)(2,1)S(1)}, u32[]{:S(2)}, u32[]{:S(2)}) collective-permute-start(bf16[32,72,128]{2,0,1:T(8,128)(2,1)S(1)} %select_bitcast_fusion), channel_id=1, source_target_pairs={{0,8},{8,0},{1,9},{9,1},{2,10},{10,2},{3,11},{11,3},{4,12},{12,4},... | collective-permute-start | bytes 1769480 | tf_op jit(solution)/shard_map/ppermute | solution.py:171
  206.4 10.0 %all-to-all-start.4 = ((f32[8,9,128]{2,1,0:T(8,128)}), f32[8,9,128]{2,1,0:T(8,128)S(1)}, u32[]{:S(2)}, u32[]{:S(2)}) async-start(f32[8,9,128]{2,1,0:T(8,128)} %broadcast_in_dim.20), calls=%async_computation.4 | async-start | bytes 131072 | tf_op jit(solution)/shard_map/all_to_all | solution.py:43
  (11 other events, 19.3 us)
Sparse Core Ops, SparseCore 0:
  22.5 85.4 all-gather.2

commit v2 on v1

v2 whole, which is shorter than its diff:
```python
import jax
import jax.numpy as jnp
from jax import lax
from jax.sharding import Mesh
from jax.sharding import PartitionSpec as P

NORM_EPS = 1e-06
DPO_BETA = 10.0
ADAPTER_SCALE = 1.0
FINE = ("xh", "z", "c", "xl", "y")
OWNERS = ("xh", "z", "c")
TOKENS = ("xl", "y")
F32 = jnp.float32
BF16 = jnp.bfloat16
SWAP = [(0, 1), (1, 0)]


def exact_dot(a, b):
    return jnp.dot(a, b, preferred_element_type=F32, precision=lax.Precision.HIGHEST)


def dot(a, b):
    return jnp.dot(a, b, preferred_element_type=F32)


def dot_t(a, b):
    return lax.dot_general(a, b, (((1,), (1,)), ((), ())), preferred_element_type=F32)


def t_dot(a, b):
    return lax.dot_general(a, b, (((0,), (0,)), ((), ())), preferred_element_type=F32)


def spread(value, axes, size):
    return lax.all_to_all(jnp.broadcast_to(value[None], (size,) + value.shape), axes, 0, 0)


def gather_small(down, up, last, zs, seqs, core, seq):
    own, rank = down.shape
    channels = last.shape[1]
    packed = jnp.concatenate(
        [down, up, jnp.concatenate([last[:own], last[own:]], axis=1)], axis=0
    )
    piece = 4 * own // (2 * seqs)
    packed = packed.reshape(2, seqs, piece, rank)
    packed = lax.dynamic_index_in_dim(packed, seq, 1, keepdims=False)
    packed = jnp.broadcast_to(packed[None], (2 * zs,) + packed.shape)
    packed = lax.all_to_all(packed.reshape((4 * zs, piece, rank)), OWNERS, 0, 0)
    here = spread(packed, TOKENS, seqs)
    there = lax.ppermute(here, "c", SWAP)
    both = jnp.where(core == 0, jnp.stack([here, there]), jnp.stack([there, here]))
    both = both.reshape(2 * seqs, 4 * zs, piece, rank).transpose(1, 0, 2, 3)
    both = both.reshape(4 * zs, 4 * own, rank)
    down = both[:, :own].reshape(-1, rank)
    up = both[:, own : 3 * own].reshape(-1, rank)
    last = both[:, 3 * own :].reshape(4 * zs, own, 2, channels).transpose(0, 2, 1, 3)
    return down, up, last.reshape(-1, channels)


def local(
    attended,
    residual,
    targets,
    repaint_mask,
    timesteps,
    modulation,
    output_weight,
    adapter_down,
    adapter_up,
    latent_weight,
):
    _, kinds, tokens, depth = attended.shape
    width = residual.shape[-1]
    channels = targets.shape[-1]
    rank = adapter_down.shape[1]
    rows = kinds * tokens
    own = output_weight.shape[0]
    zs, ys = lax.axis_size("z"), lax.axis_size("y")
    seqs = 2 * ys
    xh, core = lax.axis_index("xh"), lax.axis_index("c")
    normaliser = float(tokens * seqs * channels)

    pair = lax.ppermute(output_weight, "xh", SWAP)
    pair = jnp.where(
        xh == 0, jnp.stack([output_weight, pair]), jnp.stack([pair, output_weight])
    )
    here = lax.all_gather(pair, "z", axis=0).reshape(depth // 2, width)

    down_all, up_all, final_all = gather_small(
        adapter_down, adapter_up, latent_weight, zs, seqs, core, lax.axis_index(TOKENS)
    )
    flat_in = attended.reshape(rows, depth)
    in_cores = flat_in.reshape(rows, 2, zs, 2, own).transpose(3, 0, 2, 1, 4)
    in_cores = in_cores.reshape(2, rows, depth // 2)
    in_here = jnp.where(core == 0, in_cores[0], in_cores[1])
    in_there = jnp.where(core == 0, in_cores[1], in_cores[0])
    stream = residual.reshape(rows, width).astype(F32)
    shift, scale, gate = modulation[0, 0:1], 1.0 + modulation[0, 1:2], modulation[0, 2:3]
    final32 = final_all.astype(F32)
    scale_final, shift_final = exact_dot(scale, final32), exact_dot(shift, final32)
    down_projected = dot(flat_in, down_all).astype(BF16)
    adapter_term = ADAPTER_SCALE * dot_t(down_projected, up_all)

    here, in_here, in_there, final_all, up_all, down_projected, adapter_term = (
        lax.optimization_barrier(
            (here, in_here, in_there, final_all, up_all, down_projected, adapter_term)
        )
    )
    there = lax.ppermute(here, "c", SWAP)
    frozen = dot(in_here, here) + dot(in_there, there)
    hidden_ref = stream + gate * frozen
    hidden_pol = hidden_ref + gate * adapter_term

    def head_out(hidden):
        centred = hidden - jnp.mean(hidden, axis=-1, keepdims=True)
        variance = jnp.mean(centred * centred, axis=-1, keepdims=True)
        inverse = lax.rsqrt(variance + NORM_EPS)
        normed = centred * inverse
        return dot((normed * scale + shift).astype(BF16), final_all), normed, inverse

    pred_pol, normed, inverse = head_out(hidden_pol)
    pred_ref, _, _ = head_out(hidden_ref)
    target_rows = targets.reshape(rows, channels).astype(F32)
    miss_pol = pred_pol - target_rows
    miss_ref = pred_ref - target_rows
    mask_rows = jnp.broadcast_to(repaint_mask.astype(F32)[0], (kinds, tokens)).reshape(rows, 1)

    def by_kind(value):
        return jnp.sum(value.reshape(kinds, -1), axis=1)

    errors = jnp.concatenate(
        [by_kind(mask_rows * miss_pol * miss_pol), by_kind(mask_rows * miss_ref * miss_ref)]
    )
    weight_t = (2.0 - timesteps.astype(F32) / 1000.0) / seqs
    errors = jnp.concatenate([errors / normaliser, weight_t])
    errors = jnp.pad(errors[None, :], ((0, 7), (0, 127 - 2 * kinds)))
    errors, miss_pol = lax.optimization_barrier((errors, miss_pol))
    errors = spread(errors, ("c",) + TOKENS, 2 * seqs)[:, 0]
    errors = jnp.sum(errors.reshape(2, seqs, 128), axis=1)
    delta = errors[:, 0] - errors[:, 2] - (errors[:, 1] - errors[:, 3])
    weight_t = errors[:, 4]
    logits = -DPO_BETA * weight_t * delta
    pair_loss = lax.dynamic_slice_in_dim(jax.nn.softplus(-logits), core, 1)
    slope = jax.nn.sigmoid(-logits) * DPO_BETA * weight_t / normaliser
    slope_here = jnp.where(core == 0, slope[0], slope[1])
    slope_there = jnp.where(core == 0, slope[1], slope[0])

    signs = jnp.repeat(jnp.array([2.0, -2.0], F32), tokens)[:, None]
    grad_pred = (signs * mask_rows * miss_pol).astype(BF16)
    grad32 = grad_pred.astype(F32)
    first = jnp.sum(grad32 * scale_final, axis=1, keepdims=True) / width
    second = jnp.sum(grad32 * (pred_pol - shift_final), axis=1, keepdims=True) / width
    grad_norm = dot_t(grad_pred, final_all) * scale
    update = (gate * (inverse * (grad_norm - first - normed * second))).astype(BF16)
    up_gradient = ADAPTER_SCALE * t_dot(update, down_projected)
    grad_low = (ADAPTER_SCALE * dot(update, up_all)).astype(BF16)
    down_here = t_dot(in_here, grad_low)
    down_there = t_dot(in_there, grad_low)

    up_gradient = up_gradient.reshape(2, zs, 2, 2 * own, rank)
    up_here = jnp.where(core == 0, up_gradient[:, :, 0], up_gradient[:, :, 1])
    up_there = jnp.where(core == 0, up_gradient[:, :, 1], up_gradient[:, :, 0])

    def by_owner(down, up):
        down = down.reshape(zs, 2, own, rank).transpose(1, 0, 2, 3)
        return jnp.concatenate([down, up], axis=2)

    grads = by_owner(down_there, up_there).astype(BF16)
    grads = lax.ppermute(grads, "c", SWAP).astype(F32)
    grads = slope_here * by_owner(down_here, up_here) + slope_there * grads
    piece = 3 * own // seqs
    grads = grads.astype(BF16).reshape(2, zs, seqs, piece, rank).transpose(0, 2, 1, 3, 4)
    grads = lax.all_to_all(grads.reshape(2 * seqs, zs, piece, rank), ("xh",) + TOKENS, 0, 0)
    grads = jnp.sum(grads.astype(F32), axis=0).astype(BF16)
    grads = jnp.sum(lax.all_to_all(grads, "z", 0, 0).astype(F32), axis=0)
    grads = spread(grads, TOKENS, seqs).reshape(3 * own, rank)
    return (pair_loss, grads[:own], grads[own:])


def solution(mesh):
    seqs = mesh.shape["seq"]
    fsdp = mesh.shape["fsdp"]
    fine = Mesh(mesh.devices.reshape(2, fsdp // 4, 2, 2, seqs // 2), FINE)
    in_specs = (
        P(OWNERS, None, TOKENS, None),
        P(OWNERS, None, TOKENS, None),
        P(OWNERS, None, TOKENS, None),
        P(OWNERS, TOKENS),
        P(OWNERS),
        P(OWNERS, None, None),
        P(OWNERS, None),
        P(OWNERS, None),
        P(OWNERS, None),
        P(OWNERS, None),
    )
    out_specs = (P(OWNERS), P(OWNERS, None), P(OWNERS, None))
    return jax.shard_map(local, mesh=fine, in_specs=in_specs, out_specs=out_specs, check_vma=False)
```

time: 226 us -> 200 us (0.88)
  waiting for transfers between devices: 98.1 us -> 29.2 us
  blocking collectives: 51.8 us -> 92 us
  starting transfers between devices: 14.7 us -> 21.2 us
    all_gather x1, waiting for transfers between devices: 85.6 us -> 16.7 us  [local(): here = lax.all_gather(pair, 'z', axis=0).reshape(depth // 2, width)]
    all_to_all x3 -> x4, blocking collectives: 51.8 us -> 92 us  [the longest x1 37.2 us: gather_small(): packed = lax.all_to_all(packed.reshape((4 * zs, piece, rank)), OWNERS, 0, 0)]
    ppermute x2 -> x4, starting transfers between devices: 3.83 us -> 10.2 us  [the longest x1 4.16 us: local(): pair = lax.ppermute(output_weight, 'xh', SWAP)]
    select_n x5, other arithmetic: 0.56 us -> 6.56 us  [the longest x1 2.2 us: gather_small(): jnp.where(core == 0, jnp.stack([here, there]), jnp.stack([there, here]))]
    reshape x1 -> x6, local copies, waits for them, and re-layouts: 0.01 us -> 3.53 us  [the longest x2 3.32 us: gather_small(): both[:, 3 * own:].reshape(4 * zs, own, 2, channels).transpose(0, 2, 1, 3)]
    convert_element_type x4 -> x1, other arithmetic: 3.37 us -> 0.2 us  [local(): grads.astype(BF16).reshape(2, zs, seqs, piece, rank)]
    ppermute x2 -> x4, waiting for transfers between devices: 3.39 us -> 6.47 us  [the longest x1 5.15 us: local(): pair = lax.ppermute(output_weight, 'xh', SWAP)]
    all_to_all x2, waiting for transfers between devices: 9.07 us -> 6.04 us  [spread(): lax.all_to_all(jnp.broadcast_to(value[None], (size,) + value.shape), axes...]
  transfers between devices with their start and end apart: 5 -> 7, of which waited for: 5 -> 5; matrix products, arithmetic and copies ran while one was open for 3% -> 12% of each run, Pallas kernels for 0% -> 0%
where the time goes in v2:
time: 200 us; the launch traced here: 199 us
  blocking collectives  92 us (46%)
  waiting for transfers between devices  29.2 us (15%)
  starting transfers between devices  21.2 us (11%)
  between operations  17.7 us (9%)
  matrix products  15.6 us (8%)
  local copies, waits for them, and re-layouts  12.6 us (6%)
  other arithmetic  10.5 us (5%)
    all_to_all x1, blocking collectives, gather_small(): packed = lax.all_to_all(packed.reshape((4 * zs, piece, rank)), OWNERS, 0, 0)  37.2 us
    all_to_all x1, blocking collectives, local(): grads = jnp.sum(lax.all_to_all(grads, 'z', 0, 0).astype(F32), axis=0)  19.7 us
    all_to_all x1, blocking collectives, spread(): lax.all_to_all(jnp.broadcast_to(value[None], (size,) + value.shape), axes...  17.7 us
    all_to_all x1, blocking collectives, local(): lax.all_to_all(grads.reshape(2 * seqs, zs, piece, rank), ('xh',) + TOKENS...  17.4 us
    all_gather x1, waiting for transfers between devices, local(): here = lax.all_gather(pair, 'z', axis=0).reshape(depth // 2, width)  16.7 us
    all_to_all x2, starting transfers between devices, spread(): lax.all_to_all(jnp.broadcast_to(value[None], (size,) + value.shape), axes...  10.9 us
    dot_general x6, matrix products, dot(): return jnp.dot(a, b, preferred_element_type=F32)  8.62 us
    all_to_all x2, waiting for transfers between devices, spread(): lax.all_to_all(jnp.broadcast_to(value[None], (size,) + value.shape), axes...  6.04 us
  transfers between devices with their start and end apart: 7, of which 5 were waited for; matrix products, arithmetic and copies ran while one was open for 12% of the time, Pallas kernels for 0%

profile of v2, /device:TPU:2, one launch (start us, length us, event | category | flops | bytes accessed | tf_op | source)
XLA Modules:
  0.0 199.0 jit_solution(11817495430422430929)
XLA Ops:
  7.2 4.2 %collective-permute-start = (bf16[24,3072]{1,0:T(8,128)(2,1)}, bf16[24,3072]{1,0:T(8,128)(2,1)S(1)}, u32[]{:S(2)}, u32[]{:S(2)}) collective-permute-start(bf16[24,3072]{1,0:T(8,128)(2,1)} %param.17), channel_id=1, source_target_pairs={{0,256},{256,0},{1,257},{257,1},{2,258},{258,2},{3,259},{259,3},{4... | collective-permute-start | bytes 442376 | tf_op jit(solution)/shard_map/ppermute | solution.py:83
  11.4 5.1 %collective-permute-done = bf16[24,3072]{1,0:T(8,128)(2,1)S(1)} collective-permute-done((bf16[24,3072]{1,0:T(8,128)(2,1)}, bf16[24,3072]{1,0:T(8,128)(2,1)S(1)}, u32[]{:S(2)}, u32[]{:S(2)}) %collective-permute-start) | collective-permute-done | bytes 147488 | tf_op jit(solution)/shard_map/ppermute | solution.py:83
  16.5 1.8 maximum_select_fusion.1
  19.9 37.2 %all_to_all.30 = bf16[64,6,128]{2,1,0:T(8,128)(2,1)S(1)} all-to-all(bf16[64,6,128]{2,1,0:T(8,128)(2,1)S(1)} %bitcast.138), channel_id=1, replica_groups=mesh['xh'=2,'z'=16,'c'=2,'xl'=2,'y'=4] {'xh','z','c'}, dimensions={0} | all-to-all | bytes 196608 | tf_op jit(solution)/shard_map/all_to_all | solution.py:48
  57.4 17.7 %all_to_all.31 = bf16[8,64,6,128]{3,1,2,0:T(8,128)(2,1)} all-to-all(bf16[8,64,6,128]{3,1,2,0:T(8,128)(2,1)S(1)} %broadcast_in_dim.19), channel_id=1, replica_groups=mesh['xh'=2,'z'=16,'c'=2,'xl'=2,'y'=4] {'xl','y'}, dimensions={0} | all-to-all | bytes 1572864 | tf_op jit(solution)/shard_map/all_to_all | solution.py:35
  75.0 1.9 collective-permute-start.1
  78.2 1.3 collective-permute-done.1
  79.6 2.2 %maximum_select_fusion = bf16[2,8,64,6,128]{4,2,3,1,0:T(8,128)(2,1)S(1)} fusion(bf16[1,8,64,6,128]{4,2,3,1,0:T(8,128)(2,1)} %bitcast.13, bf16[1,8,64,6,128]{4,2,3,1,0:T(8,128)(2,1)} %bitcast.12, pred[]{:T(512)S(6)} %eq.5), kind=kLoop, calls=%fused_computation.14 | loop fusion | flops 2359296 | bytes 3145729 | tf_op jit(solution)/shard_map/jit(_where)/select_n | solution.py:51
  82.7 1.2 reshape.218
  83.9 2.1 %copy.107 = bf16[64,24,2,64]{3,1,2,0:T(8,128)(2,1)S(1)} copy(bf16[64,24,2,64]{3,2,0,1:T(2,128)(2,1)} %reshape.218) | data formatting | bytes 786432 | tf_op jit(solution)/shard_map/reshape | solution.py:56
  87.0 2.3 %fusion.26 = f32[256,3072]{1,0:T(8,128)} fusion(bf16[128,256]{1,0:T(8,128)(2,1)S(1)} %convolution_convert_fusion.1, bf16[3072,128]{1,0:T(8,128)(2,1)S(1)} %bitcast.117), kind=kOutput, calls=%fused_computation.77 | convolution fusion | flops 201326592 | bytes 3997696 | tf_op jit(solution)/shard_map/dot_general | solution.py:27
  89.3 16.7 %all-gather.2.cloned.1.call-done = bf16[16,2,24,3072]{3,2,1,0:T(8,128)(2,1)} async-done(((bf16[1,2,24,3072]{3,2,1,0:T(8,128)(2,1)}), bf16[16,2,24,3072]{3,2,1,0:T(8,128)(2,1)}) %all-gather.2.cloned.1.call-update) | async-done | bytes 4718608 | tf_op jit(solution)/shard_map/all_gather | solution.py:87
  106.0 2.1 %collective-permute-start.2 = (bf16[768,3072]{1,0:T(8,128)(2,1)}, bf16[768,3072]{1,0:T(8,128)(2,1)S(1)}, u32[]{:S(2)}, u32[]{:S(2)}) collective-permute-start(bf16[768,3072]{1,0:T(8,128)(2,1)} %bitcast.115), channel_id=1, source_target_pairs={{0,8},{8,0},{1,9},{9,1},{2,10},{10,2},{3,11},{11,3},{4,12},{12,4},... | collective-permute-start | bytes 14155784 | tf_op jit(solution)/shard_map/ppermute | solution.py:109
  112.7 3.9 %fusion.27 = f32[256,3072]{1,0:T(8,128)S(1)} fusion(bf16[256,768]{0,1:T(8,128)(2,1)S(1)} %bitcast.122, bf16[768,3072]{1,0:T(8,128)(2,1)} %bitcast.116), kind=kOutput, calls=%fused_computation.78 | convolution fusion | flops 1207959552 | bytes 8257536 | tf_op jit(solution)/shard_map/dot_general | solution.py:23
  116.6 2.1 %fusion.25 = (f32[256]{0:T(256)S(1)}, f32[256,3072]{1,0:T(8,128)S(1)}) fusion(f32[256,3072]{1,0:T(8,128)S(1)} %fusion.27, bf16[256,768]{0,1:T(8,128)(2,1)S(1)} %bitcast.124, bf16[768,3072]{1,0:T(8,128)(2,1)S(1)} %collective-permute-done.2, f32[3072]{0:T(1024)S(1)} %bitcast.144, bf16[256,3072]{1,0:T(8,128)(2,1)S(1)} %bitcast.132), kind=kOutput, calls=%fused_computation.76 | convolution fusion | flops 1211891456 | bytes 12989440 | tf_op jit(solution)/shard_map/dot_general | solution.py:23
  122.2 1.4 fusion.6
  125.5 1.3 select_bitcast_fusion
  127.5 6.2 %all-to-all-start.2 = ((f32[16,8,128]{2,1,0:T(8,128)}), f32[16,8,128]{2,1,0:T(8,128)}, u32[]{:S(2)}, u32[]{:S(2)}) async-start(f32[16,8,128]{2,1,0:T(8,128)} %broadcast_in_dim.21), calls=%async_computation.2 | async-start | bytes 131072 | tf_op jit(solution)/shard_map/all_to_all | solution.py:35
  134.8 2.1 %collective-permute-start.3 = (bf16[2,16,72,128]{3,1,2,0:T(8,128)(2,1)S(1)}, bf16[2,16,72,128]{3,1,2,0:T(8,128)(2,1)S(1)}, u32[]{:S(2)}, u32[]{:S(2)}) collective-permute-start(bf16[2,16,72,128]{3,1,2,0:T(8,128)(2,1)S(1)} %pad_maximum_fusion), channel_id=1, source_target_pairs={{0,8},{8,0},{1,9},{9,1},{2,10},{10,2},{3,11},{11,3},{4,12},{12,4},... | collective-permute-start | bytes 1769480 | tf_op jit(solution)/shard_map/ppermute | solution.py:169
  137.2 1.7 all-to-all-done.2
  143.4 17.4 %all_to_all.32 = bf16[16,16,9,128]{3,1,2,0:T(8,128)(2,1)S(1)} all-to-all(bf16[16,16,9,128]{3,1,2,0:T(8,128)(2,1)S(1)} %bitcast.128), channel_id=1, replica_groups=mesh['xh'=2,'z'=16,'c'=2,'xl'=2,'y'=4] {'xh','xl','y'}, dimensions={0} | all-to-all | bytes 1179648 | tf_op jit(solution)/shard_map/all_to_all | solution.py:173
  160.9 19.7 %all_to_all.33 = bf16[16,9,128]{2,1,0:T(8,128)(2,1)S(1)} all-to-all(bf16[16,9,128]{2,1,0:T(8,128)(2,1)S(1)} %copy.115), channel_id=1, replica_groups=mesh['xh'=2,'z'=16,'c'=2,'xl'=2,'y'=4] {'z'}, dimensions={0} | all-to-all | bytes 73728 | tf_op jit(solution)/shard_map/all_to_all | solution.py:175
  181.3 4.7 %all-to-all-start.5 = ((f32[8,9,128]{2,1,0:T(8,128)}), f32[8,9,128]{2,1,0:T(8,128)S(1)}, u32[]{:S(2)}, u32[]{:S(2)}) async-start(f32[8,9,128]{2,1,0:T(8,128)} %broadcast_in_dim.23), calls=%async_computation.5 | async-start | bytes 131072 | tf_op jit(solution)/shard_map/all_to_all | solution.py:35
  186.5 4.4 %all-to-all-done.5 = f32[8,9,128]{2,1,0:T(8,128)S(1)} async-done(((f32[8,9,128]{2,1,0:T(8,128)}), f32[8,9,128]{2,1,0:T(8,128)S(1)}, u32[]{:S(2)}, u32[]{:S(2)}) %all-to-all-start.5) | async-done | bytes 36896 | tf_op jit(solution)/shard_map/all_to_all | solution.py:35
  (89 shorter events, 20.6 us)
Async XLA Ops:
  7.2 69.8 %copy-start.3 = (bf16[1,2,128,1536]{3,2,1,0:T(8,128)(2,1)S(1)}, bf16[1,2,128,1536]{3,2,1,0:T(8,128)(2,1)}, u32[]{:S(2)}) copy-start(bf16[1,2,128,1536]{3,2,1,0:T(8,128)(2,1)} %param.11) | copy-start | bytes 2359300
  7.2 98.8 %all-gather.2.cloned.1.call-start = ((), (), s32[]{:S(2)}) async-start(), calls=%async_computation.6 | async-start | bytes 5013504 | tf_op jit(solution)/shard_map/all_gather | solution.py:87
  7.2 9.3 %collective-permute-start = (bf16[24,3072]{1,0:T(8,128)(2,1)}, bf16[24,3072]{1,0:T(8,128)(2,1)S(1)}, u32[]{:S(2)}, u32[]{:S(2)}) collective-permute-start(bf16[24,3072]{1,0:T(8,128)(2,1)} %param.17), channel_id=1, source_target_pairs={{0,256},{256,0},{1,257},{257,1},{2,258},{258,2},{3,259},{259,3},{4... | collective-permute-start | bytes 442376 | tf_op jit(solution)/shard_map/ppermute | solution.py:83
  75.0 4.5 %collective-permute-start.1 = (bf16[8,64,6,128]{3,1,2,0:T(8,128)(2,1)}, bf16[8,64,6,128]{3,1,2,0:T(8,128)(2,1)}, u32[]{:S(2)}, u32[]{:S(2)}) collective-permute-start(bf16[8,64,6,128]{3,1,2,0:T(8,128)(2,1)} %all_to_all.31), channel_id=1, source_target_pairs={{0,8},{8,0},{1,9},{9,1},{2,10},{10,2},{3,11},{11,3},{4,12},{12,4},... | collective-permute-start | bytes 2359304 | tf_op jit(solution)/shard_map/ppermute | solution.py:50
  78.2 38.4 %copy-start.1 = (bf16[1,256,16,2,24]{1,4,3,2,0:T(8,128)(2,1)}, bf16[1,256,16,2,24]{1,4,3,2,0:T(8,128)(2,1)S(1)}, u32[]{:S(2)}) copy-start(bf16[1,256,16,2,24]{1,4,3,2,0:T(8,128)(2,1)S(1)} %copy.103) | copy-start | bytes 1179652
  83.9 25.6 %copy-start.10 = (s32[1,128]{1,0:T(1,128)S(1)}, s32[1,128]{1,0:T(1,128)}, u32[]{:S(2)}) copy-start(s32[1,128]{1,0:T(1,128)} %param.14) | copy-start | bytes 1540
  83.9 25.6 %copy-start.9 = (f32[2]{0:T(128)S(1)}, f32[2]{0:T(128)}, u32[]{:S(2)}) copy-start(f32[2]{0:T(128)} %constant.66.clone) | copy-start | bytes 28
  86.4 0.6 copy-start.7
  106.0 10.6 %collective-permute-start.2 = (bf16[768,3072]{1,0:T(8,128)(2,1)}, bf16[768,3072]{1,0:T(8,128)(2,1)S(1)}, u32[]{:S(2)}, u32[]{:S(2)}) collective-permute-start(bf16[768,3072]{1,0:T(8,128)(2,1)} %bitcast.115), channel_id=1, source_target_pairs={{0,8},{8,0},{1,9},{9,1},{2,10},{10,2},{3,11},{11,3},{4,12},{12,4},... | collective-permute-start | bytes 14155784 | tf_op jit(solution)/shard_map/ppermute | solution.py:109
  112.7 4.0 %copy-start.6 = (bf16[1,2,128,3072]{3,2,1,0:T(8,128)(2,1)S(1)}, bf16[1,2,128,3072]{3,2,1,0:T(8,128)(2,1)}, u32[]{:S(2)}) copy-start(bf16[1,2,128,3072]{3,2,1,0:T(8,128)(2,1)} %param.12) | copy-start | bytes 4718596
  116.6 2.1 %copy-start = (f32[256,3072]{1,0:T(8,128)S(1)}, f32[256,3072]{1,0:T(8,128)}, u32[]{:S(2)}) copy-start(f32[256,3072]{1,0:T(8,128)} %fusion.26) | copy-start | bytes 9437188
  122.2 1.4 copy-start.8
  124.3 10.0 %copy-start.2 = (bf16[1,256,16,2,24]{1,4,3,2,0:T(8,128)(2,1)S(1)}, bf16[1,256,16,2,24]{1,4,3,2,0:T(8,128)(2,1)}, u32[]{:S(2)}) copy-start(bf16[1,256,16,2,24]{1,4,3,2,0:T(8,128)(2,1)} %copy-done.1) | copy-start | bytes 1179652
  127.5 11.4 %all-to-all-start.2 = ((f32[16,8,128]{2,1,0:T(8,128)}), f32[16,8,128]{2,1,0:T(8,128)}, u32[]{:S(2)}, u32[]{:S(2)}) async-start(f32[16,8,128]{2,1,0:T(8,128)} %broadcast_in_dim.21), calls=%async_computation.2 | async-start | bytes 131072 | tf_op jit(solution)/shard_map/all_to_all | solution.py:35
  133.7 1.0 copy-start.5
  134.3 8.9 %copy-start.4 = (f32[2,16,48,128]{3,1,2,0:T(8,128)S(1)}, f32[2,16,48,128]{3,1,2,0:T(8,128)}, u32[]{:S(2)}) copy-start(f32[2,16,48,128]{3,1,2,0:T(8,128)} %select_bitcast_fusion) | copy-start | bytes 2359300
  134.8 8.4 %collective-permute-start.3 = (bf16[2,16,72,128]{3,1,2,0:T(8,128)(2,1)S(1)}, bf16[2,16,72,128]{3,1,2,0:T(8,128)(2,1)S(1)}, u32[]{:S(2)}, u32[]{:S(2)}) collective-permute-start(bf16[2,16,72,128]{3,1,2,0:T(8,128)(2,1)S(1)} %pad_maximum_fusion), channel_id=1, source_target_pairs={{0,8},{8,0},{1,9},{9,1},{2,10},{10,2},{3,11},{11,3},{4,12},{12,4},... | collective-permute-start | bytes 1769480 | tf_op jit(solution)/shard_map/ppermute | solution.py:169
  181.3 9.7 %all-to-all-start.5 = ((f32[8,9,128]{2,1,0:T(8,128)}), f32[8,9,128]{2,1,0:T(8,128)S(1)}, u32[]{:S(2)}, u32[]{:S(2)}) async-start(f32[8,9,128]{2,1,0:T(8,128)} %broadcast_in_dim.23), calls=%async_computation.5 | async-start | bytes 131072 | tf_op jit(solution)/shard_map/all_to_all | solution.py:35
Sparse Core Ops, SparseCore 0:
  18.5 87.4 all-gather.1

commit v3 on v2

--- a/solution.py
+++ b/solution.py
@@ -29,6 +29,13 @@
 
 def t_dot(a, b):
     return lax.dot_general(a, b, (((0,), (0,)), ((), ())), preferred_element_type=F32)
+
+
+def in_three(value):
+    first = lax.reduce_precision(value, 8, 7)
+    rest = value - first
+    second = lax.reduce_precision(rest, 8, 7)
+    return jnp.stack([first, second, rest - second]).astype(BF16)
 
 
 def spread(value, axes, size):
@@ -80,20 +87,18 @@
     xh, core = lax.axis_index("xh"), lax.axis_index("c")
     normaliser = float(tokens * seqs * channels)
 
-    pair = lax.ppermute(output_weight, "xh", SWAP)
-    pair = jnp.where(
-        xh == 0, jnp.stack([output_weight, pair]), jnp.stack([pair, output_weight])
-    )
+    pair = jnp.stack([output_weight, lax.ppermute(output_weight, "xh", SWAP)])
     here = lax.all_gather(pair, "z", axis=0).reshape(depth // 2, width)
 
     down_all, up_all, final_all = gather_small(
         adapter_down, adapter_up, latent_weight, zs, seqs, core, lax.axis_index(TOKENS)
     )
     flat_in = attended.reshape(rows, depth)
-    in_cores = flat_in.reshape(rows, 2, zs, 2, own).transpose(3, 0, 2, 1, 4)
-    in_cores = in_cores.reshape(2, rows, depth // 2)
-    in_here = jnp.where(core == 0, in_cores[0], in_cores[1])
-    in_there = jnp.where(core == 0, in_cores[1], in_cores[0])
+    in_cores = flat_in.reshape(rows, 2, zs, 2, own).transpose(3, 1, 0, 2, 4)
+    in_cores = jnp.where(core == 0, in_cores, in_cores[::-1])
+    in_cores = jnp.where(xh == 0, in_cores, in_cores[:, ::-1])
+    in_cores = in_cores.transpose(0, 2, 3, 1, 4).reshape(2, rows, depth // 2)
+    in_here, in_there = in_cores[0], in_cores[1]
     stream = residual.reshape(rows, width).astype(F32)
     shift, scale, gate = modulation[0, 0:1], 1.0 + modulation[0, 1:2], modulation[0, 2:3]
     final32 = final_all.astype(F32)
@@ -101,6 +106,69 @@
     down_projected = dot(flat_in, down_all).astype(BF16)
     adapter_term = ADAPTER_SCALE * dot_t(down_projected, up_all)
 
+    target_rows = targets.reshape(rows, channels).astype(F32)
+    mask_rows = jnp.broadcast_to(repaint_mask.astype(F32)[0], (kinds, tokens)).reshape(rows, 1)
+
+    ready = (in_here, in_there, final_all, up_all, down_projected, adapter_term)
+    ready = ready + (scale, shift, gate, scale_final, shift_final, target_rows, mask_rows)
+    here, ready = lax.optimization_barrier((here, ready))
+    in_here, in_there, final_all, up_all, down_projected, adapter_term = ready[:6]
+    scale, shift, gate, scale_final, shift_final, target_rows, mask_rows = ready[6:]
+    there = lax.ppermute(here, "c", SWAP)
+    both = jnp.where(core == 0, jnp.stack([here, there]), jnp.stack([there, here]))
+    both = both.reshape(2 * seqs, 4 * zs, piece, rank).transpose(1, 0, 2, 3)
+    both = both.reshape(4 * zs, 4 * own, rank)
+    down = both[:, :own].reshape(-1, rank)
+    up = both[:, own : 3 * own].reshape(-1, rank)
+    last = both[:, 3 * own :].reshape(4 * zs, own, 2, channels).transpose(0, 2, 1, 3)
+    return down, up, last.reshape(-1, channels)
+
+
+def local(
+    attended,
+    residual,
+    targets,
+    repaint_mask,
+    timesteps,
+    modulation,
+    output_weight,
+    adapter_down,
+    adapter_up,
+    latent_weight,
+):
+    _, kinds, tokens, depth = attended.shape
+    width = residual.shape[-1]
+    channels = targets.shape[-1]
+    rank = adapter_down.shape[1]
+    rows = kinds * tokens
+    own = output_weight.shape[0]
+    zs, ys = lax.axis_size("z"), lax.axis_size("y")
+    seqs = 2 * ys
+    xh, core = lax.axis_index("xh"), lax.axis_index("c")
+    normaliser = float(tokens * seqs * channels)
+
+    pair = jnp.stack([output_weight, lax.ppermute(output_weight, "xh", SWAP)])
+    here = lax.all_gather(pair, "z", axis=0).reshape(depth // 2, width)
+
+    down_all, up_all, final_all = gather_small(
+        adapter_down, adapter_up, latent_weight, zs, seqs, core, lax.axis_index(TOKENS)
+    )
+    flat_in = attended.reshape(rows, depth)
+    in_cores = flat_in.reshape(rows, 2, zs, 2, own).transpose(3, 1, 0, 2, 4)
+    in_cores = jnp.where(core == 0, in_cores, in_cores[::-1])
+    in_cores = jnp.where(xh == 0, in_cores, in_cores[:, ::-1])
+    in_cores = in_cores.transpose(0, 2, 3, 1, 4).reshape(2, rows, depth // 2)
+    in_here, in_there = in_cores[0], in_cores[1]
+    stream = residual.reshape(rows, width).astype(F32)
+    shift, scale, gate = modulation[0, 0:1], 1.0 + modulation[0, 1:2], modulation[0, 2:3]
+    final32 = final_all.astype(F32)
+    scale_final, shift_final = exact_dot(scale, final32), exact_dot(shift, final32)
+    down_projected = dot(flat_in, down_all).astype(BF16)
+    adapter_term = ADAPTER_SCALE * dot_t(down_projected, up_all)
+
+    target_rows = targets.reshape(rows, channels).astype(F32)
+    mask_rows = jnp.broadcast_to(repaint_mask.astype(F32)[0], (kinds, tokens)).reshape(rows, 1)
+
     here, in_here, in_there, final_all, up_all, down_projected, adapter_term = (
         lax.optimization_barrier(
             (here, in_here, in_there, final_all, up_all, down_projected, adapter_term)
@@ -120,10 +188,8 @@
 
     pred_pol, normed, inverse = head_out(hidden_pol)
     pred_ref, _, _ = head_out(hidden_ref)
-    target_rows = targets.reshape(rows, channels).astype(F32)
     miss_pol = pred_pol - target_rows
     miss_ref = pred_ref - target_rows
-    mask_rows = jnp.broadcast_to(repaint_mask.astype(F32)[0], (kinds, tokens)).reshape(rows, 1)
 
     def by_kind(value):
         return jnp.sum(value.reshape(kinds, -1), axis=1)
@@ -133,17 +199,6 @@
     )
     weight_t = (2.0 - timesteps.astype(F32) / 1000.0) / seqs
     errors = jnp.concatenate([errors / normaliser, weight_t])
-    errors = jnp.pad(errors[None, :], ((0, 7), (0, 127 - 2 * kinds)))
-    errors, miss_pol = lax.optimization_barrier((errors, miss_pol))
-    errors = spread(errors, ("c",) + TOKENS, 2 * seqs)[:, 0]
-    errors = jnp.sum(errors.reshape(2, seqs, 128), axis=1)
-    delta = errors[:, 0] - errors[:, 2] - (errors[:, 1] - errors[:, 3])
-    weight_t = errors[:, 4]
-    logits = -DPO_BETA * weight_t * delta
-    pair_loss = lax.dynamic_slice_in_dim(jax.nn.softplus(-logits), core, 1)
-    slope = jax.nn.sigmoid(-logits) * DPO_BETA * weight_t / normaliser
-    slope_here = jnp.where(core == 0, slope[0], slope[1])
-    slope_there = jnp.where(core == 0, slope[1], slope[0])
 
     signs = jnp.repeat(jnp.array([2.0, -2.0], F32), tokens)[:, None]
     grad_pred = (signs * mask_rows * miss_pol).astype(BF16)
@@ -154,26 +209,33 @@
     update = (gate * (inverse * (grad_norm - first - normed * second))).astype(BF16)
     up_gradient = ADAPTER_SCALE * t_dot(update, down_projected)
     grad_low = (ADAPTER_SCALE * dot(update, up_all)).astype(BF16)
-    down_here = t_dot(in_here, grad_low)
-    down_there = t_dot(in_there, grad_low)
-
-    up_gradient = up_gradient.reshape(2, zs, 2, 2 * own, rank)
-    up_here = jnp.where(core == 0, up_gradient[:, :, 0], up_gradient[:, :, 1])
-    up_there = jnp.where(core == 0, up_gradient[:, :, 1], up_gradient[:, :, 0])
-
-    def by_owner(down, up):
-        down = down.reshape(zs, 2, own, rank).transpose(1, 0, 2, 3)
-        return jnp.concatenate([down, up], axis=2)
-
-    grads = by_owner(down_there, up_there).astype(BF16)
-    grads = lax.ppermute(grads, "c", SWAP).astype(F32)
-    grads = slope_here * by_owner(down_here, up_here) + slope_there * grads
+    down_gradient = jnp.stack([t_dot(in_here, grad_low), t_dot(in_there, grad_low)])
+
+    down_gradient = down_gradient.reshape(2, zs, 2, own, rank)
+    down_gradient = jnp.where(core == 0, down_gradient, down_gradient[::-1])
+    down_gradient = jnp.where(xh == 0, down_gradient, down_gradient[:, :, ::-1])
+    down_gradient = down_gradient.transpose(2, 0, 1, 3, 4)
+    up_gradient = up_gradient.reshape(2, zs, 2, 2 * own, rank).transpose(0, 2, 1, 3, 4)
     piece = 3 * own // seqs
-    grads = grads.astype(BF16).reshape(2, zs, seqs, piece, rank).transpose(0, 2, 1, 3, 4)
-    grads = lax.all_to_all(grads.reshape(2 * seqs, zs, piece, rank), ("xh",) + TOKENS, 0, 0)
-    grads = jnp.sum(grads.astype(F32), axis=0).astype(BF16)
-    grads = jnp.sum(lax.all_to_all(grads, "z", 0, 0).astype(F32), axis=0)
-    grads = spread(grads, TOKENS, seqs).reshape(3 * own, rank)
+    grads = jnp.concatenate([down_gradient, up_gradient], axis=3)
+    grads = grads.reshape(2, 2, zs, seqs, piece, rank).transpose(0, 1, 3, 2, 4, 5)
+    grads = grads.reshape(4 * seqs, zs * piece, rank).astype(BF16)
+    errors = jnp.pad(in_three(errors), ((0, 13), (0, rank - errors.shape[0])))
+    errors = jnp.broadcast_to(errors[None], (4 * seqs,) + errors.shape)
+    grads = jnp.concatenate([grads, errors], axis=1)
+    grads = lax.all_to_all(grads, ("xh", "c") + TOKENS, 0, 0)
+    errors = jnp.sum(grads[:, zs * piece : zs * piece + 3].astype(F32), axis=1)
+    errors = jnp.sum(errors.reshape(4, seqs, rank), axis=1)
+    delta = errors[:, 0:1] - errors[:, 2:3] - (errors[:, 1:2] - errors[:, 3:4])
+    weight_t = errors[:, 4:5]
+    logits = -DPO_BETA * weight_t * delta
+    mine = jnp.arange(4)[:, None] == 2 * xh + core
+    pair_loss = jnp.sum(jnp.where(mine, jax.nn.softplus(-logits), 0.0), axis=0)
+    slope = jax.nn.sigmoid(-logits) * DPO_BETA * weight_t / normaliser
+    grads = grads[:, : zs * piece].astype(F32).reshape(4, seqs, zs * piece, rank)
+    grads = jnp.sum(slope[:, :, None, None] * grads, axis=(0, 1))
+    grads = lax.all_to_all(grads.reshape(zs, piece, rank), "z", 0, 0)
+    grads = spread(jnp.sum(grads, axis=0), TOKENS, seqs).reshape(3 * own, rank)
     return (pair_loss, grads[:own], grads[own:])
 
 

time: 200 us -> 196 us (0.980)
  the two profiles are of different devices: /device:TPU:2 before, /device:TPU:4 now
where the time goes in v3:
time: 196 us; the launch traced here: 195 us
  blocking collectives  81.8 us (42%)
  waiting for transfers between devices  40.3 us (21%)
  starting transfers between devices  19.6 us (10%)
  matrix products  15.5 us (8%)
  between operations  15.1 us (8%)
  local copies, waits for them, and re-layouts  13.9 us (7%)
  other arithmetic  8.51 us (4%)
    all_to_all x1, blocking collectives, gather_small(): packed = lax.all_to_all(packed.reshape((4 * zs, piece, rank)), OWNERS, 0, 0)  33.4 us
    all_to_all x2, blocking collectives, spread(): lax.all_to_all(jnp.broadcast_to(value[None], (size,) + value.shape), axes...  28 us
    all_to_all x1, blocking collectives, local(): grads = lax.all_to_all(grads.reshape(zs, piece, rank), 'z', 0, 0)  20.4 us
    all_to_all x1, waiting for transfers between devices, local(): grads = lax.all_to_all(grads, ('xh', 'c') + TOKENS, 0, 0)  18.4 us
    all_gather x1, waiting for transfers between devices, local(): here = lax.all_gather(pair, 'z', axis=0).reshape(depth // 2, width)  17.9 us
    dot_general x6, matrix products, dot(): return jnp.dot(a, b, preferred_element_type=F32)  8.54 us
    ppermute x1, starting transfers between devices, local(): pair = jnp.stack([output_weight, lax.ppermute(output_weight, 'xh', SWAP)])  7.92 us
    all_to_all x1, starting transfers between devices, local(): grads = lax.all_to_all(grads, ('xh', 'c') + TOKENS, 0, 0)  7.68 us
  transfers between devices with their start and end apart: 5, of which 4 were waited for; matrix products, arithmetic and copies ran while one was open for 11% of the time, Pallas kernels for 0%

profile of v3, /device:TPU:4, one launch (start us, length us, event | category | flops | bytes accessed | tf_op | source)
XLA Modules:
  0.0 194.8 jit_solution(15752785354835827010)
XLA Ops:
  7.2 7.9 %collective-permute-start = (bf16[24,3072]{1,0:T(8,128)(2,1)}, bf16[24,3072]{1,0:T(8,128)(2,1)S(1)}, u32[]{:S(2)}, u32[]{:S(2)}) collective-permute-start(bf16[24,3072]{1,0:T(8,128)(2,1)} %param.17), channel_id=1, source_target_pairs={{0,256},{256,0},{1,257},{257,1},{2,258},{258,2},{3,259},{259,3},{4... | collective-permute-start | bytes 442376 | tf_op jit(solution)/shard_map/ppermute | solution.py:150
  15.1 3.3 %collective-permute-done = bf16[24,3072]{1,0:T(8,128)(2,1)S(1)} collective-permute-done((bf16[24,3072]{1,0:T(8,128)(2,1)}, bf16[24,3072]{1,0:T(8,128)(2,1)S(1)}, u32[]{:S(2)}, u32[]{:S(2)}) %collective-permute-start) | collective-permute-done | bytes 147488 | tf_op jit(solution)/shard_map/ppermute | solution.py:150
  18.5 1.6 pad_maximum_fusion.2
  21.7 33.4 %all_to_all.25 = bf16[64,6,128]{2,1,0:T(8,128)(2,1)S(1)} all-to-all(bf16[64,6,128]{2,1,0:T(8,128)(2,1)S(1)} %bitcast.138), channel_id=1, replica_groups=mesh['xh'=2,'z'=16,'c'=2,'xl'=2,'y'=4] {'xh','z','c'}, dimensions={0} | all-to-all | bytes 196608 | tf_op jit(solution)/shard_map/all_to_all | solution.py:55
  55.3 18.0 %all_to_all.26 = bf16[8,64,6,128]{3,1,2,0:T(8,128)(2,1)S(1)} all-to-all(bf16[8,64,6,128]{3,1,2,0:T(8,128)(2,1)S(1)} %broadcast_in_dim.17), channel_id=1, replica_groups=mesh['xh'=2,'z'=16,'c'=2,'xl'=2,'y'=4] {'xl','y'}, dimensions={0} | all-to-all | bytes 1572864 | tf_op jit(solution)/shard_map/all_to_all | solution.py:42
  73.3 1.9 collective-permute-start.1
  77.6 1.6 maximum_select_fusion
  80.9 2.8 %reshape.266 = bf16[64,24,2,64]{3,2,0,1:T(2,128)(2,1)} reshape(bf16[64,24,128]{2,0,1:T(8,128)(2,1)} %get-tuple-element.29) | data formatting | bytes 786432 | tf_op jit(solution)/shard_map/reshape | solution.py:63
  83.8 2.1 %copy.73 = bf16[64,24,2,64]{3,1,2,0:T(8,128)(2,1)S(1)} copy(bf16[64,24,2,64]{3,2,0,1:T(2,128)(2,1)} %reshape.266) | data formatting | bytes 786432 | tf_op jit(solution)/shard_map/reshape | solution.py:63
  86.9 2.3 %fusion.38 = f32[256,3072]{1,0:T(8,128)} fusion(bf16[128,256]{1,0:T(8,128)(2,1)S(1)} %convolution_convert_fusion.1, bf16[3072,128]{1,0:T(8,128)(2,1)S(1)} %bitcast.116), kind=kOutput, calls=%fused_computation.96 | convolution fusion | flops 201326592 | bytes 3997696 | tf_op jit(solution)/shard_map/dot_general | solution.py:27
  89.1 17.9 %all-gather.3.cloned.1.call-done = bf16[32,24,3072]{2,1,0:T(8,128)(2,1)} async-done(((bf16[2,24,3072]{2,1,0:T(8,128)(2,1)}), bf16[32,24,3072]{2,1,0:T(8,128)(2,1)}) %all-gather.3.cloned.1.call-update) | async-done | bytes 4718608 | tf_op jit(solution)/shard_map/all_gather | solution.py:151
  107.0 2.1 %collective-permute-start.2 = (bf16[768,3072]{1,0:T(8,128)(2,1)}, bf16[768,3072]{1,0:T(8,128)(2,1)S(1)}, u32[]{:S(2)}, u32[]{:S(2)}) collective-permute-start(bf16[768,3072]{1,0:T(8,128)(2,1)} %bitcast.114), channel_id=1, source_target_pairs={{0,8},{8,0},{1,9},{9,1},{2,10},{10,2},{3,11},{11,3},{4,12},{12,4},... | collective-permute-start | bytes 14155784 | tf_op jit(solution)/shard_map/ppermute | solution.py:177
  111.4 1.1 convolution_bitcast_fusion
  112.6 1.1 convolution_bitcast_fusion.1
  113.7 3.9 %fusion.39 = f32[256,3072]{1,0:T(8,128)S(1)} fusion(bf16[256,768]{0,1:T(8,128)(2,1)S(1)} %bitcast.120, bf16[768,3072]{1,0:T(8,128)(2,1)} %bitcast.115), kind=kOutput, calls=%fused_computation.97 | convolution fusion | flops 1207959552 | bytes 8257536 | tf_op jit(solution)/shard_map/dot_general | solution.py:23
  117.6 2.0 %fusion.37 = (f32[256]{0:T(256)S(1)}, f32[256,3072]{1,0:T(8,128)S(1)}) fusion(f32[256,3072]{1,0:T(8,128)S(1)} %fusion.39, bf16[256,768]{0,1:T(8,128)(2,1)S(1)} %bitcast.124, bf16[768,3072]{1,0:T(8,128)(2,1)S(1)} %collective-permute-done.2, f32[3072]{0:T(1024)S(1)} %bitcast.141, bf16[256,3072]{1,0:T(8,128)(2,1)S(1)} %bitcast.132), kind=kOutput, calls=%fused_computation.95 | convolution fusion | flops 1211891456 | bytes 12989440 | tf_op jit(solution)/shard_map/dot_general | solution.py:23
  119.6 0.8 fusion.33
  121.8 1.3 fusion.6
  126.1 0.8 fusion.13
  127.4 1.6 copy.81
  128.9 7.7 %all-to-all-start.2 = ((bf16[32,160,128]{2,1,0:T(8,128)(2,1)}), bf16[32,160,128]{2,1,0:T(8,128)(2,1)S(1)}, u32[]{:S(2)}, u32[]{:S(2)}) async-start(bf16[32,160,128]{2,1,0:T(8,128)(2,1)} %copy.81), calls=%async_computation.2 | async-start | bytes 2621440 | tf_op jit(solution)/shard_map/all_to_all | solution.py:226
  136.6 18.4 %all-to-all-done.2 = bf16[32,160,128]{2,1,0:T(8,128)(2,1)S(1)} async-done(((bf16[32,160,128]{2,1,0:T(8,128)(2,1)}), bf16[32,160,128]{2,1,0:T(8,128)(2,1)S(1)}, u32[]{:S(2)}, u32[]{:S(2)}) %all-to-all-start.2) | async-done | bytes 1310752 | tf_op jit(solution)/shard_map/all_to_all | solution.py:226
  156.3 20.4 %all_to_all.27 = f32[16,9,128]{2,1,0:T(8,128)S(1)} all-to-all(f32[16,9,128]{2,1,0:T(8,128)S(1)} %reshape.274), channel_id=1, replica_groups=mesh['xh'=2,'z'=16,'c'=2,'xl'=2,'y'=4] {'z'}, dimensions={0} | all-to-all | bytes 147456 | tf_op jit(solution)/shard_map/all_to_all | solution.py:237
  176.7 10.0 %all_to_all.28 = f32[8,9,128]{2,1,0:T(8,128)S(1)} all-to-all(f32[8,9,128]{2,1,0:T(8,128)S(1)} %broadcast_in_dim.21), channel_id=1, replica_groups=mesh['xh'=2,'z'=16,'c'=2,'xl'=2,'y'=4] {'xl','y'}, dimensions={0} | all-to-all | bytes 73728 | tf_op jit(solution)/shard_map/all_to_all | solution.py:42
  (80 shorter events, 15.5 us)
Async XLA Ops:
  7.2 68.0 %copy-start.1 = (bf16[1,2,128,1536]{3,2,1,0:T(8,128)(2,1)S(1)}, bf16[1,2,128,1536]{3,2,1,0:T(8,128)(2,1)}, u32[]{:S(2)}) copy-start(bf16[1,2,128,1536]{3,2,1,0:T(8,128)(2,1)} %param.11) | copy-start | bytes 2359300
  7.2 99.8 %all-gather.3.cloned.1.call-start = ((), (), s32[]{:S(2)}) async-start(), calls=%async_computation.5 | async-start | bytes 5013504 | tf_op jit(solution)/shard_map/all_gather | solution.py:151
  7.2 11.2 %collective-permute-start = (bf16[24,3072]{1,0:T(8,128)(2,1)}, bf16[24,3072]{1,0:T(8,128)(2,1)S(1)}, u32[]{:S(2)}, u32[]{:S(2)}) collective-permute-start(bf16[24,3072]{1,0:T(8,128)(2,1)} %param.17), channel_id=1, source_target_pairs={{0,256},{256,0},{1,257},{257,1},{2,258},{258,2},{3,259},{259,3},{4... | collective-permute-start | bytes 442376 | tf_op jit(solution)/shard_map/ppermute | solution.py:150
  73.3 4.3 %collective-permute-start.1 = (bf16[8,64,6,128]{3,1,2,0:T(8,128)(2,1)S(1)}, bf16[8,64,6,128]{3,1,2,0:T(8,128)(2,1)}, u32[]{:S(2)}, u32[]{:S(2)}) collective-permute-start(bf16[8,64,6,128]{3,1,2,0:T(8,128)(2,1)S(1)} %all_to_all.26), channel_id=1, source_target_pairs={{0,8},{8,0},{1,9},{9,1},{2,10},{10,2},{3,11},{11,3},{4,12},{12,4},... | collective-permute-start | bytes 2359304 | tf_op jit(solution)/shard_map/ppermute | solution.py:57
  83.7 26.8 %copy-start.6 = (s32[1,128]{1,0:T(1,128)S(1)}, s32[1,128]{1,0:T(1,128)}, u32[]{:S(2)}) copy-start(s32[1,128]{1,0:T(1,128)} %param.14) | copy-start | bytes 1540
  83.7 26.8 %copy-start.5 = (f32[2]{0:T(128)S(1)}, f32[2]{0:T(128)}, u32[]{:S(2)}) copy-start(f32[2]{0:T(128)} %constant.65.clone) | copy-start | bytes 28
  86.2 0.6 copy-start.3
  107.0 10.6 %collective-permute-start.2 = (bf16[768,3072]{1,0:T(8,128)(2,1)}, bf16[768,3072]{1,0:T(8,128)(2,1)S(1)}, u32[]{:S(2)}, u32[]{:S(2)}) collective-permute-start(bf16[768,3072]{1,0:T(8,128)(2,1)} %bitcast.114), channel_id=1, source_target_pairs={{0,8},{8,0},{1,9},{9,1},{2,10},{10,2},{3,11},{11,3},{4,12},{12,4},... | collective-permute-start | bytes 14155784 | tf_op jit(solution)/shard_map/ppermute | solution.py:177
  113.7 3.9 %copy-start.2 = (bf16[1,2,128,3072]{3,2,1,0:T(8,128)(2,1)S(1)}, bf16[1,2,128,3072]{3,2,1,0:T(8,128)(2,1)}, u32[]{:S(2)}) copy-start(bf16[1,2,128,3072]{3,2,1,0:T(8,128)(2,1)} %param.12) | copy-start | bytes 4718596
  117.6 2.0 %copy-start = (f32[256,3072]{1,0:T(8,128)S(1)}, f32[256,3072]{1,0:T(8,128)}, u32[]{:S(2)}) copy-start(f32[256,3072]{1,0:T(8,128)} %fusion.38) | copy-start | bytes 9437188
  123.1 1.4 copy-start.4
  128.9 26.1 %all-to-all-start.2 = ((bf16[32,160,128]{2,1,0:T(8,128)(2,1)}), bf16[32,160,128]{2,1,0:T(8,128)(2,1)S(1)}, u32[]{:S(2)}, u32[]{:S(2)}) async-start(bf16[32,160,128]{2,1,0:T(8,128)(2,1)} %copy.81), calls=%async_computation.2 | async-start | bytes 2621440 | tf_op jit(solution)/shard_map/all_to_all | solution.py:226
Sparse Core Ops, SparseCore 0:
  20.3 86.7 all-gather.2

commit v4 on v3

--- a/solution.py
+++ b/solution.py
@@ -42,22 +42,21 @@
     return lax.all_to_all(jnp.broadcast_to(value[None], (size,) + value.shape), axes, 0, 0)
 
 
-def gather_small(down, up, last, zs, seqs, core, seq):
+def gather_small(down, up, last, zs, seqs, xh, core, seq):
     own, rank = down.shape
     channels = last.shape[1]
     packed = jnp.concatenate(
         [down, up, jnp.concatenate([last[:own], last[own:]], axis=1)], axis=0
     )
-    piece = 4 * own // (2 * seqs)
-    packed = packed.reshape(2, seqs, piece, rank)
-    packed = lax.dynamic_index_in_dim(packed, seq, 1, keepdims=False)
-    packed = jnp.broadcast_to(packed[None], (2 * zs,) + packed.shape)
-    packed = lax.all_to_all(packed.reshape((4 * zs, piece, rank)), OWNERS, 0, 0)
+    piece = 4 * own // seqs
+    packed = lax.dynamic_index_in_dim(packed.reshape(seqs, piece, rank), seq, 0, keepdims=False)
+    packed = jnp.stack([packed, lax.ppermute(packed, "xh", SWAP)])
+    packed = lax.all_gather(packed, "z", axis=0)
     here = spread(packed, TOKENS, seqs)
     there = lax.ppermute(here, "c", SWAP)
     both = jnp.where(core == 0, jnp.stack([here, there]), jnp.stack([there, here]))
-    both = both.reshape(2 * seqs, 4 * zs, piece, rank).transpose(1, 0, 2, 3)
-    both = both.reshape(4 * zs, 4 * own, rank)
+    both = jnp.where(xh == 0, both, both[:, :, :, ::-1])
+    both = both.transpose(3, 2, 0, 1, 4, 5).reshape(4 * zs, 4 * own, rank)
     down = both[:, :own].reshape(-1, rank)
     up = both[:, own : 3 * own].reshape(-1, rank)
     last = both[:, 3 * own :].reshape(4 * zs, own, 2, channels).transpose(0, 2, 1, 3)
@@ -91,7 +90,7 @@
     here = lax.all_gather(pair, "z", axis=0).reshape(depth // 2, width)
 
     down_all, up_all, final_all = gather_small(
-        adapter_down, adapter_up, latent_weight, zs, seqs, core, lax.axis_index(TOKENS)
+        adapter_down, adapter_up, latent_weight, zs, seqs, xh, core, lax.axis_index(TOKENS)
     )
     flat_in = attended.reshape(rows, depth)
     in_cores = flat_in.reshape(rows, 2, zs, 2, own).transpose(3, 1, 0, 2, 4)
@@ -151,7 +150,7 @@
     here = lax.all_gather(pair, "z", axis=0).reshape(depth // 2, width)
 
     down_all, up_all, final_all = gather_small(
-        adapter_down, adapter_up, latent_weight, zs, seqs, core, lax.axis_index(TOKENS)
+        adapter_down, adapter_up, latent_weight, zs, seqs, xh, core, lax.axis_index(TOKENS)
     )
     flat_in = attended.reshape(rows, depth)
     in_cores = flat_in.reshape(rows, 2, zs, 2, own).transpose(3, 1, 0, 2, 4)
@@ -218,13 +217,13 @@
     up_gradient = up_gradient.reshape(2, zs, 2, 2 * own, rank).transpose(0, 2, 1, 3, 4)
     piece = 3 * own // seqs
     grads = jnp.concatenate([down_gradient, up_gradient], axis=3)
-    grads = grads.reshape(2, 2, zs, seqs, piece, rank).transpose(0, 1, 3, 2, 4, 5)
-    grads = grads.reshape(4 * seqs, zs * piece, rank).astype(BF16)
-    errors = jnp.pad(in_three(errors), ((0, 13), (0, rank - errors.shape[0])))
-    errors = jnp.broadcast_to(errors[None], (4 * seqs,) + errors.shape)
+    grads = grads.reshape(2, 2, zs, seqs, piece, rank).transpose(0, 1, 3, 4, 2, 5)
+    grads = grads.reshape(4 * seqs, piece, zs, rank).astype(BF16)
+    errors = jnp.pad(in_three(errors), ((0, zs - 3), (0, rank - errors.shape[0])))
+    errors = jnp.broadcast_to(errors[None, None], (4 * seqs, 1) + errors.shape)
     grads = jnp.concatenate([grads, errors], axis=1)
     grads = lax.all_to_all(grads, ("xh", "c") + TOKENS, 0, 0)
-    errors = jnp.sum(grads[:, zs * piece : zs * piece + 3].astype(F32), axis=1)
+    errors = jnp.sum(grads[:, piece, :3].astype(F32), axis=1)
     errors = jnp.sum(errors.reshape(4, seqs, rank), axis=1)
     delta = errors[:, 0:1] - errors[:, 2:3] - (errors[:, 1:2] - errors[:, 3:4])
     weight_t = errors[:, 4:5]
@@ -232,9 +231,9 @@
     mine = jnp.arange(4)[:, None] == 2 * xh + core
     pair_loss = jnp.sum(jnp.where(mine, jax.nn.softplus(-logits), 0.0), axis=0)
     slope = jax.nn.sigmoid(-logits) * DPO_BETA * weight_t / normaliser
-    grads = grads[:, : zs * piece].astype(F32).reshape(4, seqs, zs * piece, rank)
-    grads = jnp.sum(slope[:, :, None, None] * grads, axis=(0, 1))
-    grads = lax.all_to_all(grads.reshape(zs, piece, rank), "z", 0, 0)
+    grads = grads[:, :piece].astype(F32).reshape(4, seqs, piece, zs, rank)
+    grads = jnp.sum(slope[:, :, None, None, None] * grads, axis=(0, 1))
+    grads = lax.all_to_all(grads.transpose(1, 0, 2), "z", 0, 0)
     grads = spread(jnp.sum(grads, axis=0), TOKENS, seqs).reshape(3 * own, rank)
     return (pair_loss, grads[:own], grads[own:])
 

time: 196 us -> 191 us (0.974)
  waiting for transfers between devices: 40.3 us -> 29.9 us
  starting transfers between devices: 19.6 us -> 24.9 us
    all_gather x0 -> x1, blocking collectives: none -> 34.4 us  [gather_small(): packed = lax.all_gather(packed, 'z', axis=0)]
    all_to_all x2 -> x1, blocking collectives: 53.8 us -> 20.7 us  [local(): grads = lax.all_to_all(grads.transpose(1, 0, 2), 'z', 0, 0)]
    all_gather x1, waiting for transfers between devices: 17.9 us -> 5.98 us  [local(): here = lax.all_gather(pair, 'z', axis=0).reshape(depth // 2, width)]
    ppermute x0 -> x1, starting transfers between devices: none -> 5.43 us  [gather_small(): packed = jnp.stack([packed, lax.ppermute(packed, 'xh', SWAP)])]
    all_to_all x2, blocking collectives: 28 us -> 24.9 us  [spread(): lax.all_to_all(jnp.broadcast_to(value[None], (size,) + value.shape), axes...]
    transpose x0 -> x2, local copies, waits for them, and re-layouts: none -> 2.47 us  [the longest x1 2.44 us: gather_small(): both = both.transpose(3, 2, 0, 1, 4, 5).reshape(4 * zs, 4 * own, rank)]
  transfers between devices with their start and end apart: 5 -> 6, of which waited for: 4 -> 5; matrix products, arithmetic and copies ran while one was open for 11% -> 13% of each run, Pallas kernels for 0% -> 0%
where the time goes in v4:
time: 191 us; the launch traced here: 190 us
  blocking collectives  80 us (42%)
  waiting for transfers between devices  29.9 us (16%)
  starting transfers between devices  24.9 us (13%)
  matrix products  15.5 us (8%)
  between operations  15.1 us (8%)
  local copies, waits for them, and re-layouts  14.4 us (8%)
  other arithmetic  10 us (5%)
    all_gather x1, blocking collectives, gather_small(): packed = lax.all_gather(packed, 'z', axis=0)  34.4 us
    all_to_all x2, blocking collectives, spread(): lax.all_to_all(jnp.broadcast_to(value[None], (size,) + value.shape), axes...  24.9 us
    all_to_all x1, blocking collectives, local(): grads = lax.all_to_all(grads.transpose(1, 0, 2), 'z', 0, 0)  20.7 us
    all_to_all x1, waiting for transfers between devices, local(): grads = lax.all_to_all(grads, ('xh', 'c') + TOKENS, 0, 0)  18.4 us
    dot_general x6, matrix products, dot(): return jnp.dot(a, b, preferred_element_type=F32)  8.54 us
    ppermute x1, starting transfers between devices, local(): pair = jnp.stack([output_weight, lax.ppermute(output_weight, 'xh', SWAP)])  7.92 us
    all_to_all x1, starting transfers between devices, local(): grads = lax.all_to_all(grads, ('xh', 'c') + TOKENS, 0, 0)  7.55 us
    all_gather x1, waiting for transfers between devices, local(): here = lax.all_gather(pair, 'z', axis=0).reshape(depth // 2, width)  5.98 us
  transfers between devices with their start and end apart: 6, of which 5 were waited for; matrix products, arithmetic and copies ran while one was open for 13% of the time, Pallas kernels for 0%

profile of v4, /device:TPU:4, one launch (start us, length us, event | category | flops | bytes accessed | tf_op | source)
XLA Modules:
  0.0 189.9 jit_solution(10263154718456159561)
XLA Ops:
  7.2 7.9 %collective-permute-start = (bf16[24,3072]{1,0:T(8,128)(2,1)}, bf16[24,3072]{1,0:T(8,128)(2,1)S(1)}, u32[]{:S(2)}, u32[]{:S(2)}) collective-permute-start(bf16[24,3072]{1,0:T(8,128)(2,1)} %param.17), channel_id=1, source_target_pairs={{0,256},{256,0},{1,257},{257,1},{2,258},{258,2},{3,259},{259,3},{4... | collective-permute-start | bytes 442376 | tf_op jit(solution)/shard_map/ppermute | solution.py:149
  15.1 3.3 %collective-permute-done = bf16[24,3072]{1,0:T(8,128)(2,1)S(1)} collective-permute-done((bf16[24,3072]{1,0:T(8,128)(2,1)}, bf16[24,3072]{1,0:T(8,128)(2,1)S(1)}, u32[]{:S(2)}, u32[]{:S(2)}) %collective-permute-start) | collective-permute-done | bytes 147488 | tf_op jit(solution)/shard_map/ppermute | solution.py:149
  18.5 1.6 pad_maximum_fusion.2
  21.7 5.4 %collective-permute-start.1 = (bf16[12,128]{1,0:T(8,128)(2,1)S(1)}, bf16[12,128]{1,0:T(8,128)(2,1)S(1)}, u32[]{:S(2)}, u32[]{:S(2)}) collective-permute-start(bf16[12,128]{1,0:T(8,128)(2,1)S(1)} %fusion.65), channel_id=1, source_target_pairs={{0,256},{256,0},{1,257},{257,1},{2,258},{258,2},{3,259},{259,3},{4... | collective-permute-start | bytes 9224 | tf_op jit(solution)/shard_map/ppermute | solution.py:53
  27.1 1.6 collective-permute-done.1
  28.7 34.4 %all-gather.1 = bf16[32,12,128]{2,1,0:T(8,128)(2,1)S(1)} all-gather(bf16[2,12,128]{2,1,0:T(8,128)(2,1)S(1)} %pad_maximum_fusion.3), channel_id=3, replica_groups=mesh['xh'=2,'z'=16,'c'=2,'xl'=2,'y'=4] {'z'}, dimensions={0}, use_global_device_ids=true | all-gather | bytes 104448 | tf_op jit(solution)/shard_map/all_gather | solution.py:54
  63.3 14.9 %all_to_all.20 = bf16[8,16,2,12,128]{4,1,3,2,0:T(8,128)(2,1)S(1)} all-to-all(bf16[8,16,2,12,128]{4,1,3,2,0:T(8,128)(2,1)S(1)} %broadcast_in_dim.11), channel_id=1, replica_groups=mesh['xh'=2,'z'=16,'c'=2,'xl'=2,'y'=4] {'xl','y'}, dimensions={0} | all-to-all | bytes 1572864 | tf_op jit(solution)/shard_map/all_to_all | solution.py:42
  78.1 1.9 %collective-permute-start.2 = (bf16[8,16,2,12,128]{4,1,3,2,0:T(8,128)(2,1)S(1)}, bf16[8,16,2,12,128]{4,1,3,2,0:T(8,128)(2,1)}, u32[]{:S(2)}, u32[]{:S(2)}) collective-permute-start(bf16[8,16,2,12,128]{4,1,3,2,0:T(8,128)(2,1)S(1)} %all_to_all.20), channel_id=1, source_target_pairs={{0,8},{8,0},{1,9},{9,1},{2,10},{10,2},{3,11},{11,3},{4,12},{12,4},... | collective-permute-start | bytes 2359304 | tf_op jit(solution)/shard_map/ppermute | solution.py:56
  82.4 1.6 maximum_select_fusion
  84.6 2.4 %copy.79 = bf16[2,16,2,8,12,128]{5,2,1,0,4,3:T(2,128)(2,1)S(1)} copy(bf16[2,16,2,8,12,128]{5,1,4,0,3,2:T(8,128)(2,1)S(1)} %fusion.7) | data formatting | bytes 3145728 | tf_op jit(solution)/shard_map/transpose | solution.py:59
  88.7 2.8 %reshape.255 = bf16[64,24,2,64]{3,2,0,1:T(2,128)(2,1)} reshape(bf16[64,24,128]{2,0,1:T(8,128)(2,1)} %get-tuple-element.29) | data formatting | bytes 786432 | tf_op jit(solution)/shard_map/reshape | solution.py:62
  91.5 2.1 %copy.80 = bf16[64,24,2,64]{3,1,2,0:T(8,128)(2,1)S(1)} copy(bf16[64,24,2,64]{3,2,0,1:T(2,128)(2,1)} %reshape.255) | data formatting | bytes 786432 | tf_op jit(solution)/shard_map/reshape | solution.py:62
  94.6 2.3 %fusion.39 = f32[256,3072]{1,0:T(8,128)} fusion(bf16[128,256]{1,0:T(8,128)(2,1)S(1)} %convolution_convert_fusion.1, bf16[3072,128]{1,0:T(8,128)(2,1)S(1)} %bitcast.117), kind=kOutput, calls=%fused_computation.99 | convolution fusion | flops 201326592 | bytes 3997696 | tf_op jit(solution)/shard_map/dot_general | solution.py:27
  96.9 6.0 %all-gather.4.cloned.1.call-done = bf16[32,24,3072]{2,1,0:T(8,128)(2,1)} async-done(((bf16[2,24,3072]{2,1,0:T(8,128)(2,1)}), bf16[32,24,3072]{2,1,0:T(8,128)(2,1)}) %all-gather.4.cloned.1.call-update) | async-done | bytes 4718608 | tf_op jit(solution)/shard_map/all_gather | solution.py:150
  102.9 2.1 %collective-permute-start.3 = (bf16[768,3072]{1,0:T(8,128)(2,1)}, bf16[768,3072]{1,0:T(8,128)(2,1)S(1)}, u32[]{:S(2)}, u32[]{:S(2)}) collective-permute-start(bf16[768,3072]{1,0:T(8,128)(2,1)} %bitcast.115), channel_id=1, source_target_pairs={{0,8},{8,0},{1,9},{9,1},{2,10},{10,2},{3,11},{11,3},{4,12},{12,4},... | collective-permute-start | bytes 14155784 | tf_op jit(solution)/shard_map/ppermute | solution.py:176
  108.4 1.1 convolution_bitcast_fusion.1
  109.5 3.9 %fusion.40 = f32[256,3072]{1,0:T(8,128)S(1)} fusion(bf16[256,768]{0,1:T(8,128)(2,1)S(1)} %bitcast.121, bf16[768,3072]{1,0:T(8,128)(2,1)} %bitcast.116), kind=kOutput, calls=%fused_computation.100 | convolution fusion | flops 1207959552 | bytes 8257536 | tf_op jit(solution)/shard_map/dot_general | solution.py:23
  113.5 2.0 %fusion.38 = (f32[256]{0:T(256)S(1)}, f32[256,3072]{1,0:T(8,128)S(1)}) fusion(f32[256,3072]{1,0:T(8,128)S(1)} %fusion.40, bf16[256,768]{0,1:T(8,128)(2,1)S(1)} %bitcast.124, bf16[768,3072]{1,0:T(8,128)(2,1)S(1)} %collective-permute-done.3, f32[3072]{0:T(1024)S(1)} %bitcast.142, bf16[256,3072]{1,0:T(8,128)(2,1)S(1)} %bitcast.132), kind=kOutput, calls=%fused_computation.98 | convolution fusion | flops 1211891456 | bytes 12989440 | tf_op jit(solution)/shard_map/dot_general | solution.py:23
  117.7 1.3 fusion.6
  122.8 1.2 pad_maximum_fusion
  124.0 7.6 %all-to-all-start.1 = ((bf16[32,10,16,128]{3,2,1,0:T(8,128)(2,1)}), bf16[32,10,16,128]{3,2,1,0:T(8,128)(2,1)S(1)}, u32[]{:S(2)}, u32[]{:S(2)}) async-start(bf16[32,10,16,128]{3,2,1,0:T(8,128)(2,1)} %pad_maximum_fusion), calls=%async_computation.1 | async-start | bytes 2621440 | tf_op jit(solution)/shard_map/all_to_all | solution.py:225
  131.5 18.4 %all-to-all-done.1 = bf16[32,10,16,128]{3,2,1,0:T(8,128)(2,1)S(1)} async-done(((bf16[32,10,16,128]{3,2,1,0:T(8,128)(2,1)}), bf16[32,10,16,128]{3,2,1,0:T(8,128)(2,1)S(1)}, u32[]{:S(2)}, u32[]{:S(2)}) %all-to-all-start.1) | async-done | bytes 1310752 | tf_op jit(solution)/shard_map/all_to_all | solution.py:225
  151.2 20.7 %all_to_all.21 = f32[16,9,128]{2,1,0:T(8,128)S(1)} all-to-all(f32[16,9,128]{2,1,0:T(8,128)S(1)} %copy.87), channel_id=1, replica_groups=mesh['xh'=2,'z'=16,'c'=2,'xl'=2,'y'=4] {'z'}, dimensions={0} | all-to-all | bytes 147456 | tf_op jit(solution)/shard_map/all_to_all | solution.py:236
  171.9 10.0 %all_to_all.22 = f32[8,9,128]{2,1,0:T(8,128)S(1)} all-to-all(f32[8,9,128]{2,1,0:T(8,128)S(1)} %broadcast_in_dim.15), channel_id=1, replica_groups=mesh['xh'=2,'z'=16,'c'=2,'xl'=2,'y'=4] {'xl','y'}, dimensions={0} | all-to-all | bytes 73728 | tf_op jit(solution)/shard_map/all_to_all | solution.py:42
  (83 shorter events, 18.3 us)
Async XLA Ops:
  7.2 72.9 %copy-start.1 = (bf16[1,2,128,1536]{3,2,1,0:T(8,128)(2,1)S(1)}, bf16[1,2,128,1536]{3,2,1,0:T(8,128)(2,1)}, u32[]{:S(2)}) copy-start(bf16[1,2,128,1536]{3,2,1,0:T(8,128)(2,1)} %param.11) | copy-start | bytes 2359300
  7.2 95.7 %all-gather.4.cloned.1.call-start = ((), (), s32[]{:S(2)}) async-start(), calls=%async_computation.4 | async-start | bytes 5013504 | tf_op jit(solution)/shard_map/all_gather | solution.py:150
  7.2 11.2 %collective-permute-start = (bf16[24,3072]{1,0:T(8,128)(2,1)}, bf16[24,3072]{1,0:T(8,128)(2,1)S(1)}, u32[]{:S(2)}, u32[]{:S(2)}) collective-permute-start(bf16[24,3072]{1,0:T(8,128)(2,1)} %param.17), channel_id=1, source_target_pairs={{0,256},{256,0},{1,257},{257,1},{2,258},{258,2},{3,259},{259,3},{4... | collective-permute-start | bytes 442376 | tf_op jit(solution)/shard_map/ppermute | solution.py:149
  21.7 7.0 %collective-permute-start.1 = (bf16[12,128]{1,0:T(8,128)(2,1)S(1)}, bf16[12,128]{1,0:T(8,128)(2,1)S(1)}, u32[]{:S(2)}, u32[]{:S(2)}) collective-permute-start(bf16[12,128]{1,0:T(8,128)(2,1)S(1)} %fusion.65), channel_id=1, source_target_pairs={{0,256},{256,0},{1,257},{257,1},{2,258},{258,2},{3,259},{259,3},{4... | collective-permute-start | bytes 9224 | tf_op jit(solution)/shard_map/ppermute | solution.py:53
  78.1 4.3 %collective-permute-start.2 = (bf16[8,16,2,12,128]{4,1,3,2,0:T(8,128)(2,1)S(1)}, bf16[8,16,2,12,128]{4,1,3,2,0:T(8,128)(2,1)}, u32[]{:S(2)}, u32[]{:S(2)}) collective-permute-start(bf16[8,16,2,12,128]{4,1,3,2,0:T(8,128)(2,1)S(1)} %all_to_all.20), channel_id=1, source_target_pairs={{0,8},{8,0},{1,9},{9,1},{2,10},{10,2},{3,11},{11,3},{4,12},{12,4},... | collective-permute-start | bytes 2359304 | tf_op jit(solution)/shard_map/ppermute | solution.py:56
  91.5 14.9 %copy-start.6 = (s32[1,128]{1,0:T(1,128)S(1)}, s32[1,128]{1,0:T(1,128)}, u32[]{:S(2)}) copy-start(s32[1,128]{1,0:T(1,128)} %param.14) | copy-start | bytes 1540
  91.5 14.9 %copy-start.5 = (f32[2]{0:T(128)S(1)}, f32[2]{0:T(128)}, u32[]{:S(2)}) copy-start(f32[2]{0:T(128)} %constant.65.clone) | copy-start | bytes 28
  94.0 0.6 copy-start.3
  102.9 10.6 %collective-permute-start.3 = (bf16[768,3072]{1,0:T(8,128)(2,1)}, bf16[768,3072]{1,0:T(8,128)(2,1)S(1)}, u32[]{:S(2)}, u32[]{:S(2)}) collective-permute-start(bf16[768,3072]{1,0:T(8,128)(2,1)} %bitcast.115), channel_id=1, source_target_pairs={{0,8},{8,0},{1,9},{9,1},{2,10},{10,2},{3,11},{11,3},{4,12},{12,4},... | collective-permute-start | bytes 14155784 | tf_op jit(solution)/shard_map/ppermute | solution.py:176
  109.5 3.9 %copy-start.2 = (bf16[1,2,128,3072]{3,2,1,0:T(8,128)(2,1)S(1)}, bf16[1,2,128,3072]{3,2,1,0:T(8,128)(2,1)}, u32[]{:S(2)}) copy-start(bf16[1,2,128,3072]{3,2,1,0:T(8,128)(2,1)} %param.12) | copy-start | bytes 4718596
  113.4 2.0 %copy-start = (f32[256,3072]{1,0:T(8,128)S(1)}, f32[256,3072]{1,0:T(8,128)}, u32[]{:S(2)}) copy-start(f32[256,3072]{1,0:T(8,128)} %fusion.39) | copy-start | bytes 9437188
  119.0 1.4 copy-start.4
  124.0 25.9 %all-to-all-start.1 = ((bf16[32,10,16,128]{3,2,1,0:T(8,128)(2,1)}), bf16[32,10,16,128]{3,2,1,0:T(8,128)(2,1)S(1)}, u32[]{:S(2)}, u32[]{:S(2)}) async-start(bf16[32,10,16,128]{3,2,1,0:T(8,128)(2,1)} %pad_maximum_fusion), calls=%async_computation.1 | async-start | bytes 2621440 | tf_op jit(solution)/shard_map/all_to_all | solution.py:225
Sparse Core Ops, SparseCore 0:
  20.3 82.5 all-gather.3

commit v5 on v4

--- a/solution.py
+++ b/solution.py
@@ -86,18 +86,17 @@
     xh, core = lax.axis_index("xh"), lax.axis_index("c")
     normaliser = float(tokens * seqs * channels)
 
-    pair = jnp.stack([output_weight, lax.ppermute(output_weight, "xh", SWAP)])
+    pair = lax.all_gather(output_weight, "xh", axis=0)
     here = lax.all_gather(pair, "z", axis=0).reshape(depth // 2, width)
 
     down_all, up_all, final_all = gather_small(
         adapter_down, adapter_up, latent_weight, zs, seqs, xh, core, lax.axis_index(TOKENS)
     )
     flat_in = attended.reshape(rows, depth)
-    in_cores = flat_in.reshape(rows, 2, zs, 2, own).transpose(3, 1, 0, 2, 4)
-    in_cores = jnp.where(core == 0, in_cores, in_cores[::-1])
-    in_cores = jnp.where(xh == 0, in_cores, in_cores[:, ::-1])
-    in_cores = in_cores.transpose(0, 2, 3, 1, 4).reshape(2, rows, depth // 2)
-    in_here, in_there = in_cores[0], in_cores[1]
+    in_cores = flat_in.reshape(rows, 2, zs, 2, own).transpose(3, 0, 2, 1, 4)
+    in_cores = in_cores.reshape(2, rows, depth // 2)
+    in_here = jnp.where(core == 0, in_cores[0], in_cores[1])
+    in_there = jnp.where(core == 0, in_cores[1], in_cores[0])
     stream = residual.reshape(rows, width).astype(F32)
     shift, scale, gate = modulation[0, 0:1], 1.0 + modulation[0, 1:2], modulation[0, 2:3]
     final32 = final_all.astype(F32)
@@ -109,70 +108,8 @@
     mask_rows = jnp.broadcast_to(repaint_mask.astype(F32)[0], (kinds, tokens)).reshape(rows, 1)
 
     ready = (in_here, in_there, final_all, up_all, down_projected, adapter_term)
-    ready = ready + (scale, shift, gate, scale_final, shift_final, target_rows, mask_rows)
     here, ready = lax.optimization_barrier((here, ready))
-    in_here, in_there, final_all, up_all, down_projected, adapter_term = ready[:6]
-    scale, shift, gate, scale_final, shift_final, target_rows, mask_rows = ready[6:]
-    there = lax.ppermute(here, "c", SWAP)
-    both = jnp.where(core == 0, jnp.stack([here, there]), jnp.stack([there, here]))
-    both = both.reshape(2 * seqs, 4 * zs, piece, rank).transpose(1, 0, 2, 3)
-    both = both.reshape(4 * zs, 4 * own, rank)
-    down = both[:, :own].reshape(-1, rank)
-    up = both[:, own : 3 * own].reshape(-1, rank)
-    last = both[:, 3 * own :].reshape(4 * zs, own, 2, channels).transpose(0, 2, 1, 3)
-    return down, up, last.reshape(-1, channels)
-
-
-def local(
-    attended,
-    residual,
-    targets,
-    repaint_mask,
-    timesteps,
-    modulation,
-    output_weight,
-    adapter_down,
-    adapter_up,
-    latent_weight,
-):
-    _, kinds, tokens, depth = attended.shape
-    width = residual.shape[-1]
-    channels = targets.shape[-1]
-    rank = adapter_down.shape[1]
-    rows = kinds * tokens
-    own = output_weight.shape[0]
-    zs, ys = lax.axis_size("z"), lax.axis_size("y")
-    seqs = 2 * ys
-    xh, core = lax.axis_index("xh"), lax.axis_index("c")
-    normaliser = float(tokens * seqs * channels)
-
-    pair = jnp.stack([output_weight, lax.ppermute(output_weight, "xh", SWAP)])
-    here = lax.all_gather(pair, "z", axis=0).reshape(depth // 2, width)
-
-    down_all, up_all, final_all = gather_small(
-        adapter_down, adapter_up, latent_weight, zs, seqs, xh, core, lax.axis_index(TOKENS)
-    )
-    flat_in = attended.reshape(rows, depth)
-    in_cores = flat_in.reshape(rows, 2, zs, 2, own).transpose(3, 1, 0, 2, 4)
-    in_cores = jnp.where(core == 0, in_cores, in_cores[::-1])
-    in_cores = jnp.where(xh == 0, in_cores, in_cores[:, ::-1])
-    in_cores = in_cores.transpose(0, 2, 3, 1, 4).reshape(2, rows, depth // 2)
-    in_here, in_there = in_cores[0], in_cores[1]
-    stream = residual.reshape(rows, width).astype(F32)
-    shift, scale, gate = modulation[0, 0:1], 1.0 + modulation[0, 1:2], modulation[0, 2:3]
-    final32 = final_all.astype(F32)
-    scale_final, shift_final = exact_dot(scale, final32), exact_dot(shift, final32)
-    down_projected = dot(flat_in, down_all).astype(BF16)
-    adapter_term = ADAPTER_SCALE * dot_t(down_projected, up_all)
-
-    target_rows = targets.reshape(rows, channels).astype(F32)
-    mask_rows = jnp.broadcast_to(repaint_mask.astype(F32)[0], (kinds, tokens)).reshape(rows, 1)
-
-    here, in_here, in_there, final_all, up_all, down_projected, adapter_term = (
-        lax.optimization_barrier(
-            (here, in_here, in_there, final_all, up_all, down_projected, adapter_term)
-        )
-    )
+    in_here, in_there, final_all, up_all, down_projected, adapter_term = ready
     there = lax.ppermute(here, "c", SWAP)
     frozen = dot(in_here, here) + dot(in_there, there)
     hidden_ref = stream + gate * frozen
@@ -212,18 +149,17 @@
 
     down_gradient = down_gradient.reshape(2, zs, 2, own, rank)
     down_gradient = jnp.where(core == 0, down_gradient, down_gradient[::-1])
-    down_gradient = jnp.where(xh == 0, down_gradient, down_gradient[:, :, ::-1])
     down_gradient = down_gradient.transpose(2, 0, 1, 3, 4)
     up_gradient = up_gradient.reshape(2, zs, 2, 2 * own, rank).transpose(0, 2, 1, 3, 4)
     piece = 3 * own // seqs
     grads = jnp.concatenate([down_gradient, up_gradient], axis=3)
     grads = grads.reshape(2, 2, zs, seqs, piece, rank).transpose(0, 1, 3, 4, 2, 5)
-    grads = grads.reshape(4 * seqs, piece, zs, rank).astype(BF16)
-    errors = jnp.pad(in_three(errors), ((0, zs - 3), (0, rank - errors.shape[0])))
-    errors = jnp.broadcast_to(errors[None, None], (4 * seqs, 1) + errors.shape)
+    grads = grads.reshape(4 * seqs, piece * zs, rank).astype(BF16)
+    errors = jnp.pad(in_three(errors), ((0, 5), (0, rank - errors.shape[0])))
+    errors = jnp.broadcast_to(errors[None], (4 * seqs,) + errors.shape)
     grads = jnp.concatenate([grads, errors], axis=1)
     grads = lax.all_to_all(grads, ("xh", "c") + TOKENS, 0, 0)
-    errors = jnp.sum(grads[:, piece, :3].astype(F32), axis=1)
+    errors = jnp.sum(grads[:, piece * zs : piece * zs + 3].astype(F32), axis=1)
     errors = jnp.sum(errors.reshape(4, seqs, rank), axis=1)
     delta = errors[:, 0:1] - errors[:, 2:3] - (errors[:, 1:2] - errors[:, 3:4])
     weight_t = errors[:, 4:5]
@@ -231,7 +167,7 @@
     mine = jnp.arange(4)[:, None] == 2 * xh + core
     pair_loss = jnp.sum(jnp.where(mine, jax.nn.softplus(-logits), 0.0), axis=0)
     slope = jax.nn.sigmoid(-logits) * DPO_BETA * weight_t / normaliser
-    grads = grads[:, :piece].astype(F32).reshape(4, seqs, piece, zs, rank)
+    grads = grads[:, : piece * zs].astype(F32).reshape(4, seqs, piece, zs, rank)
     grads = jnp.sum(slope[:, :, None, None, None] * grads, axis=(0, 1))
     grads = lax.all_to_all(grads.transpose(1, 0, 2), "z", 0, 0)
     grads = spread(jnp.sum(grads, axis=0), TOKENS, seqs).reshape(3 * own, rank)

time: 191 us -> 187 us (0.979)
  blocking collectives: 80 us -> 90.3 us
  starting transfers between devices: 24.9 us -> 15.5 us
  other arithmetic: 10 us -> 7.9 us
  waiting for transfers between devices: 29.9 us -> 27.8 us
    all_gather x0 -> x1, blocking collectives: none -> 11.7 us  [local(): pair = lax.all_gather(output_weight, 'xh', axis=0)]
    ppermute x1 -> x0, starting transfers between devices: 7.92 us -> none  [local(): pair = jnp.stack([output_weight, lax.ppermute(output_weight, 'xh', SWAP)])]
    ppermute x1 -> x0, waiting for transfers between devices: 3.32 us -> none  [local(): pair = jnp.stack([output_weight, lax.ppermute(output_weight, 'xh', SWAP)])]
  transfers between devices with their start and end apart: 6 -> 5, of which waited for: 5 -> 4; matrix products, arithmetic and copies ran while one was open for 13% -> 13% of each run, Pallas kernels for 0% -> 0%
where the time goes in v5:
time: 187 us; the launch traced here: 186 us
  blocking collectives  90.3 us (48%)
  waiting for transfers between devices  27.8 us (15%)
  starting transfers between devices  15.5 us (8%)
  matrix products  15.5 us (8%)
  between operations  15.1 us (8%)
  local copies, waits for them, and re-layouts  14.4 us (8%)
  other arithmetic  7.9 us (4%)
    all_gather x1, blocking collectives, gather_small(): packed = lax.all_gather(packed, 'z', axis=0)  32.8 us
    all_to_all x2, blocking collectives, spread(): lax.all_to_all(jnp.broadcast_to(value[None], (size,) + value.shape), axes...  25 us
    all_to_all x1, blocking collectives, local(): grads = lax.all_to_all(grads.transpose(1, 0, 2), 'z', 0, 0)  20.8 us
    all_to_all x1, waiting for transfers between devices, local(): grads = lax.all_to_all(grads, ('xh', 'c') + TOKENS, 0, 0)  17.6 us
    all_gather x1, blocking collectives, local(): pair = lax.all_gather(output_weight, 'xh', axis=0)  11.7 us
    dot_general x6, matrix products, dot(): return jnp.dot(a, b, preferred_element_type=F32)  8.54 us
    all_to_all x1, starting transfers between devices, local(): grads = lax.all_to_all(grads, ('xh', 'c') + TOKENS, 0, 0)  7.56 us
    all_gather x1, waiting for transfers between devices, local(): here = lax.all_gather(pair, 'z', axis=0).reshape(depth // 2, width)  5.98 us
  transfers between devices with their start and end apart: 5, of which 4 were waited for; matrix products, arithmetic and copies ran while one was open for 13% of the time, Pallas kernels for 0%

profile of v5, /device:TPU:4, one launch (start us, length us, event | category | flops | bytes accessed | tf_op | source)
XLA Modules:
  0.0 186.5 jit_solution(3783493939812853684)
XLA Ops:
  7.2 11.7 %all-gather = bf16[48,3072]{1,0:T(8,128)(2,1)} all-gather(bf16[24,3072]{1,0:T(8,128)(2,1)} %param.17), channel_id=2, replica_groups=mesh['xh'=2,'z'=16,'c'=2,'xl'=2,'y'=4] {'xh'}, dimensions={0}, use_global_device_ids=true | all-gather | bytes 442368 | tf_op jit(solution)/shard_map/all_gather | solution.py:89
  20.4 3.9 %collective-permute-start = (bf16[12,128]{1,0:T(8,128)(2,1)S(1)}, bf16[12,128]{1,0:T(8,128)(2,1)S(1)}, u32[]{:S(2)}, u32[]{:S(2)}) collective-permute-start(bf16[12,128]{1,0:T(8,128)(2,1)S(1)} %fusion.63), channel_id=1, source_target_pairs={{0,256},{256,0},{1,257},{257,1},{2,258},{258,2},{3,259},{259,3},{4... | collective-permute-start | bytes 9224 | tf_op jit(solution)/shard_map/ppermute | solution.py:53
  24.4 3.1 %collective-permute-done = bf16[12,128]{1,0:T(8,128)(2,1)S(1)} collective-permute-done((bf16[12,128]{1,0:T(8,128)(2,1)S(1)}, bf16[12,128]{1,0:T(8,128)(2,1)S(1)}, u32[]{:S(2)}, u32[]{:S(2)}) %collective-permute-start) | collective-permute-done | bytes 3104 | tf_op jit(solution)/shard_map/ppermute | solution.py:53
  27.5 32.8 %all-gather.2 = bf16[32,12,128]{2,1,0:T(8,128)(2,1)S(1)} all-gather(bf16[2,12,128]{2,1,0:T(8,128)(2,1)S(1)} %pad_maximum_fusion.2), channel_id=4, replica_groups=mesh['xh'=2,'z'=16,'c'=2,'xl'=2,'y'=4] {'z'}, dimensions={0}, use_global_device_ids=true | all-gather | bytes 104448 | tf_op jit(solution)/shard_map/all_gather | solution.py:54
  60.5 14.9 %all_to_all.20 = bf16[8,16,2,12,128]{4,1,3,2,0:T(8,128)(2,1)S(1)} all-to-all(bf16[8,16,2,12,128]{4,1,3,2,0:T(8,128)(2,1)S(1)} %broadcast_in_dim.11), channel_id=1, replica_groups=mesh['xh'=2,'z'=16,'c'=2,'xl'=2,'y'=4] {'xl','y'}, dimensions={0} | all-to-all | bytes 1572864 | tf_op jit(solution)/shard_map/all_to_all | solution.py:42
  75.4 1.9 %collective-permute-start.1 = (bf16[8,16,2,12,128]{4,1,3,2,0:T(8,128)(2,1)S(1)}, bf16[8,16,2,12,128]{4,1,3,2,0:T(8,128)(2,1)}, u32[]{:S(2)}, u32[]{:S(2)}) collective-permute-start(bf16[8,16,2,12,128]{4,1,3,2,0:T(8,128)(2,1)S(1)} %all_to_all.20), channel_id=1, source_target_pairs={{0,8},{8,0},{1,9},{9,1},{2,10},{10,2},{3,11},{11,3},{4,12},{12,4},... | collective-permute-start | bytes 2359304 | tf_op jit(solution)/shard_map/ppermute | solution.py:56
  78.6 1.1 collective-permute-done.1
  79.7 1.6 maximum_select_fusion
  81.8 2.4 %copy.79 = bf16[2,16,2,8,12,128]{5,2,1,0,4,3:T(2,128)(2,1)S(1)} copy(bf16[2,16,2,8,12,128]{5,1,4,0,3,2:T(8,128)(2,1)S(1)} %fusion.7) | data formatting | bytes 3145728 | tf_op jit(solution)/shard_map/transpose | solution.py:59
  85.9 2.8 %reshape.257 = bf16[64,24,2,64]{3,2,0,1:T(2,128)(2,1)} reshape(bf16[64,24,128]{2,0,1:T(8,128)(2,1)} %get-tuple-element.29) | data formatting | bytes 786432 | tf_op jit(solution)/shard_map/reshape | solution.py:62
  88.8 2.1 %copy.80 = bf16[64,24,2,64]{3,1,2,0:T(8,128)(2,1)S(1)} copy(bf16[64,24,2,64]{3,2,0,1:T(2,128)(2,1)} %reshape.257) | data formatting | bytes 786432 | tf_op jit(solution)/shard_map/reshape | solution.py:62
  91.9 2.3 %fusion.37 = f32[256,3072]{1,0:T(8,128)} fusion(bf16[128,256]{1,0:T(8,128)(2,1)S(1)} %convolution_convert_fusion.1, bf16[3072,128]{1,0:T(8,128)(2,1)S(1)} %bitcast.116), kind=kOutput, calls=%fused_computation.95 | convolution fusion | flops 201326592 | bytes 3997696 | tf_op jit(solution)/shard_map/dot_general | solution.py:27
  94.1 6.0 %all-gather.5.cloned.1.call-done = bf16[32,24,3072]{2,1,0:T(8,128)(2,1)} async-done(((bf16[2,24,3072]{2,1,0:T(8,128)(2,1)}), bf16[32,24,3072]{2,1,0:T(8,128)(2,1)}) %all-gather.5.cloned.1.call-update) | async-done | bytes 4718608 | tf_op jit(solution)/shard_map/all_gather | solution.py:90
  100.1 2.1 %collective-permute-start.2 = (bf16[768,3072]{1,0:T(8,128)(2,1)}, bf16[768,3072]{1,0:T(8,128)(2,1)S(1)}, u32[]{:S(2)}, u32[]{:S(2)}) collective-permute-start(bf16[768,3072]{1,0:T(8,128)(2,1)} %bitcast.114), channel_id=1, source_target_pairs={{0,8},{8,0},{1,9},{9,1},{2,10},{10,2},{3,11},{11,3},{4,12},{12,4},... | collective-permute-start | bytes 14155784 | tf_op jit(solution)/shard_map/ppermute | solution.py:113
  104.5 1.1 convolution_bitcast_fusion
  105.6 1.1 convolution_bitcast_fusion.1
  106.8 3.9 %fusion.38 = f32[256,3072]{1,0:T(8,128)S(1)} fusion(bf16[256,768]{0,1:T(8,128)(2,1)S(1)} %bitcast.120, bf16[768,3072]{1,0:T(8,128)(2,1)} %bitcast.115), kind=kOutput, calls=%fused_computation.96 | convolution fusion | flops 1207959552 | bytes 8257536 | tf_op jit(solution)/shard_map/dot_general | solution.py:23
  110.7 2.0 %fusion.36 = (f32[256]{0:T(256)S(1)}, f32[256,3072]{1,0:T(8,128)S(1)}) fusion(f32[256,3072]{1,0:T(8,128)S(1)} %fusion.38, bf16[256,768]{0,1:T(8,128)(2,1)S(1)} %bitcast.123, bf16[768,3072]{1,0:T(8,128)(2,1)S(1)} %collective-permute-done.2, f32[3072]{0:T(1024)S(1)} %bitcast.140, bf16[256,3072]{1,0:T(8,128)(2,1)S(1)} %bitcast.131), kind=kOutput, calls=%fused_computation.94 | convolution fusion | flops 1211891456 | bytes 12989440 | tf_op jit(solution)/shard_map/dot_general | solution.py:23
  114.9 1.3 fusion.6
  119.9 1.1 pad_maximum_fusion
  121.0 7.6 %all-to-all-start.1 = ((bf16[32,152,128]{2,1,0:T(8,128)(2,1)}), bf16[32,152,128]{2,1,0:T(8,128)(2,1)S(1)}, u32[]{:S(2)}, u32[]{:S(2)}) async-start(bf16[32,152,128]{2,1,0:T(8,128)(2,1)} %pad_maximum_fusion), calls=%async_computation.1 | async-start | bytes 2490368 | tf_op jit(solution)/shard_map/all_to_all | solution.py:161
  128.6 17.6 %all-to-all-done.1 = bf16[32,152,128]{2,1,0:T(8,128)(2,1)S(1)} async-done(((bf16[32,152,128]{2,1,0:T(8,128)(2,1)}), bf16[32,152,128]{2,1,0:T(8,128)(2,1)S(1)}, u32[]{:S(2)}, u32[]{:S(2)}) %all-to-all-start.1) | async-done | bytes 1245216 | tf_op jit(solution)/shard_map/all_to_all | solution.py:161
  147.5 20.8 %all_to_all.21 = f32[16,9,128]{2,1,0:T(8,128)S(1)} all-to-all(f32[16,9,128]{2,1,0:T(8,128)S(1)} %copy.87), channel_id=1, replica_groups=mesh['xh'=2,'z'=16,'c'=2,'xl'=2,'y'=4] {'z'}, dimensions={0} | all-to-all | bytes 147456 | tf_op jit(solution)/shard_map/all_to_all | solution.py:172
  168.3 10.1 %all_to_all.22 = f32[8,9,128]{2,1,0:T(8,128)S(1)} all-to-all(f32[8,9,128]{2,1,0:T(8,128)S(1)} %broadcast_in_dim.15), channel_id=1, replica_groups=mesh['xh'=2,'z'=16,'c'=2,'xl'=2,'y'=4] {'xl','y'}, dimensions={0} | all-to-all | bytes 73728 | tf_op jit(solution)/shard_map/all_to_all | solution.py:42
  (78 shorter events, 16.0 us)
Async XLA Ops:
  7.2 70.2 %copy-start.1 = (bf16[1,2,128,1536]{3,2,1,0:T(8,128)(2,1)S(1)}, bf16[1,2,128,1536]{3,2,1,0:T(8,128)(2,1)}, u32[]{:S(2)}) copy-start(bf16[1,2,128,1536]{3,2,1,0:T(8,128)(2,1)} %param.11) | copy-start | bytes 2359300
  7.2 92.9 %all-gather.5.cloned.1.call-start = ((), (), s32[]{:S(2)}) async-start(), calls=%async_computation.4 | async-start | bytes 5013504 | tf_op jit(solution)/shard_map/all_gather | solution.py:90
  20.4 7.0 %collective-permute-start = (bf16[12,128]{1,0:T(8,128)(2,1)S(1)}, bf16[12,128]{1,0:T(8,128)(2,1)S(1)}, u32[]{:S(2)}, u32[]{:S(2)}) collective-permute-start(bf16[12,128]{1,0:T(8,128)(2,1)S(1)} %fusion.63), channel_id=1, source_target_pairs={{0,256},{256,0},{1,257},{257,1},{2,258},{258,2},{3,259},{259,3},{4... | collective-permute-start | bytes 9224 | tf_op jit(solution)/shard_map/ppermute | solution.py:53
  75.4 4.3 %collective-permute-start.1 = (bf16[8,16,2,12,128]{4,1,3,2,0:T(8,128)(2,1)S(1)}, bf16[8,16,2,12,128]{4,1,3,2,0:T(8,128)(2,1)}, u32[]{:S(2)}, u32[]{:S(2)}) collective-permute-start(bf16[8,16,2,12,128]{4,1,3,2,0:T(8,128)(2,1)S(1)} %all_to_all.20), channel_id=1, source_target_pairs={{0,8},{8,0},{1,9},{9,1},{2,10},{10,2},{3,11},{11,3},{4,12},{12,4},... | collective-permute-start | bytes 2359304 | tf_op jit(solution)/shard_map/ppermute | solution.py:56
  88.8 14.9 %copy-start.6 = (s32[1,128]{1,0:T(1,128)S(1)}, s32[1,128]{1,0:T(1,128)}, u32[]{:S(2)}) copy-start(s32[1,128]{1,0:T(1,128)} %param.14) | copy-start | bytes 1540
  88.8 14.9 %copy-start.5 = (f32[2]{0:T(128)S(1)}, f32[2]{0:T(128)}, u32[]{:S(2)}) copy-start(f32[2]{0:T(128)} %constant.65.clone) | copy-start | bytes 28
  91.2 0.6 copy-start.3
  100.1 10.6 %collective-permute-start.2 = (bf16[768,3072]{1,0:T(8,128)(2,1)}, bf16[768,3072]{1,0:T(8,128)(2,1)S(1)}, u32[]{:S(2)}, u32[]{:S(2)}) collective-permute-start(bf16[768,3072]{1,0:T(8,128)(2,1)} %bitcast.114), channel_id=1, source_target_pairs={{0,8},{8,0},{1,9},{9,1},{2,10},{10,2},{3,11},{11,3},{4,12},{12,4},... | collective-permute-start | bytes 14155784 | tf_op jit(solution)/shard_map/ppermute | solution.py:113
  106.8 3.9 %copy-start.2 = (bf16[1,2,128,3072]{3,2,1,0:T(8,128)(2,1)S(1)}, bf16[1,2,128,3072]{3,2,1,0:T(8,128)(2,1)}, u32[]{:S(2)}) copy-start(bf16[1,2,128,3072]{3,2,1,0:T(8,128)(2,1)} %param.12) | copy-start | bytes 4718596
  110.7 2.0 %copy-start = (f32[256,3072]{1,0:T(8,128)S(1)}, f32[256,3072]{1,0:T(8,128)}, u32[]{:S(2)}) copy-start(f32[256,3072]{1,0:T(8,128)} %fusion.37) | copy-start | bytes 9437188
  116.2 1.3 copy-start.4
  121.0 25.2 %all-to-all-start.1 = ((bf16[32,152,128]{2,1,0:T(8,128)(2,1)}), bf16[32,152,128]{2,1,0:T(8,128)(2,1)S(1)}, u32[]{:S(2)}, u32[]{:S(2)}) async-start(bf16[32,152,128]{2,1,0:T(8,128)(2,1)} %pad_maximum_fusion), calls=%async_computation.1 | async-start | bytes 2490368 | tf_op jit(solution)/shard_map/all_to_all | solution.py:161
Sparse Core Ops, SparseCore 0:
  19.0 81.0 all-gather.4

commit v6 on v5

--- a/solution.py
+++ b/solution.py
@@ -36,6 +36,11 @@
     rest = value - first
     second = lax.reduce_precision(rest, 8, 7)
     return jnp.stack([first, second, rest - second]).astype(BF16)
+
+
+def in_two(value, axis):
+    first = lax.reduce_precision(value, 8, 7)
+    return jnp.concatenate([first, value - first], axis=axis).astype(BF16)
 
 
 def spread(value, axes, size):
@@ -103,13 +108,14 @@
     scale_final, shift_final = exact_dot(scale, final32), exact_dot(shift, final32)
     down_projected = dot(flat_in, down_all).astype(BF16)
     adapter_term = ADAPTER_SCALE * dot_t(down_projected, up_all)
+    final_twice = jnp.concatenate([final_all, final_all], axis=1)
 
     target_rows = targets.reshape(rows, channels).astype(F32)
     mask_rows = jnp.broadcast_to(repaint_mask.astype(F32)[0], (kinds, tokens)).reshape(rows, 1)
 
-    ready = (in_here, in_there, final_all, up_all, down_projected, adapter_term)
+    ready = (in_here, in_there, final_all, final_twice, up_all, down_projected, adapter_term)
     here, ready = lax.optimization_barrier((here, ready))
-    in_here, in_there, final_all, up_all, down_projected, adapter_term = ready
+    in_here, in_there, final_all, final_twice, up_all, down_projected, adapter_term = ready
     there = lax.ppermute(here, "c", SWAP)
     frozen = dot(in_here, here) + dot(in_there, there)
     hidden_ref = stream + gate * frozen
@@ -137,15 +143,15 @@
     errors = jnp.concatenate([errors / normaliser, weight_t])
 
     signs = jnp.repeat(jnp.array([2.0, -2.0], F32), tokens)[:, None]
-    grad_pred = (signs * mask_rows * miss_pol).astype(BF16)
-    grad32 = grad_pred.astype(F32)
-    first = jnp.sum(grad32 * scale_final, axis=1, keepdims=True) / width
-    second = jnp.sum(grad32 * (pred_pol - shift_final), axis=1, keepdims=True) / width
-    grad_norm = dot_t(grad_pred, final_all) * scale
+    grad_pred = signs * mask_rows * miss_pol
+    first = jnp.sum(grad_pred * scale_final, axis=1, keepdims=True) / width
+    second = jnp.sum(grad_pred * (pred_pol - shift_final), axis=1, keepdims=True) / width
+    grad_norm = dot_t(in_two(grad_pred, 1), final_twice) * scale
     update = (gate * (inverse * (grad_norm - first - normed * second))).astype(BF16)
     up_gradient = ADAPTER_SCALE * t_dot(update, down_projected)
-    grad_low = (ADAPTER_SCALE * dot(update, up_all)).astype(BF16)
+    grad_low = in_two(ADAPTER_SCALE * dot(update, up_all), 1)
     down_gradient = jnp.stack([t_dot(in_here, grad_low), t_dot(in_there, grad_low)])
+    down_gradient = down_gradient[:, :, :rank] + down_gradient[:, :, rank:]
 
     down_gradient = down_gradient.reshape(2, zs, 2, own, rank)
     down_gradient = jnp.where(core == 0, down_gradient, down_gradient[::-1])
@@ -169,7 +175,7 @@
     slope = jax.nn.sigmoid(-logits) * DPO_BETA * weight_t / normaliser
     grads = grads[:, : piece * zs].astype(F32).reshape(4, seqs, piece, zs, rank)
     grads = jnp.sum(slope[:, :, None, None, None] * grads, axis=(0, 1))
-    grads = lax.all_to_all(grads.transpose(1, 0, 2), "z", 0, 0)
+    grads = lax.all_to_all(grads.transpose(1, 0, 2).astype(BF16), "z", 0, 0).astype(F32)
     grads = spread(jnp.sum(grads, axis=0), TOKENS, seqs).reshape(3 * own, rank)
     return (pair_loss, grads[:own], grads[own:])
 

time: 187 us -> 185 us (0.989)
  the two profiles are of different devices: /device:TPU:4 before, /device:TPU:2 now
where the time goes in v6:
time: 185 us; the launch traced here: 184 us
  blocking collectives  88.5 us (48%)
  waiting for transfers between devices  30.8 us (17%)
  between operations  15.1 us (8%)
  starting transfers between devices  14.8 us (8%)
  matrix products  14.4 us (8%)
  local copies, waits for them, and re-layouts  13 us (7%)
  other arithmetic  7.72 us (4%)
    all_gather x1, blocking collectives, gather_small(): packed = lax.all_gather(packed, 'z', axis=0)  36.3 us
    all_to_all x2, blocking collectives, spread(): lax.all_to_all(jnp.broadcast_to(value[None], (size,) + value.shape), axes...  24.1 us
    all_to_all x1, blocking collectives, local(): lax.all_to_all(grads.transpose(1, 0, 2).astype(BF16), 'z', 0, 0).astype(F32)  19.5 us
    all_to_all x1, waiting for transfers between devices, local(): grads = lax.all_to_all(grads, ('xh', 'c') + TOKENS, 0, 0)  17.5 us
    dot_general x6, matrix products, dot(): return jnp.dot(a, b, preferred_element_type=F32)  8.68 us
    all_gather x1, blocking collectives, local(): pair = lax.all_gather(output_weight, 'xh', axis=0)  8.64 us
    all_to_all x1, starting transfers between devices, local(): grads = lax.all_to_all(grads, ('xh', 'c') + TOKENS, 0, 0)  7.12 us
    all_gather x1, waiting for transfers between devices, local(): here = lax.all_gather(pair, 'z', axis=0).reshape(depth // 2, width)  6.45 us
  transfers between devices with their start and end apart: 5, of which 5 were waited for; matrix products, arithmetic and copies ran while one was open for 12% of the time, Pallas kernels for 0%

profile of v6, /device:TPU:2, one launch (start us, length us, event | category | flops | bytes accessed | tf_op | source)
XLA Modules:
  0.0 184.3 jit_solution(6788934095607231706)
XLA Ops:
  7.2 8.6 %all-gather = bf16[48,3072]{1,0:T(8,128)(2,1)} all-gather(bf16[24,3072]{1,0:T(8,128)(2,1)} %param.17), channel_id=2, replica_groups=mesh['xh'=2,'z'=16,'c'=2,'xl'=2,'y'=4] {'xh'}, dimensions={0}, use_global_device_ids=true | all-gather | bytes 442368 | tf_op jit(solution)/shard_map/all_gather | solution.py:94
  17.4 3.6 %collective-permute-start = (bf16[12,128]{1,0:T(8,128)(2,1)S(1)}, bf16[12,128]{1,0:T(8,128)(2,1)S(1)}, u32[]{:S(2)}, u32[]{:S(2)}) collective-permute-start(bf16[12,128]{1,0:T(8,128)(2,1)S(1)} %fusion.66), channel_id=1, source_target_pairs={{0,256},{256,0},{1,257},{257,1},{2,258},{258,2},{3,259},{259,3},{4... | collective-permute-start | bytes 9224 | tf_op jit(solution)/shard_map/ppermute | solution.py:58
  21.1 3.4 %collective-permute-done = bf16[12,128]{1,0:T(8,128)(2,1)S(1)} collective-permute-done((bf16[12,128]{1,0:T(8,128)(2,1)S(1)}, bf16[12,128]{1,0:T(8,128)(2,1)S(1)}, u32[]{:S(2)}, u32[]{:S(2)}) %collective-permute-start) | collective-permute-done | bytes 3104 | tf_op jit(solution)/shard_map/ppermute | solution.py:58
  24.4 36.3 %all-gather.2 = bf16[32,12,128]{2,1,0:T(8,128)(2,1)S(1)} all-gather(bf16[2,12,128]{2,1,0:T(8,128)(2,1)S(1)} %pad_maximum_fusion.7), channel_id=4, replica_groups=mesh['xh'=2,'z'=16,'c'=2,'xl'=2,'y'=4] {'z'}, dimensions={0}, use_global_device_ids=true | all-gather | bytes 104448 | tf_op jit(solution)/shard_map/all_gather | solution.py:59
  60.9 14.5 %all_to_all.20 = bf16[8,16,2,12,128]{4,1,3,2,0:T(8,128)(2,1)S(1)} all-to-all(bf16[8,16,2,12,128]{4,1,3,2,0:T(8,128)(2,1)S(1)} %broadcast_in_dim.11), channel_id=1, replica_groups=mesh['xh'=2,'z'=16,'c'=2,'xl'=2,'y'=4] {'xl','y'}, dimensions={0} | all-to-all | bytes 1572864 | tf_op jit(solution)/shard_map/all_to_all | solution.py:47
  75.4 1.9 %collective-permute-start.1 = (bf16[8,16,2,12,128]{4,1,3,2,0:T(8,128)(2,1)S(1)}, bf16[8,16,2,12,128]{4,1,3,2,0:T(8,128)(2,1)}, u32[]{:S(2)}, u32[]{:S(2)}) collective-permute-start(bf16[8,16,2,12,128]{4,1,3,2,0:T(8,128)(2,1)S(1)} %all_to_all.20), channel_id=1, source_target_pairs={{0,8},{8,0},{1,9},{9,1},{2,10},{10,2},{3,11},{11,3},{4,12},{12,4},... | collective-permute-start | bytes 2359304 | tf_op jit(solution)/shard_map/ppermute | solution.py:61
  78.6 1.1 collective-permute-done.1
  79.7 1.6 maximum_select_fusion
  81.8 2.4 %copy.79 = bf16[2,16,2,8,12,128]{5,2,1,0,4,3:T(2,128)(2,1)S(1)} copy(bf16[2,16,2,8,12,128]{5,1,4,0,3,2:T(8,128)(2,1)S(1)} %fusion.7) | data formatting | bytes 3145728 | tf_op jit(solution)/shard_map/transpose | solution.py:64
  85.9 2.8 %reshape.256 = bf16[64,24,2,64]{3,2,0,1:T(2,128)(2,1)} reshape(bf16[64,24,128]{2,0,1:T(8,128)(2,1)} %get-tuple-element.32) | data formatting | bytes 786432 | tf_op jit(solution)/shard_map/reshape | solution.py:67
  88.8 2.1 %copy.80 = bf16[64,24,2,64]{3,1,2,0:T(8,128)(2,1)S(1)} copy(bf16[64,24,2,64]{3,2,0,1:T(2,128)(2,1)} %reshape.256) | data formatting | bytes 786432 | tf_op jit(solution)/shard_map/reshape | solution.py:67
  91.3 2.3 %fusion.45 = f32[256,3072]{1,0:T(8,128)} fusion(bf16[128,256]{1,0:T(8,128)(2,1)S(1)} %convolution_convert_fusion.1, bf16[3072,128]{1,0:T(8,128)(2,1)S(1)} %bitcast.112), kind=kOutput, calls=%fused_computation.111 | convolution fusion | flops 201326592 | bytes 3997696 | tf_op jit(solution)/shard_map/dot_general | solution.py:27
  94.0 6.5 %all-gather.5.cloned.1.call-done = bf16[32,24,3072]{2,1,0:T(8,128)(2,1)} async-done(((bf16[2,24,3072]{2,1,0:T(8,128)(2,1)}), bf16[32,24,3072]{2,1,0:T(8,128)(2,1)}) %all-gather.5.cloned.1.call-update) | async-done | bytes 4718608 | tf_op jit(solution)/shard_map/all_gather | solution.py:95
  100.5 2.1 %collective-permute-start.2 = (bf16[768,3072]{1,0:T(8,128)(2,1)}, bf16[768,3072]{1,0:T(8,128)(2,1)S(1)}, u32[]{:S(2)}, u32[]{:S(2)}) collective-permute-start(bf16[768,3072]{1,0:T(8,128)(2,1)} %bitcast.110), channel_id=1, source_target_pairs={{0,8},{8,0},{1,9},{9,1},{2,10},{10,2},{3,11},{11,3},{4,12},{12,4},... | collective-permute-start | bytes 14155784 | tf_op jit(solution)/shard_map/ppermute | solution.py:119
  104.2 3.9 %fusion.46 = f32[256,3072]{1,0:T(8,128)S(1)} fusion(bf16[256,768]{0,1:T(8,128)(2,1)S(1)} %bitcast.116, bf16[768,3072]{1,0:T(8,128)(2,1)} %bitcast.111), kind=kOutput, calls=%fused_computation.112 | convolution fusion | flops 1207959552 | bytes 8257536 | tf_op jit(solution)/shard_map/dot_general | solution.py:23
  108.2 2.3 %collective-permute-done.2 = bf16[768,3072]{1,0:T(8,128)(2,1)S(1)} collective-permute-done((bf16[768,3072]{1,0:T(8,128)(2,1)}, bf16[768,3072]{1,0:T(8,128)(2,1)S(1)}, u32[]{:S(2)}, u32[]{:S(2)}) %collective-permute-start.2) | collective-permute-done | bytes 4718624 | tf_op jit(solution)/shard_map/ppermute | solution.py:119
  110.5 2.0 %fusion.44 = (f32[256]{0:T(256)S(1)}, f32[256,3072]{1,0:T(8,128)S(1)}) fusion(f32[256,3072]{1,0:T(8,128)S(1)} %fusion.46, bf16[256,768]{0,1:T(8,128)(2,1)S(1)} %bitcast.119, bf16[768,3072]{1,0:T(8,128)(2,1)S(1)} %collective-permute-done.2, f32[3072]{0:T(1024)S(1)} %bitcast.135, bf16[256,3072]{1,0:T(8,128)(2,1)S(1)} %bitcast.128), kind=kOutput, calls=%fused_computation.110 | convolution fusion | flops 1211891456 | bytes 12989440 | tf_op jit(solution)/shard_map/dot_general | solution.py:23
  114.7 1.4 fusion.6
  118.7 0.8 fusion.16
  120.0 1.1 pad_maximum_fusion
  121.2 7.1 %all-to-all-start.1 = ((bf16[32,152,128]{2,1,0:T(8,128)(2,1)}), bf16[32,152,128]{2,1,0:T(8,128)(2,1)S(1)}, u32[]{:S(2)}, u32[]{:S(2)}) async-start(bf16[32,152,128]{2,1,0:T(8,128)(2,1)} %pad_maximum_fusion), calls=%async_computation.1 | async-start | bytes 2490368 | tf_op jit(solution)/shard_map/all_to_all | solution.py:167
  128.3 17.5 %all-to-all-done.1 = bf16[32,152,128]{2,1,0:T(8,128)(2,1)S(1)} async-done(((bf16[32,152,128]{2,1,0:T(8,128)(2,1)}), bf16[32,152,128]{2,1,0:T(8,128)(2,1)S(1)}, u32[]{:S(2)}, u32[]{:S(2)}) %all-to-all-start.1) | async-done | bytes 1245216 | tf_op jit(solution)/shard_map/all_to_all | solution.py:167
  147.1 19.5 %all_to_all.21 = bf16[16,9,128]{2,1,0:T(8,128)(2,1)S(1)} all-to-all(bf16[16,9,128]{2,1,0:T(8,128)(2,1)S(1)} %copy.87), channel_id=1, replica_groups=mesh['xh'=2,'z'=16,'c'=2,'xl'=2,'y'=4] {'z'}, dimensions={0} | all-to-all | bytes 73728 | tf_op jit(solution)/shard_map/all_to_all | solution.py:178
  166.6 9.6 %all_to_all.22 = f32[8,9,128]{2,1,0:T(8,128)S(1)} all-to-all(f32[8,9,128]{2,1,0:T(8,128)S(1)} %broadcast_in_dim.15), channel_id=1, replica_groups=mesh['xh'=2,'z'=16,'c'=2,'xl'=2,'y'=4] {'xl','y'}, dimensions={0} | all-to-all | bytes 73728 | tf_op jit(solution)/shard_map/all_to_all | solution.py:47
  (84 shorter events, 14.6 us)
Async XLA Ops:
  7.2 70.2 %copy-start.1 = (bf16[1,2,128,1536]{3,2,1,0:T(8,128)(2,1)S(1)}, bf16[1,2,128,1536]{3,2,1,0:T(8,128)(2,1)}, u32[]{:S(2)}) copy-start(bf16[1,2,128,1536]{3,2,1,0:T(8,128)(2,1)} %param.11) | copy-start | bytes 2359300
  7.2 93.3 %all-gather.5.cloned.1.call-start = ((), (), s32[]{:S(2)}) async-start(), calls=%async_computation.4 | async-start | bytes 5013504 | tf_op jit(solution)/shard_map/all_gather | solution.py:95
  17.4 7.0 %collective-permute-start = (bf16[12,128]{1,0:T(8,128)(2,1)S(1)}, bf16[12,128]{1,0:T(8,128)(2,1)S(1)}, u32[]{:S(2)}, u32[]{:S(2)}) collective-permute-start(bf16[12,128]{1,0:T(8,128)(2,1)S(1)} %fusion.66), channel_id=1, source_target_pairs={{0,256},{256,0},{1,257},{257,1},{2,258},{258,2},{3,259},{259,3},{4... | collective-permute-start | bytes 9224 | tf_op jit(solution)/shard_map/ppermute | solution.py:58
  75.4 4.3 %collective-permute-start.1 = (bf16[8,16,2,12,128]{4,1,3,2,0:T(8,128)(2,1)S(1)}, bf16[8,16,2,12,128]{4,1,3,2,0:T(8,128)(2,1)}, u32[]{:S(2)}, u32[]{:S(2)}) collective-permute-start(bf16[8,16,2,12,128]{4,1,3,2,0:T(8,128)(2,1)S(1)} %all_to_all.20), channel_id=1, source_target_pairs={{0,8},{8,0},{1,9},{9,1},{2,10},{10,2},{3,11},{11,3},{4,12},{12,4},... | collective-permute-start | bytes 2359304 | tf_op jit(solution)/shard_map/ppermute | solution.py:61
  91.2 2.3 %copy-start.3 = (bf16[128,256]{1,0:T(8,128)(2,1)}, bf16[128,256]{1,0:T(8,128)(2,1)S(1)}, u32[]{:S(2)}) copy-start(bf16[128,256]{1,0:T(8,128)(2,1)S(1)} %convolution_convert_fusion.1) | copy-start | bytes 196612
  91.2 11.3 %copy-start.6 = (bf16[1,2,128,64]{2,3,1,0:T(8,128)(2,1)S(1)}, bf16[1,2,128,64]{2,3,1,0:T(8,128)(2,1)}, u32[]{:S(2)}) copy-start(bf16[1,2,128,64]{2,3,1,0:T(8,128)(2,1)} %param.13) | copy-start | bytes 98308
  91.3 12.0 %copy-start.8 = (s32[1,128]{1,0:T(1,128)S(1)}, s32[1,128]{1,0:T(1,128)}, u32[]{:S(2)}) copy-start(s32[1,128]{1,0:T(1,128)} %param.14) | copy-start | bytes 1540
  91.3 12.0 %copy-start.7 = (f32[2]{0:T(128)S(1)}, f32[2]{0:T(128)}, u32[]{:S(2)}) copy-start(f32[2]{0:T(128)} %constant.65.clone) | copy-start | bytes 28
  91.3 12.1 %copy-start.5 = (f32[1,3,3072]{2,0,1:T(1,128)S(1)}, f32[1,3,3072]{2,0,1:T(1,128)}, u32[]{:S(2)}) copy-start(f32[1,3,3072]{2,0,1:T(1,128)} %param.16) | copy-start | bytes 110596
  100.5 10.0 %collective-permute-start.2 = (bf16[768,3072]{1,0:T(8,128)(2,1)}, bf16[768,3072]{1,0:T(8,128)(2,1)S(1)}, u32[]{:S(2)}, u32[]{:S(2)}) collective-permute-start(bf16[768,3072]{1,0:T(8,128)(2,1)} %bitcast.110), channel_id=1, source_target_pairs={{0,8},{8,0},{1,9},{9,1},{2,10},{10,2},{3,11},{11,3},{4,12},{12,4},... | collective-permute-start | bytes 14155784 | tf_op jit(solution)/shard_map/ppermute | solution.py:119
  104.2 6.2 %copy-start.2 = (bf16[1,2,128,3072]{3,2,1,0:T(8,128)(2,1)S(1)}, bf16[1,2,128,3072]{3,2,1,0:T(8,128)(2,1)}, u32[]{:S(2)}) copy-start(bf16[1,2,128,3072]{3,2,1,0:T(8,128)(2,1)} %param.12) | copy-start | bytes 4718596
  110.5 2.0 %copy-start = (f32[256,3072]{1,0:T(8,128)S(1)}, f32[256,3072]{1,0:T(8,128)}, u32[]{:S(2)}) copy-start(f32[256,3072]{1,0:T(8,128)} %fusion.45) | copy-start | bytes 9437188
  116.8 0.9 copy-start.4
  121.2 24.7 %all-to-all-start.1 = ((bf16[32,152,128]{2,1,0:T(8,128)(2,1)}), bf16[32,152,128]{2,1,0:T(8,128)(2,1)S(1)}, u32[]{:S(2)}, u32[]{:S(2)}) async-start(bf16[32,152,128]{2,1,0:T(8,128)(2,1)} %pad_maximum_fusion), calls=%async_computation.1 | async-start | bytes 2490368 | tf_op jit(solution)/shard_map/all_to_all | solution.py:167
Sparse Core Ops, SparseCore 0:
  16.0 84.4 all-gather.4

commit v7 on v6

--- a/solution.py
+++ b/solution.py
@@ -91,7 +91,7 @@
     xh, core = lax.axis_index("xh"), lax.axis_index("c")
     normaliser = float(tokens * seqs * channels)
 
-    pair = lax.all_gather(output_weight, "xh", axis=0)
+    pair = lax.all_gather(output_weight, ("xh", "xl"), axis=0, axis_index_groups=[[0, 3], [1, 2]])
     here = lax.all_gather(pair, "z", axis=0).reshape(depth // 2, width)
 
     down_all, up_all, final_all = gather_small(

time: 185 us -> 185 us (level)
  starting transfers between devices: 14.8 us -> 18.8 us
  blocking collectives: 88.5 us -> 85.9 us
    ppermute x1, starting transfers between devices: 3.61 us -> 7.66 us  [gather_small(): packed = jnp.stack([packed, lax.ppermute(packed, 'xh', SWAP)])]
    all_gather x1, blocking collectives: 36.3 us -> 33.9 us  [gather_small(): packed = lax.all_gather(packed, 'z', axis=0)]
where the time goes in v7:
time: 185 us; the launch traced here: 184 us
  blocking collectives  85.9 us (46%)
  waiting for transfers between devices  29 us (16%)
  starting transfers between devices  18.8 us (10%)
  between operations  15.1 us (8%)
  matrix products  14.4 us (8%)
  local copies, waits for them, and re-layouts  13 us (7%)
  other arithmetic  7.72 us (4%)
    all_gather x1, blocking collectives, gather_small(): packed = lax.all_gather(packed, 'z', axis=0)  33.9 us
    all_to_all x2, blocking collectives, spread(): lax.all_to_all(jnp.broadcast_to(value[None], (size,) + value.shape), axes...  24.3 us
    all_to_all x1, blocking collectives, local(): lax.all_to_all(grads.transpose(1, 0, 2).astype(BF16), 'z', 0, 0).astype(F32)  19.6 us
    all_to_all x1, waiting for transfers between devices, local(): grads = lax.all_to_all(grads, ('xh', 'c') + TOKENS, 0, 0)  17.5 us
    dot_general x6, matrix products, dot(): return jnp.dot(a, b, preferred_element_type=F32)  8.68 us
    all_gather x1, blocking collectives, local(): lax.all_gather(output_weight, ('xh', 'xl'), axis=0, axis_index_groups=[[0...  8.01 us
    ppermute x1, starting transfers between devices, gather_small(): packed = jnp.stack([packed, lax.ppermute(packed, 'xh', SWAP)])  7.66 us
    all_to_all x1, starting transfers between devices, local(): grads = lax.all_to_all(grads, ('xh', 'c') + TOKENS, 0, 0)  7.12 us
  transfers between devices with their start and end apart: 5, of which 5 were waited for; matrix products, arithmetic and copies ran while one was open for 12% of the time, Pallas kernels for 0%

profile of v7, /device:TPU:2, one launch (start us, length us, event | category | flops | bytes accessed | tf_op | source)
XLA Modules:
  0.0 183.9 jit_solution(7355514064041097412)
XLA Ops:
  7.2 8.0 %all-gather = bf16[48,3072]{1,0:T(8,128)(2,1)} all-gather(bf16[24,3072]{1,0:T(8,128)(2,1)} %param.17), channel_id=2, replica_groups={{0,260},{4,256},{1,261},{5,257},{2,262},{6,258},{3,263},{7,259},{8,268}..., dimensions={0}, use_global_device_ids=true | all-gather | bytes 442368 | tf_op jit(solution)/shard_map/all_gather | solution.py:94
  16.8 7.7 %collective-permute-start = (bf16[12,128]{1,0:T(8,128)(2,1)S(1)}, bf16[12,128]{1,0:T(8,128)(2,1)S(1)}, u32[]{:S(2)}, u32[]{:S(2)}) collective-permute-start(bf16[12,128]{1,0:T(8,128)(2,1)S(1)} %fusion.66), channel_id=1, source_target_pairs={{0,256},{256,0},{1,257},{257,1},{2,258},{258,2},{3,259},{259,3},{4... | collective-permute-start | bytes 9224 | tf_op jit(solution)/shard_map/ppermute | solution.py:58
  24.5 1.6 collective-permute-done
  26.0 33.9 %all-gather.2 = bf16[32,12,128]{2,1,0:T(8,128)(2,1)S(1)} all-gather(bf16[2,12,128]{2,1,0:T(8,128)(2,1)S(1)} %pad_maximum_fusion.7), channel_id=4, replica_groups=mesh['xh'=2,'z'=16,'c'=2,'xl'=2,'y'=4] {'z'}, dimensions={0}, use_global_device_ids=true | all-gather | bytes 104448 | tf_op jit(solution)/shard_map/all_gather | solution.py:59
  60.2 14.7 %all_to_all.20 = bf16[8,16,2,12,128]{4,1,3,2,0:T(8,128)(2,1)S(1)} all-to-all(bf16[8,16,2,12,128]{4,1,3,2,0:T(8,128)(2,1)S(1)} %broadcast_in_dim.11), channel_id=1, replica_groups=mesh['xh'=2,'z'=16,'c'=2,'xl'=2,'y'=4] {'xl','y'}, dimensions={0} | all-to-all | bytes 1572864 | tf_op jit(solution)/shard_map/all_to_all | solution.py:47
  74.9 1.9 %collective-permute-start.1 = (bf16[8,16,2,12,128]{4,1,3,2,0:T(8,128)(2,1)S(1)}, bf16[8,16,2,12,128]{4,1,3,2,0:T(8,128)(2,1)}, u32[]{:S(2)}, u32[]{:S(2)}) collective-permute-start(bf16[8,16,2,12,128]{4,1,3,2,0:T(8,128)(2,1)S(1)} %all_to_all.20), channel_id=1, source_target_pairs={{0,8},{8,0},{1,9},{9,1},{2,10},{10,2},{3,11},{11,3},{4,12},{12,4},... | collective-permute-start | bytes 2359304 | tf_op jit(solution)/shard_map/ppermute | solution.py:61
  78.1 1.1 collective-permute-done.1
  79.2 1.6 maximum_select_fusion
  81.3 2.4 %copy.79 = bf16[2,16,2,8,12,128]{5,2,1,0,4,3:T(2,128)(2,1)S(1)} copy(bf16[2,16,2,8,12,128]{5,1,4,0,3,2:T(8,128)(2,1)S(1)} %fusion.7) | data formatting | bytes 3145728 | tf_op jit(solution)/shard_map/transpose | solution.py:64
  85.4 2.8 %reshape.256 = bf16[64,24,2,64]{3,2,0,1:T(2,128)(2,1)} reshape(bf16[64,24,128]{2,0,1:T(8,128)(2,1)} %get-tuple-element.32) | data formatting | bytes 786432 | tf_op jit(solution)/shard_map/reshape | solution.py:67
  88.2 2.0 %copy.80 = bf16[64,24,2,64]{3,1,2,0:T(8,128)(2,1)S(1)} copy(bf16[64,24,2,64]{3,2,0,1:T(2,128)(2,1)} %reshape.256) | data formatting | bytes 786432 | tf_op jit(solution)/shard_map/reshape | solution.py:67
  90.8 2.3 %fusion.45 = f32[256,3072]{1,0:T(8,128)} fusion(bf16[128,256]{1,0:T(8,128)(2,1)S(1)} %convolution_convert_fusion.1, bf16[3072,128]{1,0:T(8,128)(2,1)S(1)} %bitcast.112), kind=kOutput, calls=%fused_computation.111 | convolution fusion | flops 201326592 | bytes 3997696 | tf_op jit(solution)/shard_map/dot_general | solution.py:27
  93.5 6.5 %all-gather.5.cloned.1.call-done = bf16[32,24,3072]{2,1,0:T(8,128)(2,1)} async-done(((bf16[2,24,3072]{2,1,0:T(8,128)(2,1)}), bf16[32,24,3072]{2,1,0:T(8,128)(2,1)}) %all-gather.5.cloned.1.call-update) | async-done | bytes 4718608 | tf_op jit(solution)/shard_map/all_gather | solution.py:95
  100.0 2.1 %collective-permute-start.2 = (bf16[768,3072]{1,0:T(8,128)(2,1)}, bf16[768,3072]{1,0:T(8,128)(2,1)S(1)}, u32[]{:S(2)}, u32[]{:S(2)}) collective-permute-start(bf16[768,3072]{1,0:T(8,128)(2,1)} %bitcast.110), channel_id=1, source_target_pairs={{0,8},{8,0},{1,9},{9,1},{2,10},{10,2},{3,11},{11,3},{4,12},{12,4},... | collective-permute-start | bytes 14155784 | tf_op jit(solution)/shard_map/ppermute | solution.py:119
  103.7 3.9 %fusion.46 = f32[256,3072]{1,0:T(8,128)S(1)} fusion(bf16[256,768]{0,1:T(8,128)(2,1)S(1)} %bitcast.116, bf16[768,3072]{1,0:T(8,128)(2,1)} %bitcast.111), kind=kOutput, calls=%fused_computation.112 | convolution fusion | flops 1207959552 | bytes 8257536 | tf_op jit(solution)/shard_map/dot_general | solution.py:23
  107.7 2.3 %collective-permute-done.2 = bf16[768,3072]{1,0:T(8,128)(2,1)S(1)} collective-permute-done((bf16[768,3072]{1,0:T(8,128)(2,1)}, bf16[768,3072]{1,0:T(8,128)(2,1)S(1)}, u32[]{:S(2)}, u32[]{:S(2)}) %collective-permute-start.2) | collective-permute-done | bytes 4718624 | tf_op jit(solution)/shard_map/ppermute | solution.py:119
  110.0 2.0 %fusion.44 = (f32[256]{0:T(256)S(1)}, f32[256,3072]{1,0:T(8,128)S(1)}) fusion(f32[256,3072]{1,0:T(8,128)S(1)} %fusion.46, bf16[256,768]{0,1:T(8,128)(2,1)S(1)} %bitcast.119, bf16[768,3072]{1,0:T(8,128)(2,1)S(1)} %collective-permute-done.2, f32[3072]{0:T(1024)S(1)} %bitcast.135, bf16[256,3072]{1,0:T(8,128)(2,1)S(1)} %bitcast.128), kind=kOutput, calls=%fused_computation.110 | convolution fusion | flops 1211891456 | bytes 12989440 | tf_op jit(solution)/shard_map/dot_general | solution.py:23
  114.2 1.4 fusion.6
  118.2 0.8 fusion.16
  119.5 1.1 pad_maximum_fusion
  120.7 7.1 %all-to-all-start.1 = ((bf16[32,152,128]{2,1,0:T(8,128)(2,1)}), bf16[32,152,128]{2,1,0:T(8,128)(2,1)S(1)}, u32[]{:S(2)}, u32[]{:S(2)}) async-start(bf16[32,152,128]{2,1,0:T(8,128)(2,1)} %pad_maximum_fusion), calls=%async_computation.1 | async-start | bytes 2490368 | tf_op jit(solution)/shard_map/all_to_all | solution.py:167
  127.8 17.5 %all-to-all-done.1 = bf16[32,152,128]{2,1,0:T(8,128)(2,1)S(1)} async-done(((bf16[32,152,128]{2,1,0:T(8,128)(2,1)}), bf16[32,152,128]{2,1,0:T(8,128)(2,1)S(1)}, u32[]{:S(2)}, u32[]{:S(2)}) %all-to-all-start.1) | async-done | bytes 1245216 | tf_op jit(solution)/shard_map/all_to_all | solution.py:167
  146.6 19.6 %all_to_all.21 = bf16[16,9,128]{2,1,0:T(8,128)(2,1)S(1)} all-to-all(bf16[16,9,128]{2,1,0:T(8,128)(2,1)S(1)} %copy.87), channel_id=1, replica_groups=mesh['xh'=2,'z'=16,'c'=2,'xl'=2,'y'=4] {'z'}, dimensions={0} | all-to-all | bytes 73728 | tf_op jit(solution)/shard_map/all_to_all | solution.py:178
  166.2 9.6 %all_to_all.22 = f32[8,9,128]{2,1,0:T(8,128)S(1)} all-to-all(f32[8,9,128]{2,1,0:T(8,128)S(1)} %broadcast_in_dim.15), channel_id=1, replica_groups=mesh['xh'=2,'z'=16,'c'=2,'xl'=2,'y'=4] {'xl','y'}, dimensions={0} | all-to-all | bytes 73728 | tf_op jit(solution)/shard_map/all_to_all | solution.py:47
  (84 shorter events, 14.6 us)
Async XLA Ops:
  7.2 69.7 %copy-start.1 = (bf16[1,2,128,1536]{3,2,1,0:T(8,128)(2,1)S(1)}, bf16[1,2,128,1536]{3,2,1,0:T(8,128)(2,1)}, u32[]{:S(2)}) copy-start(bf16[1,2,128,1536]{3,2,1,0:T(8,128)(2,1)} %param.11) | copy-start | bytes 2359300
  7.2 92.8 %all-gather.5.cloned.1.call-start = ((), (), s32[]{:S(2)}) async-start(), calls=%async_computation.4 | async-start | bytes 5013504 | tf_op jit(solution)/shard_map/all_gather | solution.py:95
  16.8 9.2 %collective-permute-start = (bf16[12,128]{1,0:T(8,128)(2,1)S(1)}, bf16[12,128]{1,0:T(8,128)(2,1)S(1)}, u32[]{:S(2)}, u32[]{:S(2)}) collective-permute-start(bf16[12,128]{1,0:T(8,128)(2,1)S(1)} %fusion.66), channel_id=1, source_target_pairs={{0,256},{256,0},{1,257},{257,1},{2,258},{258,2},{3,259},{259,3},{4... | collective-permute-start | bytes 9224 | tf_op jit(solution)/shard_map/ppermute | solution.py:58
  74.9 4.3 %collective-permute-start.1 = (bf16[8,16,2,12,128]{4,1,3,2,0:T(8,128)(2,1)S(1)}, bf16[8,16,2,12,128]{4,1,3,2,0:T(8,128)(2,1)}, u32[]{:S(2)}, u32[]{:S(2)}) collective-permute-start(bf16[8,16,2,12,128]{4,1,3,2,0:T(8,128)(2,1)S(1)} %all_to_all.20), channel_id=1, source_target_pairs={{0,8},{8,0},{1,9},{9,1},{2,10},{10,2},{3,11},{11,3},{4,12},{12,4},... | collective-permute-start | bytes 2359304 | tf_op jit(solution)/shard_map/ppermute | solution.py:61
  90.7 2.3 %copy-start.3 = (bf16[128,256]{1,0:T(8,128)(2,1)}, bf16[128,256]{1,0:T(8,128)(2,1)S(1)}, u32[]{:S(2)}) copy-start(bf16[128,256]{1,0:T(8,128)(2,1)S(1)} %convolution_convert_fusion.1) | copy-start | bytes 196612
  90.7 11.3 %copy-start.6 = (bf16[1,2,128,64]{2,3,1,0:T(8,128)(2,1)S(1)}, bf16[1,2,128,64]{2,3,1,0:T(8,128)(2,1)}, u32[]{:S(2)}) copy-start(bf16[1,2,128,64]{2,3,1,0:T(8,128)(2,1)} %param.13) | copy-start | bytes 98308
  90.7 12.0 %copy-start.8 = (s32[1,128]{1,0:T(1,128)S(1)}, s32[1,128]{1,0:T(1,128)}, u32[]{:S(2)}) copy-start(s32[1,128]{1,0:T(1,128)} %param.14) | copy-start | bytes 1540
  90.7 12.1 %copy-start.7 = (f32[2]{0:T(128)S(1)}, f32[2]{0:T(128)}, u32[]{:S(2)}) copy-start(f32[2]{0:T(128)} %constant.65.clone) | copy-start | bytes 28
  90.7 12.1 %copy-start.5 = (f32[1,3,3072]{2,0,1:T(1,128)S(1)}, f32[1,3,3072]{2,0,1:T(1,128)}, u32[]{:S(2)}) copy-start(f32[1,3,3072]{2,0,1:T(1,128)} %param.16) | copy-start | bytes 110596
  100.0 10.0 %collective-permute-start.2 = (bf16[768,3072]{1,0:T(8,128)(2,1)}, bf16[768,3072]{1,0:T(8,128)(2,1)S(1)}, u32[]{:S(2)}, u32[]{:S(2)}) collective-permute-start(bf16[768,3072]{1,0:T(8,128)(2,1)} %bitcast.110), channel_id=1, source_target_pairs={{0,8},{8,0},{1,9},{9,1},{2,10},{10,2},{3,11},{11,3},{4,12},{12,4},... | collective-permute-start | bytes 14155784 | tf_op jit(solution)/shard_map/ppermute | solution.py:119
  103.7 6.2 %copy-start.2 = (bf16[1,2,128,3072]{3,2,1,0:T(8,128)(2,1)S(1)}, bf16[1,2,128,3072]{3,2,1,0:T(8,128)(2,1)}, u32[]{:S(2)}) copy-start(bf16[1,2,128,3072]{3,2,1,0:T(8,128)(2,1)} %param.12) | copy-start | bytes 4718596
  110.0 2.0 %copy-start = (f32[256,3072]{1,0:T(8,128)S(1)}, f32[256,3072]{1,0:T(8,128)}, u32[]{:S(2)}) copy-start(f32[256,3072]{1,0:T(8,128)} %fusion.45) | copy-start | bytes 9437188
  116.3 0.9 copy-start.4
  120.7 24.7 %all-to-all-start.1 = ((bf16[32,152,128]{2,1,0:T(8,128)(2,1)}), bf16[32,152,128]{2,1,0:T(8,128)(2,1)S(1)}, u32[]{:S(2)}, u32[]{:S(2)}) async-start(bf16[32,152,128]{2,1,0:T(8,128)(2,1)} %pad_maximum_fusion), calls=%async_computation.1 | async-start | bytes 2490368 | tf_op jit(solution)/shard_map/all_to_all | solution.py:167
Sparse Core Ops, SparseCore 0:
  15.4 84.5 all-gather.4

commit v8 on v7

--- a/solution.py
+++ b/solution.py
@@ -102,6 +102,7 @@
     in_cores = in_cores.reshape(2, rows, depth // 2)
     in_here = jnp.where(core == 0, in_cores[0], in_cores[1])
     in_there = jnp.where(core == 0, in_cores[1], in_cores[0])
+    in_away = lax.ppermute(in_there, "c", SWAP)
     stream = residual.reshape(rows, width).astype(F32)
     shift, scale, gate = modulation[0, 0:1], 1.0 + modulation[0, 1:2], modulation[0, 2:3]
     final32 = final_all.astype(F32)
@@ -113,11 +114,13 @@
     target_rows = targets.reshape(rows, channels).astype(F32)
     mask_rows = jnp.broadcast_to(repaint_mask.astype(F32)[0], (kinds, tokens)).reshape(rows, 1)
 
-    ready = (in_here, in_there, final_all, final_twice, up_all, down_projected, adapter_term)
+    ready = (in_here, in_there, in_away, final_all, final_twice, up_all)
+    ready = ready + (down_projected, adapter_term)
     here, ready = lax.optimization_barrier((here, ready))
-    in_here, in_there, final_all, final_twice, up_all, down_projected, adapter_term = ready
-    there = lax.ppermute(here, "c", SWAP)
-    frozen = dot(in_here, here) + dot(in_there, there)
+    in_here, in_there, in_away, final_all, final_twice, up_all = ready[:6]
+    down_projected, adapter_term = ready[6:]
+    away = lax.ppermute(dot(in_away, here).astype(BF16), "c", SWAP)
+    frozen = dot(in_here, here) + away.astype(F32)
     hidden_ref = stream + gate * frozen
     hidden_pol = hidden_ref + gate * adapter_term
 

time: 185 us -> 184 us (level)
  starting transfers between devices: 18.8 us -> 21.6 us
  local copies, waits for them, and re-layouts: 13 us -> 10.3 us
    reshape x2, local copies, waits for them, and re-layouts: 4.89 us -> 1.25 us  [gather_small(): both[:, 3 * own:].reshape(4 * zs, own, 2, channels).transpose(0, 2, 1, 3)]
    ppermute x1 -> x2, starting transfers between devices: 2.09 us -> 4.51 us  [the longest x1 2.41 us: local(): in_away = lax.ppermute(in_there, 'c', SWAP)]
  transfers between devices with their start and end apart: 5 -> 6, of which waited for: 5 -> 4; matrix products, arithmetic and copies ran while one was open for 12% -> 8% of each run, Pallas kernels for 0% -> 0%
where the time goes in v8:
time: 184 us; the launch traced here: 183 us
  blocking collectives  85.5 us (46%)
  waiting for transfers between devices  28.4 us (15%)
  starting transfers between devices  21.6 us (12%)
  between operations  15.2 us (8%)
  matrix products  14.5 us (8%)
  local copies, waits for them, and re-layouts  10.3 us (6%)
  other arithmetic  7.73 us (4%)
    all_gather x1, blocking collectives, gather_small(): packed = lax.all_gather(packed, 'z', axis=0)  33.9 us
    all_to_all x2, blocking collectives, spread(): lax.all_to_all(jnp.broadcast_to(value[None], (size,) + value.shape), axes...  24.3 us
    all_to_all x1, blocking collectives, local(): lax.all_to_all(grads.transpose(1, 0, 2).astype(BF16), 'z', 0, 0).astype(F32)  19.3 us
    all_to_all x1, waiting for transfers between devices, local(): grads = lax.all_to_all(grads, ('xh', 'c') + TOKENS, 0, 0)  17.5 us
    dot_general x6, matrix products, dot(): return jnp.dot(a, b, preferred_element_type=F32)  8.81 us
    all_gather x1, blocking collectives, local(): lax.all_gather(output_weight, ('xh', 'xl'), axis=0, axis_index_groups=[[0...  8.01 us
    ppermute x1, starting transfers between devices, gather_small(): packed = jnp.stack([packed, lax.ppermute(packed, 'xh', SWAP)])  7.69 us
    all_to_all x1, starting transfers between devices, local(): grads = lax.all_to_all(grads, ('xh', 'c') + TOKENS, 0, 0)  7.44 us
  transfers between devices with their start and end apart: 6, of which 4 were waited for; matrix products, arithmetic and copies ran while one was open for 8% of the time, Pallas kernels for 0%

profile of v8, /device:TPU:2, one launch (start us, length us, event | category | flops | bytes accessed | tf_op | source)
XLA Modules:
  0.0 183.2 jit_solution(9431010542792040178)
XLA Ops:
  7.2 8.0 %all-gather = bf16[48,3072]{1,0:T(8,128)(2,1)} all-gather(bf16[24,3072]{1,0:T(8,128)(2,1)} %param.17), channel_id=2, replica_groups={{0,260},{4,256},{1,261},{5,257},{2,262},{6,258},{3,263},{7,259},{8,268}..., dimensions={0}, use_global_device_ids=true | all-gather | bytes 442368 | tf_op jit(solution)/shard_map/all_gather | solution.py:94
  16.8 7.7 %collective-permute-start.1 = (bf16[12,128]{1,0:T(8,128)(2,1)S(1)}, bf16[12,128]{1,0:T(8,128)(2,1)S(1)}, u32[]{:S(2)}, u32[]{:S(2)}) collective-permute-start(bf16[12,128]{1,0:T(8,128)(2,1)S(1)} %fusion.65), channel_id=1, source_target_pairs={{0,256},{256,0},{1,257},{257,1},{2,258},{258,2},{3,259},{259,3},{4... | collective-permute-start | bytes 9224 | tf_op jit(solution)/shard_map/ppermute | solution.py:58
  24.5 1.6 collective-permute-done.1
  26.1 33.9 %all-gather.2 = bf16[32,12,128]{2,1,0:T(8,128)(2,1)S(1)} all-gather(bf16[2,12,128]{2,1,0:T(8,128)(2,1)S(1)} %pad_maximum_fusion.7), channel_id=4, replica_groups=mesh['xh'=2,'z'=16,'c'=2,'xl'=2,'y'=4] {'z'}, dimensions={0}, use_global_device_ids=true | all-gather | bytes 104448 | tf_op jit(solution)/shard_map/all_gather | solution.py:59
  60.2 14.7 %all_to_all.20 = bf16[8,16,2,12,128]{4,1,3,2,0:T(8,128)(2,1)S(1)} all-to-all(bf16[8,16,2,12,128]{4,1,3,2,0:T(8,128)(2,1)S(1)} %broadcast_in_dim.11), channel_id=1, replica_groups=mesh['xh'=2,'z'=16,'c'=2,'xl'=2,'y'=4] {'xl','y'}, dimensions={0} | all-to-all | bytes 1572864 | tf_op jit(solution)/shard_map/all_to_all | solution.py:47
  74.9 1.9 %collective-permute-start.2 = (bf16[8,16,2,12,128]{4,1,3,2,0:T(8,128)(2,1)S(1)}, bf16[8,16,2,12,128]{4,1,3,2,0:T(8,128)(2,1)}, u32[]{:S(2)}, u32[]{:S(2)}) collective-permute-start(bf16[8,16,2,12,128]{4,1,3,2,0:T(8,128)(2,1)S(1)} %all_to_all.20), channel_id=1, source_target_pairs={{0,8},{8,0},{1,9},{9,1},{2,10},{10,2},{3,11},{11,3},{4,12},{12,4},... | collective-permute-start | bytes 2359304 | tf_op jit(solution)/shard_map/ppermute | solution.py:61
  78.0 2.4 %collective-permute-start = (bf16[256,768]{0,1:T(8,128)(2,1)S(1)}, bf16[256,768]{0,1:T(8,128)(2,1)}, u32[]{:S(2)}, u32[]{:S(2)}) collective-permute-start(bf16[256,768]{0,1:T(8,128)(2,1)S(1)} %bitcast.128), channel_id=1, source_target_pairs={{0,8},{8,0},{1,9},{9,1},{2,10},{10,2},{3,11},{11,3},{4,12},{12,4},... | collective-permute-start | bytes 1179656 | tf_op jit(solution)/shard_map/ppermute | solution.py:105
  80.5 1.4 copy.83
  82.6 1.7 maximum_select_fusion
  84.7 2.4 %copy.79 = bf16[2,16,2,8,12,128]{5,2,1,0,4,3:T(2,128)(2,1)S(1)} copy(bf16[2,16,2,8,12,128]{5,1,4,0,3,2:T(8,128)(2,1)S(1)} %fusion.7) | data formatting | bytes 3145728 | tf_op jit(solution)/shard_map/transpose | solution.py:64
  88.4 2.3 %fusion.45 = f32[256,3072]{1,0:T(8,128)} fusion(bf16[128,256]{1,0:T(8,128)(2,1)S(1)} %convolution_convert_fusion.2, bf16[3072,128]{1,0:T(8,128)(2,1)S(1)} %bitcast.114), kind=kOutput, calls=%fused_computation.112 | convolution fusion | flops 201326592 | bytes 3997696 | tf_op jit(solution)/shard_map/dot_general | solution.py:27
  91.1 0.9 copy.80
  92.4 7.1 %all-gather.5.cloned.1.call-done = bf16[32,24,3072]{2,1,0:T(8,128)(2,1)} async-done(((bf16[2,24,3072]{2,1,0:T(8,128)(2,1)}), bf16[32,24,3072]{2,1,0:T(8,128)(2,1)}) %all-gather.5.cloned.1.call-update) | async-done | bytes 4718608 | tf_op jit(solution)/shard_map/all_gather | solution.py:95
  99.5 4.0 %convolution_convert_fusion = bf16[256,3072]{1,0:T(8,128)(2,1)S(1)} fusion(bf16[256,768]{0,1:T(8,128)(2,1)} %collective-permute-done, bf16[768,3072]{1,0:T(8,128)(2,1)} %bitcast.105), kind=kOutput, calls=%fused_computation.9 | convolution fusion | flops 1208745984 | bytes 6684672 | tf_op jit(solution)/shard_map/dot_general | solution.py:23
  103.6 2.1 %collective-permute-start.3 = (bf16[256,3072]{1,0:T(8,128)(2,1)S(1)}, bf16[256,3072]{1,0:T(8,128)(2,1)S(1)}, u32[]{:S(2)}, u32[]{:S(2)}) collective-permute-start(bf16[256,3072]{1,0:T(8,128)(2,1)S(1)} %convolution_convert_fusion), channel_id=1, source_target_pairs={{0,8},{8,0},{1,9},{9,1},{2,10},{10,2},{3,11},{11,3},{4,12},{12,4},... | collective-permute-start | bytes 4718600 | tf_op jit(solution)/shard_map/ppermute | solution.py:122
  106.7 2.2 %collective-permute-done.3 = bf16[256,3072]{1,0:T(8,128)(2,1)S(1)} collective-permute-done((bf16[256,3072]{1,0:T(8,128)(2,1)S(1)}, bf16[256,3072]{1,0:T(8,128)(2,1)S(1)}, u32[]{:S(2)}, u32[]{:S(2)}) %collective-permute-start.3) | collective-permute-done | bytes 1572896 | tf_op jit(solution)/shard_map/ppermute | solution.py:122
  108.9 2.0 %fusion.44 = (f32[256]{0:T(256)S(1)}, f32[256,3072]{1,0:T(8,128)S(1)}) fusion(bf16[256,3072]{1,0:T(8,128)(2,1)S(1)} %collective-permute-done.3, bf16[256,768]{0,1:T(8,128)(2,1)S(1)} %bitcast.119, bf16[768,3072]{1,0:T(8,128)(2,1)S(1)} %bitcast.108, f32[3072]{0:T(1024)S(1)} %bitcast.137, bf16[256,3072]{1,0:T(8,128)(2,1)S(1)} %bitcast.126), kind=kOutput, calls=%fused_computation.111 | convolution fusion | flops 1212677888 | bytes 11416576 | tf_op jit(solution)/shard_map/dot_general | solution.py:23
  113.5 1.4 fusion.6
  117.6 0.8 fusion.16
  118.9 1.1 pad_maximum_fusion
  120.0 7.4 %all-to-all-start.1 = ((bf16[32,152,128]{2,1,0:T(8,128)(2,1)}), bf16[32,152,128]{2,1,0:T(8,128)(2,1)S(1)}, u32[]{:S(2)}, u32[]{:S(2)}) async-start(bf16[32,152,128]{2,1,0:T(8,128)(2,1)} %pad_maximum_fusion), calls=%async_computation.1 | async-start | bytes 2490368 | tf_op jit(solution)/shard_map/all_to_all | solution.py:170
  127.4 17.5 %all-to-all-done.1 = bf16[32,152,128]{2,1,0:T(8,128)(2,1)S(1)} async-done(((bf16[32,152,128]{2,1,0:T(8,128)(2,1)}), bf16[32,152,128]{2,1,0:T(8,128)(2,1)S(1)}, u32[]{:S(2)}, u32[]{:S(2)}) %all-to-all-start.1) | async-done | bytes 1245216 | tf_op jit(solution)/shard_map/all_to_all | solution.py:170
  146.2 19.3 %all_to_all.21 = bf16[16,9,128]{2,1,0:T(8,128)(2,1)S(1)} all-to-all(bf16[16,9,128]{2,1,0:T(8,128)(2,1)S(1)} %copy.87), channel_id=1, replica_groups=mesh['xh'=2,'z'=16,'c'=2,'xl'=2,'y'=4] {'z'}, dimensions={0} | all-to-all | bytes 73728 | tf_op jit(solution)/shard_map/all_to_all | solution.py:181
  165.5 9.6 %all_to_all.22 = f32[8,9,128]{2,1,0:T(8,128)S(1)} all-to-all(f32[8,9,128]{2,1,0:T(8,128)S(1)} %broadcast_in_dim.15), channel_id=1, replica_groups=mesh['xh'=2,'z'=16,'c'=2,'xl'=2,'y'=4] {'xl','y'}, dimensions={0} | all-to-all | bytes 73728 | tf_op jit(solution)/shard_map/all_to_all | solution.py:47
  (91 shorter events, 14.5 us)
Async XLA Ops:
  7.2 69.6 %copy-start.1 = (bf16[1,2,128,1536]{3,2,1,0:T(8,128)(2,1)S(1)}, bf16[1,2,128,1536]{3,2,1,0:T(8,128)(2,1)}, u32[]{:S(2)}) copy-start(bf16[1,2,128,1536]{3,2,1,0:T(8,128)(2,1)} %param.11) | copy-start | bytes 2359300
  7.2 92.3 %all-gather.5.cloned.1.call-start = ((), (), s32[]{:S(2)}) async-start(), calls=%async_computation.4 | async-start | bytes 5013504 | tf_op jit(solution)/shard_map/all_gather | solution.py:95
  16.8 9.3 %collective-permute-start.1 = (bf16[12,128]{1,0:T(8,128)(2,1)S(1)}, bf16[12,128]{1,0:T(8,128)(2,1)S(1)}, u32[]{:S(2)}, u32[]{:S(2)}) collective-permute-start(bf16[12,128]{1,0:T(8,128)(2,1)S(1)} %fusion.65), channel_id=1, source_target_pairs={{0,256},{256,0},{1,257},{257,1},{2,258},{258,2},{3,259},{259,3},{4... | collective-permute-start | bytes 9224 | tf_op jit(solution)/shard_map/ppermute | solution.py:58
  74.9 7.7 %collective-permute-start.2 = (bf16[8,16,2,12,128]{4,1,3,2,0:T(8,128)(2,1)S(1)}, bf16[8,16,2,12,128]{4,1,3,2,0:T(8,128)(2,1)}, u32[]{:S(2)}, u32[]{:S(2)}) collective-permute-start(bf16[8,16,2,12,128]{4,1,3,2,0:T(8,128)(2,1)S(1)} %all_to_all.20), channel_id=1, source_target_pairs={{0,8},{8,0},{1,9},{9,1},{2,10},{10,2},{3,11},{11,3},{4,12},{12,4},... | collective-permute-start | bytes 2359304 | tf_op jit(solution)/shard_map/ppermute | solution.py:61
  78.0 14.4 %collective-permute-start = (bf16[256,768]{0,1:T(8,128)(2,1)S(1)}, bf16[256,768]{0,1:T(8,128)(2,1)}, u32[]{:S(2)}, u32[]{:S(2)}) collective-permute-start(bf16[256,768]{0,1:T(8,128)(2,1)S(1)} %bitcast.128), channel_id=1, source_target_pairs={{0,8},{8,0},{1,9},{9,1},{2,10},{10,2},{3,11},{11,3},{4,12},{12,4},... | collective-permute-start | bytes 1179656 | tf_op jit(solution)/shard_map/ppermute | solution.py:105
  88.4 2.3 %copy-start.4 = (bf16[128,256]{1,0:T(8,128)(2,1)}, bf16[128,256]{1,0:T(8,128)(2,1)S(1)}, u32[]{:S(2)}) copy-start(bf16[128,256]{1,0:T(8,128)(2,1)S(1)} %convolution_convert_fusion.2) | copy-start | bytes 196612
  99.5 9.4 %slice-start = ((s8[4718592]{0:T(1024)(128)(4,1)}), s8[4194304]{0:T(1024)(128)(4,1)S(1)}, s32[]{:S(2)}) async-start(s8[4718592]{0:T(1024)(128)(4,1)} %bitcast.106), calls=%async_computation.5 | async-start | bytes 8388608
  99.5 6.2 %copy-start.8 = (s32[1,128]{1,0:T(1,128)S(1)}, s32[1,128]{1,0:T(1,128)}, u32[]{:S(2)}) copy-start(s32[1,128]{1,0:T(1,128)} %param.14) | copy-start | bytes 1540
  99.5 6.2 %copy-start.7 = (f32[2]{0:T(128)S(1)}, f32[2]{0:T(128)}, u32[]{:S(2)}) copy-start(f32[2]{0:T(128)} %constant.65.clone) | copy-start | bytes 28
  99.5 6.3 %copy-start.6 = (f32[1,3,3072]{2,0,1:T(1,128)S(1)}, f32[1,3,3072]{2,0,1:T(1,128)}, u32[]{:S(2)}) copy-start(f32[1,3,3072]{2,0,1:T(1,128)} %param.16) | copy-start | bytes 110596
  99.5 9.4 %slice-start.1 = ((s8[4718592]{0:T(1024)(128)(4,1)}), s8[524288]{0:T(1024)(128)(4,1)S(1)}, s32[]{:S(2)}) async-start(s8[4718592]{0:T(1024)(128)(4,1)} %bitcast.106), calls=%async_computation.6 | async-start | bytes 1048576
  99.5 9.4 %copy-start.2 = (bf16[1,2,128,3072]{3,2,1,0:T(8,128)(2,1)S(1)}, bf16[1,2,128,3072]{3,2,1,0:T(8,128)(2,1)}, u32[]{:S(2)}) copy-start(bf16[1,2,128,3072]{3,2,1,0:T(8,128)(2,1)} %param.12) | copy-start | bytes 4718596
  103.6 5.3 %collective-permute-start.3 = (bf16[256,3072]{1,0:T(8,128)(2,1)S(1)}, bf16[256,3072]{1,0:T(8,128)(2,1)S(1)}, u32[]{:S(2)}, u32[]{:S(2)}) collective-permute-start(bf16[256,3072]{1,0:T(8,128)(2,1)S(1)} %convolution_convert_fusion), channel_id=1, source_target_pairs={{0,8},{8,0},{1,9},{9,1},{2,10},{10,2},{3,11},{11,3},{4,12},{12,4},... | collective-permute-start | bytes 4718600 | tf_op jit(solution)/shard_map/ppermute | solution.py:122
  108.9 2.1 %copy-start = (f32[256,3072]{1,0:T(8,128)S(1)}, f32[256,3072]{1,0:T(8,128)}, u32[]{:S(2)}) copy-start(f32[256,3072]{1,0:T(8,128)} %fusion.45) | copy-start | bytes 9437188
  111.7 0.8 copy-start.3
  115.6 0.9 copy-start.5
  120.0 25.0 %all-to-all-start.1 = ((bf16[32,152,128]{2,1,0:T(8,128)(2,1)}), bf16[32,152,128]{2,1,0:T(8,128)(2,1)S(1)}, u32[]{:S(2)}, u32[]{:S(2)}) async-start(bf16[32,152,128]{2,1,0:T(8,128)(2,1)} %pad_maximum_fusion), calls=%async_computation.1 | async-start | bytes 2490368 | tf_op jit(solution)/shard_map/all_to_all | solution.py:170
Sparse Core Ops, SparseCore 0:
  15.4 84.0 all-gather.4
